TPU v7x, 32 devices: a whole 2x2x4 slice. The times are simulated.
32 devices in a mesh: dp: 4 (over y, core), ctx: 2 (over x), fsdp: 4 (over z).
Axes of the slice: x: 2, y: 2, z: 4, core: 2. Of those that a mesh axis runs over, the one named last changes fastest.
Arguments:
- tokens: bfloat16 [16, 1024, 1152], P(('dp', 'fsdp'), 'ctx'), may hold values from -6 to 6
- segments: int32 [16, 1024], P(('dp', 'fsdp'), 'ctx'), may hold values from 0 to 1023, as said below
- cotangent: bfloat16 [16, 1024, 1152], P(('dp', 'fsdp'), 'ctx'), may hold values from -6 to 6
- attn_gain: float32 [1152], P('fsdp'), may hold values from 0.1 to 1.9
- w_query: float32 [1152, 1152], P('fsdp'), may hold values from -0.1875 to 0.1875
- key_matrix: float32 [1152, 384], P('fsdp'), may hold values from -0.1875 to 0.1875
- value_matrix: float32 [1152, 384], P('fsdp'), may hold values from -0.1875 to 0.1875
- w_out: float32 [1152, 1152], P('fsdp'), may hold values from -0.75 to 0.75
- ffn_gain: float32 [1152], P('fsdp'), may hold values from 0.1 to 1.9
- w_gate: float32 [1152, 3072], P('fsdp'), may hold values from -0.1875 to 0.1875
- w_up: float32 [1152, 3072], P('fsdp'), may hold values from -0.1875 to 0.1875
- w_down: float32 [3072, 1152], P('fsdp'), may hold values from -0.109375 to 0.109375
Outputs:
- output: bfloat16 [16, 1024, 1152], P(('dp', 'fsdp'), 'ctx')
- grad_tokens: bfloat16 [16, 1024, 1152], P(('dp', 'fsdp'), 'ctx')
- grad_attn_gain: float32 [1152], P('fsdp')
- grad_w_query: float32 [1152, 1152], P('fsdp')
- grad_w_key: float32 [1152, 384], P('fsdp')
- grad_w_value: float32 [1152, 384], P('fsdp')
- grad_w_out: float32 [1152, 1152], P('fsdp')
- grad_ffn_gain: float32 [1152], P('fsdp')
- grad_w_gate: float32 [1152, 3072], P('fsdp')
- grad_w_up: float32 [1152, 3072], P('fsdp')
- grad_w_down: float32 [3072, 1152], P('fsdp')
Inputs may be any that keep to these rules, and one draw needn't show every extreme that they name: `segments`: in each sequence the document numbers start at 0 at the first token and rise by 0 or 1 from one token to the next; in one sequence, chosen by the seed, all tokens belong to document 0; in another, also chosen by the seed, every token is a document of its own.
All inputs are finite; a program needn't handle non-finite values.
Results may differ from a plain program's by a relative error of at most 0.02.
Values may be sent and summed in bfloat16 or wider, within the bound.
No kernel may reach another device: no remote copies, remote signals or barrier semaphores. Data moves between devices by JAX's collectives and lax.ppermute only.
A program may use at most 256 MiB of HBM per device.

v0:
```python
import math

import jax
import jax.numpy as jnp
from jax import lax
from jax.sharding import PartitionSpec as P

QUERY_HEADS = 18
KEY_VALUE_HEADS = 6
HEAD_WIDTH = 64


negative_large = -1e30
eps_norm = 1e-05


def inverse_freq(head_size):
    return 10000.0 ** (-(jnp.arange(head_size // 2, dtype=jnp.float32) * 2.0) / head_size)


def rotate(field, angles, head_size):
    block_length = field.shape[0]
    heads = field.reshape(block_length, -1, head_size)
    cosine = jnp.cos(angles)[:, None, :]
    sine = jnp.sin(angles)[:, None, :]
    former = heads[..., : head_size // 2]
    latter = heads[..., head_size // 2 :]
    turned = jnp.concatenate(
        [former * cosine - latter * sine, latter * cosine + former * sine], axis=-1
    )
    return turned.reshape(block_length, -1)


def positions_of(ids):
    index = jnp.arange(ids.shape[0], dtype=jnp.int32)
    change = jnp.concatenate([jnp.ones((1,), dtype=bool), ids[1:] != ids[:-1]])
    starts = lax.cummax(jnp.where(change, index, 0), axis=0)
    return index - starts


def norm_scale(value):
    return lax.rsqrt(jnp.mean(value * value, axis=-1, keepdims=True) + eps_norm)


def norm_back(scaled, value, scale):
    return scale * scaled - value * scale**3 * jnp.mean(scaled * value, axis=-1, keepdims=True)


def outer_sum(left, right):
    return lax.dot_general(
        left, right, (((0,), (0,)), ((), ())), preferred_element_type=jnp.float32
    )


def times_transposed(left, right):
    return lax.dot_general(
        left, right, (((1,), (1,)), ((), ())), preferred_element_type=jnp.float32
    )


def plain_dot(left, right):
    return jnp.dot(left, right, preferred_element_type=jnp.float32)


def allowed_mask(place, own_ids, all_ids, start_row, block_count):
    key_place = start_row + jnp.arange(block_count, dtype=jnp.int32)
    key_ids = lax.dynamic_slice_in_dim(all_ids, start_row, block_count)
    return (key_place[None, :] <= place[:, None]) & (key_ids[None, :] == own_ids[:, None])


def score_block(query_heads_view, key_portion, allowed, scale):
    key_heads = key_portion.reshape(key_portion.shape[0], KEY_VALUE_HEADS, HEAD_WIDTH)
    raw = jnp.einsum(
        "tgrd,ngd->grtn", query_heads_view, key_heads, preferred_element_type=jnp.float32
    )
    return jnp.where(allowed, raw * scale, negative_large)


def settle(allowed, work, carry):
    return lax.cond(jnp.any(allowed), work, lambda kept: kept, carry)


def over_blocks(function, carry, parts, row_total):
    block_count = parts[0].shape[0]
    width = math.gcd(block_count, row_total)

    def turn(step, state):
        begin = step * width
        sliced = tuple((lax.dynamic_slice_in_dim(member, begin, width) for member in parts))
        return function(state, sliced, begin)

    return lax.fori_loop(0, block_count // width, turn, carry)


def shards(
    tokens,
    segments,
    cotangent,
    attn_gain,
    w_query,
    key_matrix,
    value_matrix,
    w_out,
    ffn_gain,
    w_gate,
    w_up,
    w_down,
):
    inputs = tokens[0].astype(jnp.float32)
    own_ids = segments[0]
    incoming = cotangent[0]
    row_total = inputs.shape[0]
    group_width = QUERY_HEADS // KEY_VALUE_HEADS
    scale = HEAD_WIDTH ** (-0.5)
    low_type = jnp.bfloat16
    gain_one, query_full, key_full, value_full, out_full = (
        lax.all_gather(attn_gain.astype(low_type), "fsdp", axis=0, tiled=True),
        lax.all_gather(w_query.astype(low_type), "fsdp", axis=0, tiled=True),
        lax.all_gather(key_matrix.astype(low_type), "fsdp", axis=0, tiled=True),
        lax.all_gather(value_matrix.astype(low_type), "fsdp", axis=0, tiled=True),
        lax.all_gather(w_out.astype(low_type), "fsdp", axis=0, tiled=True),
    )
    gain_two, gate_full, up_full, down_full = (
        lax.all_gather(ffn_gain.astype(low_type), "fsdp", axis=0, tiled=True),
        lax.all_gather(w_gate.astype(low_type), "fsdp", axis=0, tiled=True),
        lax.all_gather(w_up.astype(low_type), "fsdp", axis=0, tiled=True),
        lax.all_gather(w_down.astype(low_type), "fsdp", axis=0, tiled=True),
    )
    all_ids = lax.all_gather(own_ids, "ctx", axis=0, tiled=True)
    offset = lax.axis_index("ctx") * row_total
    place = offset + jnp.arange(row_total, dtype=jnp.int32)
    positions = lax.dynamic_slice_in_dim(positions_of(all_ids), offset, row_total)
    angles = positions.astype(jnp.float32)[:, None] * inverse_freq(HEAD_WIDTH)[None, :]
    scale_one = norm_scale(inputs)
    normed = (inputs * scale_one * gain_one.astype(jnp.float32)).astype(low_type)
    query_rows = rotate(plain_dot(normed, query_full), angles, HEAD_WIDTH).astype(low_type)
    key_rows = rotate(plain_dot(normed, key_full), angles, HEAD_WIDTH).astype(low_type)
    value_rows = plain_dot(normed, value_full).astype(low_type)
    query_heads_view = query_rows.reshape(row_total, KEY_VALUE_HEADS, group_width, HEAD_WIDTH)

    def stats_block(carry, parts, start_row):
        key_portion = parts[0]
        allowed = allowed_mask(place, own_ids, all_ids, start_row, key_portion.shape[0])

        def work(state):
            peak, total = state
            scores = score_block(query_heads_view, key_portion, allowed, scale)
            fresh = jnp.maximum(peak, jnp.max(scores, axis=-1))
            terms = jnp.where(allowed, jnp.exp(scores - fresh[..., None]), 0.0)
            return (fresh, total * jnp.exp(peak - fresh) + jnp.sum(terms, axis=-1))

        return settle(allowed, work, carry)

    stats_init = (
        jnp.full((KEY_VALUE_HEADS, group_width, row_total), negative_large, jnp.float32),
        jnp.zeros((KEY_VALUE_HEADS, group_width, row_total), jnp.float32),
    )
    peak, total = over_blocks(
        stats_block, stats_init, (lax.all_gather(key_rows, "ctx", axis=0, tiled=True),), row_total
    )
    log_total = peak + jnp.log(total)

    def mix_block(carry, parts, start_row):
        key_portion, value_portion = parts
        block_count = key_portion.shape[0]
        allowed = allowed_mask(place, own_ids, all_ids, start_row, block_count)

        def work(summed):
            scores = score_block(query_heads_view, key_portion, allowed, scale)
            weights = jnp.where(allowed, jnp.exp(scores - log_total[..., None]), 0.0).astype(
                low_type
            )
            value_heads = value_portion.reshape(block_count, KEY_VALUE_HEADS, HEAD_WIDTH)
            return summed + jnp.einsum(
                "grtn,ngd->tgrd", weights, value_heads, preferred_element_type=jnp.float32
            )

        return settle(allowed, work, carry)

    mixing_initial = jnp.zeros((row_total, KEY_VALUE_HEADS, group_width, HEAD_WIDTH), jnp.float32)
    attention_output = over_blocks(
        mix_block,
        mixing_initial,
        (
            lax.all_gather(key_rows, "ctx", axis=0, tiled=True),
            lax.all_gather(value_rows, "ctx", axis=0, tiled=True),
        ),
        row_total,
    ).reshape(row_total, QUERY_HEADS * HEAD_WIDTH)
    attended_low = attention_output.astype(low_type)
    middle = inputs + plain_dot(attended_low, out_full)
    scale_two = norm_scale(middle)
    normed_two = (middle * scale_two * gain_two.astype(jnp.float32)).astype(low_type)
    gate = plain_dot(normed_two, gate_full)
    upward = plain_dot(normed_two, up_full)
    sigmoid = jax.nn.sigmoid(gate)
    hidden = (gate * sigmoid * upward).astype(low_type)
    result = (middle + plain_dot(hidden, down_full)).astype(low_type)
    grad_down = outer_sum(hidden, incoming)
    grad_hidden = times_transposed(incoming, down_full)
    grad_gate = (grad_hidden * upward * sigmoid * (1.0 + gate * (1.0 - sigmoid))).astype(low_type)
    grad_upward = (grad_hidden * gate * sigmoid).astype(low_type)
    grad_w_gate = outer_sum(normed_two, grad_gate)
    grad_w_up = outer_sum(normed_two, grad_upward)
    grad_normed_two = times_transposed(grad_gate, gate_full) + times_transposed(
        grad_upward, up_full
    )
    grad_gain_two = jnp.sum(grad_normed_two * middle * scale_two, axis=0)
    grad_middle = incoming.astype(jnp.float32) + norm_back(
        grad_normed_two * gain_two.astype(jnp.float32), middle, scale_two
    )
    ffn_shards = (
        lax.psum_scatter(
            grad_gain_two.astype(jnp.bfloat16), "fsdp", scatter_dimension=0, tiled=True
        ).astype(jnp.float32),
        lax.psum_scatter(
            grad_w_gate.astype(jnp.bfloat16), "fsdp", scatter_dimension=0, tiled=True
        ).astype(jnp.float32),
        lax.psum_scatter(
            grad_w_up.astype(jnp.bfloat16), "fsdp", scatter_dimension=0, tiled=True
        ).astype(jnp.float32),
        lax.psum_scatter(
            grad_down.astype(jnp.bfloat16), "fsdp", scatter_dimension=0, tiled=True
        ).astype(jnp.float32),
    )
    grad_branch = grad_middle.astype(low_type)
    grad_w_out = outer_sum(attended_low, grad_branch)
    attention_output_gradient = times_transposed(grad_branch, out_full).astype(low_type)
    gradient_heads = attention_output_gradient.reshape(
        row_total, KEY_VALUE_HEADS, group_width, HEAD_WIDTH
    )
    delta = jnp.sum(
        attention_output_gradient.astype(jnp.float32).reshape(
            row_total, KEY_VALUE_HEADS, group_width, HEAD_WIDTH
        )
        * attention_output.reshape(row_total, KEY_VALUE_HEADS, group_width, HEAD_WIDTH),
        axis=-1,
    )
    delta = jnp.transpose(delta, (1, 2, 0))
    block_length = all_ids.shape[0]

    def back_block(carry, parts, start_row):
        key_portion, value_portion = parts
        block_count = key_portion.shape[0]
        allowed = allowed_mask(place, own_ids, all_ids, start_row, block_count)

        def work(state):
            grad_query, key_gradient_rows, value_gradient_rows = state
            key_heads = key_portion.reshape(block_count, KEY_VALUE_HEADS, HEAD_WIDTH)
            value_heads = value_portion.reshape(block_count, KEY_VALUE_HEADS, HEAD_WIDTH)
            scores = score_block(query_heads_view, key_portion, allowed, scale)
            weights = jnp.where(allowed, jnp.exp(scores - log_total[..., None]), 0.0)
            weights_low = weights.astype(low_type)
            value_segment = jnp.einsum(
                "grtn,tgrd->ngd", weights_low, gradient_heads, preferred_element_type=jnp.float32
            )
            grad_weights = jnp.einsum(
                "tgrd,ngd->grtn", gradient_heads, value_heads, preferred_element_type=jnp.float32
            )
            grad_scores = (weights * (grad_weights - delta[..., None]) * scale).astype(low_type)
            grad_query = grad_query + jnp.einsum(
                "grtn,ngd->tgrd", grad_scores, key_heads, preferred_element_type=jnp.float32
            )
            key_segment = jnp.einsum(
                "grtn,tgrd->ngd", grad_scores, query_heads_view, preferred_element_type=jnp.float32
            )
            key_gradient_rows = lax.dynamic_update_slice_in_dim(
                key_gradient_rows,
                key_segment.reshape(block_count, KEY_VALUE_HEADS * HEAD_WIDTH),
                start_row,
                0,
            )
            value_gradient_rows = lax.dynamic_update_slice_in_dim(
                value_gradient_rows,
                value_segment.reshape(block_count, KEY_VALUE_HEADS * HEAD_WIDTH),
                start_row,
                0,
            )
            return (grad_query, key_gradient_rows, value_gradient_rows)

        return settle(allowed, work, carry)

    back_init = (
        jnp.zeros((row_total, KEY_VALUE_HEADS, group_width, HEAD_WIDTH), jnp.float32),
        jnp.zeros((block_length, KEY_VALUE_HEADS * HEAD_WIDTH), jnp.float32),
        jnp.zeros((block_length, KEY_VALUE_HEADS * HEAD_WIDTH), jnp.float32),
    )
    grad_query, key_gradient_rows, value_gradient_rows = over_blocks(
        back_block,
        back_init,
        (
            lax.all_gather(key_rows, "ctx", axis=0, tiled=True),
            lax.all_gather(value_rows, "ctx", axis=0, tiled=True),
        ),
        row_total,
    )
    key_grad, value_grad = (
        lax.psum_scatter(
            key_gradient_rows.astype(jnp.bfloat16), "ctx", scatter_dimension=0, tiled=True
        ).astype(jnp.float32),
        lax.psum_scatter(
            value_gradient_rows.astype(jnp.bfloat16), "ctx", scatter_dimension=0, tiled=True
        ).astype(jnp.float32),
    )
    grad_query_low = rotate(
        grad_query.reshape(row_total, QUERY_HEADS * HEAD_WIDTH), -angles, HEAD_WIDTH
    ).astype(low_type)
    grad_key_low = rotate(key_grad, -angles, HEAD_WIDTH).astype(low_type)
    grad_value_low = value_grad.astype(low_type)
    grad_w_query = outer_sum(normed, grad_query_low)
    grad_w_key = outer_sum(normed, grad_key_low)
    grad_w_value = outer_sum(normed, grad_value_low)
    grad_normed = (
        times_transposed(grad_query_low, query_full)
        + times_transposed(grad_key_low, key_full)
        + times_transposed(grad_value_low, value_full)
    )
    grad_gain_one = jnp.sum(grad_normed * inputs * scale_one, axis=0)
    grad_inputs = (
        grad_middle + norm_back(grad_normed * gain_one.astype(jnp.float32), inputs, scale_one)
    ).astype(low_type)
    attn_shards = (
        lax.psum_scatter(
            grad_gain_one.astype(jnp.bfloat16), "fsdp", scatter_dimension=0, tiled=True
        ).astype(jnp.float32),
        lax.psum_scatter(
            grad_w_query.astype(jnp.bfloat16), "fsdp", scatter_dimension=0, tiled=True
        ).astype(jnp.float32),
        lax.psum_scatter(
            grad_w_key.astype(jnp.bfloat16), "fsdp", scatter_dimension=0, tiled=True
        ).astype(jnp.float32),
        lax.psum_scatter(
            grad_w_value.astype(jnp.bfloat16), "fsdp", scatter_dimension=0, tiled=True
        ).astype(jnp.float32),
        lax.psum_scatter(
            grad_w_out.astype(jnp.bfloat16), "fsdp", scatter_dimension=0, tiled=True
        ).astype(jnp.float32),
    )
    finals = (
        lax.psum(attn_shards[0].astype(jnp.bfloat16), ("dp", "ctx")).astype(jnp.float32),
        lax.psum(attn_shards[1].astype(jnp.bfloat16), ("dp", "ctx")).astype(jnp.float32),
        lax.psum(attn_shards[2].astype(jnp.bfloat16), ("dp", "ctx")).astype(jnp.float32),
        lax.psum(attn_shards[3].astype(jnp.bfloat16), ("dp", "ctx")).astype(jnp.float32),
        lax.psum(attn_shards[4].astype(jnp.bfloat16), ("dp", "ctx")).astype(jnp.float32),
        lax.psum(ffn_shards[0].astype(jnp.bfloat16), ("dp", "ctx")).astype(jnp.float32),
        lax.psum(ffn_shards[1].astype(jnp.bfloat16), ("dp", "ctx")).astype(jnp.float32),
        lax.psum(ffn_shards[2].astype(jnp.bfloat16), ("dp", "ctx")).astype(jnp.float32),
        lax.psum(ffn_shards[3].astype(jnp.bfloat16), ("dp", "ctx")).astype(jnp.float32),
    )
    return (
        result[None],
        grad_inputs[None],
        finals[0],
        finals[1],
        finals[2],
        finals[3],
        finals[4],
        finals[5],
        finals[6],
        finals[7],
        finals[8],
    )


def solution(mesh):
    in_specs = (
        P(("dp", "fsdp"), "ctx", None),
        P(("dp", "fsdp"), "ctx"),
        P(("dp", "fsdp"), "ctx", None),
        P("fsdp"),
        P("fsdp", None),
        P("fsdp", None),
        P("fsdp", None),
        P("fsdp", None),
        P("fsdp"),
        P("fsdp", None),
        P("fsdp", None),
        P("fsdp", None),
    )
    out_specs = (
        P(("dp", "fsdp"), "ctx", None),
        P(("dp", "fsdp"), "ctx", None),
        P("fsdp"),
        P("fsdp", None),
        P("fsdp", None),
        P("fsdp", None),
        P("fsdp", None),
        P("fsdp"),
        P("fsdp", None),
        P("fsdp", None),
        P("fsdp", None),
    )
    return jax.shard_map(shards, mesh=mesh, in_specs=in_specs, out_specs=out_specs, check_vma=False)
```

profile of v0, /device:TPU:0, one launch (start us, length us, event | category | flops | bytes accessed | tf_op | source)
XLA Modules:
  0.0 1370.3 jit_solution(13048984218736859313)
XLA Ops:
  20.0 34.8 %all_gather.41 = bf16[1152,384]{1,0:T(8,128)(2,1)S(1)} all-gather(bf16[288,384]{1,0:T(8,128)(2,1)S(1)} %convert_element_type.257), channel_id=1, replica_groups=mesh['dp'=4,'ctx'=2,'fsdp'=4] {'fsdp'}, dimensions={0}, use_global_device_ids=true | all-gather | bytes 1105920 | tf_op jit(solution)/shard_map/all_gather | solution.py:119
  58.1 13.4 all-reduce.7
  77.4 19.5 %all_gather.44 = bf16[1152,384]{1,0:T(8,128)(2,1)S(1)} all-gather(bf16[288,384]{1,0:T(8,128)(2,1)S(1)} %convert_element_type.263), channel_id=1, replica_groups=mesh['dp'=4,'ctx'=2,'fsdp'=4] {'fsdp'}, dimensions={0}, use_global_device_ids=true | all-gather | bytes 1105920 | tf_op jit(solution)/shard_map/all_gather | solution.py:120
  129.7 22.4 %while.51 = (s32[]{:T(128)}, f32[6,3,512]{2,1,0:T(4,128)S(1)}, f32[6,3,512]{2,1,0:T(4,128)S(1)}, s32[1024]{0:T(1024)S(1)}, s32[1,512]{1,0:T(1,128)S(1)}, /*index...) while((s32[]{:T(128)}, f32[6,3,512]{2,1,0:T(4,128)S(1)}, ...), condition=%wide.region_9.10_spmd.clone, body=%wide.region_3.9_spmd.clone.sunk | while | flops 642796544 | bytes 41390360 | solution.py:92
  131.4 19.0 %conditional.9 = ((f32[6,3,512]{2,1,0:T(4,128)S(1)}, f32[6,3,512]{2,1,0:T(4,128)S(1)})) conditional(s32[]{:T(128)} %convert_element_type.417, (f32[6,3,512]{2,1,0:T(4,128)S(1)}, f32[6,3,512]{2,1,0:T(4,128)S(1)}) %tuple.169, (pred[512,512]{0,1:T(8,128)(4,1)S(1)}, bf16[1024,384]{0,1:T(8,128)(2,1)S(1)}, s32[]{:T(128)}, ...), branch_computations={%region_5.5_spmd, %region_6.0_spmd} | conditional | flops 641746944 | bytes 41111580 | solution.py:80
  139.5 10.8 select_reduce_fusion
  153.9 12.9 while.52
  176.5 95.7 %all-gather.11.cloned.1.call-done = bf16[1152,3072]{1,0:T(8,128)(2,1)} async-done(((bf16[288,3072]{1,0:T(8,128)(2,1)}), bf16[1152,3072]{1,0:T(8,128)(2,1)}) %all-gather.11.cloned.1.call-update) | async-done | bytes 7077904 | tf_op jit(solution)/shard_map/all_gather | solution.py:125
  281.4 119.4 %all-gather.13.cloned.1.call-done = bf16[1152,3072]{1,0:T(8,128)(2,1)} async-done(((bf16[288,3072]{1,0:T(8,128)(2,1)}), bf16[1152,3072]{1,0:T(8,128)(2,1)}) %all-gather.13.cloned.1.call-update) | async-done | bytes 7077904 | tf_op jit(solution)/shard_map/all_gather | solution.py:126
  409.8 118.8 %all-gather.15.cloned.1.call-done = bf16[3072,1152]{1,0:T(8,128)(2,1)} async-done(((bf16[768,1152]{1,0:T(8,128)(2,1)}), bf16[3072,1152]{1,0:T(8,128)(2,1)}) %all-gather.15.cloned.1.call-update) | async-done | bytes 7077904 | tf_op jit(solution)/shard_map/all_gather | solution.py:127
  528.6 12.1 multiply_convert_fusion
  567.7 46.9 %while.53 = (s32[]{:T(128)}, f32[512,6,3,64]{0,3,2,1:T(8,128)S(1)}, bf16[1024,384]{0,1:T(8,128)(2,1)}, bf16[1024,384]{0,1:T(8,128)(2,1)}, s32[1024]{0:T(1024)S(1...) while((s32[]{:T(128)}, f32[512,6,3,64]{0,3,2,1:T(8,128)S(1)}, ...), condition=%wide.region_22.23_spmd.clone, body=%wide.region_18.0_spmd.clone.sunk | while | flops 3082880000 | bytes 161510160 | solution.py:92
  570.2 42.0 %conditional.11 = ((f32[512,6,3,64]{0,3,2,1:T(8,128)S(1)}, bf16[1024,384]{0,1:T(8,128)(2,1)}, bf16[1024,384]{0,1:T(8,128)(2,1)})) conditional(s32[]{:T(128)} %convert_element_type.419, (f32[512,6,3,64]{0,3,2,1:T(8,128)S(1)}, bf16[1024,384]{0,1:T(8,128)(2,1)}, bf16[1024,384]{0,1:T(8,128)(2,1)}) %tuple.178, (pred[512,512]{0,1:T(8,128)(4,1)}, ...), branch_computations={%region_20.20_spmd, %region_21.21_spmd} | conditional | flops 3081830400 | bytes 161231264 | solution.py:80
  579.2 11.1 fusion.23
  615.4 56.9 %reduce-scatter.10.cloned.1.call-done = bf16[512,384]{0,1:T(8,128)(2,1)} async-done(((bf16[1024,384]{0,1:T(8,128)(2,1)}), bf16[512,384]{0,1:T(8,128)(2,1)}) %reduce-scatter.10.cloned.1.call-update) | async-done | bytes 393232 | tf_op jit(solution)/shard_map/reduce_scatter | solution.py:298
  677.6 14.5 %reduce-scatter.12.cloned.1.call-done = bf16[512,384]{0,1:T(8,128)(2,1)} async-done(((bf16[1024,384]{0,1:T(8,128)(2,1)}), bf16[512,384]{0,1:T(8,128)(2,1)}) %reduce-scatter.12.cloned.1.call-update) | async-done | bytes 393232 | tf_op jit(solution)/shard_map/reduce_scatter | solution.py:301
  745.7 53.8 %reduce-scatter.14.cloned.1.call-done = bf16[288,1152]{1,0:T(8,128)(2,1)} async-done(((bf16[1152,1152]{1,0:T(8,128)(2,1)}), bf16[288,1152]{1,0:T(8,128)(2,1)}) %reduce-scatter.14.cloned.1.call-update) | async-done | bytes 663568 | tf_op jit(solution)/shard_map/reduce_scatter | solution.py:326
  799.5 54.7 %reduce-scatter.20.cloned.1.call-done = bf16[288,1152]{1,0:T(8,128)(2,1)} async-done(((bf16[1152,1152]{1,0:T(8,128)(2,1)}), bf16[288,1152]{1,0:T(8,128)(2,1)}) %reduce-scatter.20.cloned.1.call-update) | async-done | bytes 663568 | tf_op jit(solution)/shard_map/reduce_scatter | solution.py:335
  854.2 125.4 %reduce-scatter.22.cloned.1.call-done = bf16[288,3072]{1,0:T(8,128)(2,1)} async-done(((bf16[1152,3072]{1,0:T(8,128)(2,1)}), bf16[288,3072]{1,0:T(8,128)(2,1)}) %reduce-scatter.22.cloned.1.call-update) | async-done | bytes 1769488 | tf_op jit(solution)/shard_map/reduce_scatter | solution.py:216
  979.6 126.4 %reduce-scatter.24.cloned.1.call-done = bf16[288,3072]{1,0:T(8,128)(2,1)} async-done(((bf16[1152,3072]{1,0:T(8,128)(2,1)}), bf16[288,3072]{1,0:T(8,128)(2,1)}) %reduce-scatter.24.cloned.1.call-update) | async-done | bytes 1769488 | tf_op jit(solution)/shard_map/reduce_scatter | solution.py:219
  1105.9 126.2 %reduce-scatter.26.cloned.1.call-done = bf16[768,1152]{1,0:T(8,128)(2,1)} async-done(((bf16[3072,1152]{1,0:T(8,128)(2,1)}), bf16[768,1152]{1,0:T(8,128)(2,1)}) %reduce-scatter.26.cloned.1.call-update) | async-done | bytes 1769488 | tf_op jit(solution)/shard_map/reduce_scatter | solution.py:222
  1249.8 11.8 all-reduce.6
  1263.6 15.0 %all-reduce.4 = (bf16[288]{0:T(512)(128)(2,1)}, bf16[288]{0:T(512)(128)(2,1)}) all-reduce(bf16[288]{0:T(512)(128)(2,1)S(1)} %dynamic-slice.3, bf16[288]{0:T(512)(128)(2,1)} %dynamic-slice.5), channel_id=1, replica_groups=mesh['dp'=4,'ctx'=2,'fsdp'=4] {'dp','ctx'}, use_global_device_ids=true, to_apply=%region_28.29 | all-reduce | flops 576 | bytes 2304 | tf_op jit(solution)/shard_map/psum | solution.py:340
  1285.1 65.9 %all-reduce.10.cloned.1.call-done = (bf16[288,1152]{1,0:T(8,128)(2,1)}, bf16[288,384]{1,0:T(8,128)(2,1)}, bf16[288,384]{1,0:T(8,128)(2,1)}, bf16[288,1152]{1,0:T...) async-done(((bf16[288,1152]{1,0:T(8,128)(2,1)}, bf16[288,384]{1,0:T(8,128)(2,1)}, bf16[288,384]{1,0:T(8,128)(2,1)}, ...) | async-done | bytes 7077904 | tf_op jit(solution)/shard_map/psum | solution.py:341
  (272 shorter events, 272.7 us)
Async XLA Ops:
  7.2 113.1 %all-gather.7.cloned.1.call-start = ((), (), s32[]{:S(2)}) async-start(), calls=%async_computation.9 | async-start | bytes 3317760 | tf_op jit(solution)/shard_map/all_gather | solution.py:118
  9.6 160.6 %all-gather.9.cloned.1.call-start = ((), (), s32[]{:S(2)}) async-start(), calls=%async_computation.10 | async-start | bytes 3317760 | tf_op jit(solution)/shard_map/all_gather | solution.py:121
  11.9 260.3 %all-gather.11.cloned.1.call-start = ((), (), s32[]{:S(2)}) async-start(), calls=%async_computation.11 | async-start | bytes 8847360 | tf_op jit(solution)/shard_map/all_gather | solution.py:125
  13.5 387.2 %all-gather.13.cloned.1.call-start = ((), (), s32[]{:S(2)}) async-start(), calls=%async_computation.12 | async-start | bytes 8847360 | tf_op jit(solution)/shard_map/all_gather | solution.py:126
  17.2 511.5 %all-gather.15.cloned.1.call-start = ((), (), s32[]{:S(2)}) async-start(), calls=%async_computation.13 | async-start | bytes 8847360 | tf_op jit(solution)/shard_map/all_gather | solution.py:127
  18.7 57.7 %copy-start.36 = (f32[288,384]{1,0:T(8,128)S(1)}, f32[288,384]{1,0:T(8,128)}, u32[]{:S(2)}) copy-start(f32[288,384]{1,0:T(8,128)} %param.30) | copy-start | bytes 1327108
  18.7 57.7 %copy-start.8 = (bf16[1,512,1152]{2,1,0:T(8,128)(2,1)S(1)}, bf16[1,512,1152]{2,1,0:T(8,128)(2,1)}, u32[]{:S(2)}) copy-start(bf16[1,512,1152]{2,1,0:T(8,128)(2,1)} %param.24) | copy-start | bytes 3538948
  18.7 653.6 %reduce-scatter.10.cloned.1.call-start = ((), (), s32[]{:S(2)}) async-start(), calls=%async_computation.14 | async-start | bytes 1179648 | tf_op jit(solution)/shard_map/reduce_scatter | solution.py:298
  71.5 54.1 %copy-start.39 = (f32[1152]{0:T(1024)}, f32[1152]{0:T(1024)S(1)}, u32[]{:S(2)}) copy-start(f32[1152]{0:T(1024)S(1)} %convert_element_type.254) | copy-start | bytes 13828
  175.5 96.8 %copy-start.46 = (f32[512]{0:T(512)}, f32[512]{0:T(512)S(1)}, u32[]{:S(2)}) copy-start(f32[512]{0:T(512)S(1)} %get-tuple-element.996) | copy-start | bytes 6148
  176.5 224.2 %copy-start.32 = (bf16[512,1152]{1,0:T(8,128)(2,1)}, bf16[512,1152]{1,0:T(8,128)(2,1)S(1)}, u32[]{:S(2)}) copy-start(bf16[512,1152]{1,0:T(8,128)(2,1)S(1)} %multiply_convert_fusion.3) | copy-start | bytes 3538948
  281.4 247.2 %copy-start.31 = (bf16[1,512,1152]{2,1,0:T(8,128)(2,1)S(1)}, bf16[1,512,1152]{2,1,0:T(8,128)(2,1)}, u32[]{:S(2)}) copy-start(bf16[1,512,1152]{2,1,0:T(8,128)(2,1)} %param.26) | copy-start | bytes 3538948
  614.6 60.7 %copy-start.9 = (bf16[1,512,1152]{2,1,0:T(8,128)(2,1)S(1)}, bf16[1,512,1152]{2,1,0:T(8,128)(2,1)}, u32[]{:S(2)}) copy-start(bf16[1,512,1152]{2,1,0:T(8,128)(2,1)} %param.24) | copy-start | bytes 3538948
  614.6 60.7 %copy-start.40 = (f32[1152]{0:T(1024)S(1)}, f32[1152]{0:T(1024)}, u32[]{:S(2)}) copy-start(f32[1152]{0:T(1024)} %copy-done.39) | copy-start | bytes 13828
  614.6 60.6 %copy-start.45 = (f32[512]{0:T(512)S(1)}, f32[512]{0:T(512)}, u32[]{:S(2)}) copy-start(f32[512]{0:T(512)} %copy-done.44) | copy-start | bytes 6148
  614.6 77.5 %reduce-scatter.12.cloned.1.call-start = ((), (), s32[]{:S(2)}) async-start(), calls=%async_computation.15 | async-start | bytes 1179648 | tf_op jit(solution)/shard_map/reduce_scatter | solution.py:301
  615.4 119.8 %reduce-scatter.16.cloned.1.call-start = ((), (), s32[]{:S(2)}) async-start(), calls=%async_computation.17 | async-start | bytes 1105920 | tf_op jit(solution)/shard_map/reduce_scatter | solution.py:329
  677.2 68.5 %reduce-scatter.18.cloned.1.call-start = ((), (), s32[]{:S(2)}) async-start(), calls=%async_computation.18 | async-start | bytes 1105920 | tf_op jit(solution)/shard_map/reduce_scatter | solution.py:332
  695.1 104.4 %reduce-scatter.14.cloned.1.call-start = ((), (), s32[]{:S(2)}) async-start(), calls=%async_computation.16 | async-start | bytes 3317760 | tf_op jit(solution)/shard_map/reduce_scatter | solution.py:326
  701.0 153.2 %reduce-scatter.20.cloned.1.call-start = ((), (), s32[]{:S(2)}) async-start(), calls=%async_computation.19 | async-start | bytes 3317760 | tf_op jit(solution)/shard_map/reduce_scatter | solution.py:335
  707.2 272.4 %reduce-scatter.22.cloned.1.call-start = ((), (), s32[]{:S(2)}) async-start(), calls=%async_computation.20 | async-start | bytes 8847360 | tf_op jit(solution)/shard_map/reduce_scatter | solution.py:216
  716.3 389.7 %reduce-scatter.24.cloned.1.call-start = ((), (), s32[]{:S(2)}) async-start(), calls=%async_computation.21 | async-start | bytes 8847360 | tf_op jit(solution)/shard_map/reduce_scatter | solution.py:219
  725.4 506.8 %reduce-scatter.26.cloned.1.call-start = ((), (), s32[]{:S(2)}) async-start(), calls=%async_computation.22 | async-start | bytes 8847360 | tf_op jit(solution)/shard_map/reduce_scatter | solution.py:222
  735.1 615.9 %all-reduce.10.cloned.1.call-start = ((), (), s32[]{:S(2)}) async-start(), calls=%async_computation.23 | async-start | bytes 14155776 | tf_op jit(solution)/shard_map/psum | solution.py:341
  (47 other events, 460.9 us)
Sparse Core Ops, SparseCore 0:
  10.2 77.2 all-gather.6
  89.6 53.4 all-gather.8
  145.3 126.9 all-gather.10
  274.3 126.4 all-gather.12
  402.2 126.4 all-gather.14
  614.8 57.5 reduce-scatter.9
  674.7 17.4 reduce-scatter.11
  695.1 24.5 reduce-scatter.15
  722.0 23.6 reduce-scatter.17
  747.8 51.6 reduce-scatter.13
  801.8 52.3 reduce-scatter.19
  856.4 123.1 reduce-scatter.21
  981.9 124.0 reduce-scatter.23
  1108.1 123.9 reduce-scatter.25
  1236.1 114.9 all-reduce.9
where the time goes:
time: 1380 us; the launch traced here: 1370 us
  waiting for transfers between devices  969 us (70%)
  matrix products  169 us (12%)
  blocking collectives  117 us (8%)
  other arithmetic  63.5 us (5%)
  local copies, waits for them, and re-layouts  29.1 us (2%)
  between operations  16.1 us (1%)
    reduce_scatter x1, waiting for transfers between devices, shards(): lax.psum_scatter(grad_w_up.astype(jnp.bfloat16), 'fsdp', scatter_dimensio...  126 us
    reduce_scatter x1, waiting for transfers between devices, shards(): lax.psum_scatter(grad_down.astype(jnp.bfloat16), 'fsdp', scatter_dimensio...  126 us
    reduce_scatter x1, waiting for transfers between devices, shards(): lax.psum_scatter(grad_w_gate.astype(jnp.bfloat16), 'fsdp', scatter_dimens...  125 us
    all_gather x1, waiting for transfers between devices, shards(): lax.all_gather(w_up.astype(low_type), 'fsdp', axis=0, tiled=True)  119 us
    all_gather x1, waiting for transfers between devices, shards(): lax.all_gather(w_down.astype(low_type), 'fsdp', axis=0, tiled=True)  119 us
    all_gather x1, waiting for transfers between devices, shards(): lax.all_gather(w_gate.astype(low_type), 'fsdp', axis=0, tiled=True)  95.7 us
    psum x1, waiting for transfers between devices, shards(): lax.psum(attn_shards[1].astype(jnp.bfloat16), ('dp', 'ctx'))  65.9 us
    reduce_scatter x1, waiting for transfers between devices, shards(): lax.psum_scatter(key_gradient_rows.astype(jnp.bfloat16), 'ctx', scatter_d...  56.9 us
  transfers between devices with their start and end apart: 15, of which 12 were waited for; matrix products, arithmetic and copies ran while one was open for 12% of the time, Pallas kernels for 0%

commit v1 on v0

v1 whole, which is shorter than its diff:
```python
import math

import jax
import jax.numpy as jnp
from jax import lax
from jax.experimental import pallas as pl
from jax.experimental.pallas import tpu as pltpu
from jax.sharding import Mesh
from jax.sharding import PartitionSpec as P

QUERY_HEADS = 18
KEY_VALUE_HEADS = 6
HEAD_WIDTH = 64
TURN = HEAD_WIDTH // 2
GROUP = QUERY_HEADS // KEY_VALUE_HEADS
GROUPS = KEY_VALUE_HEADS // 2
HALF_QUERY = QUERY_HEADS // 2 * HEAD_WIDTH
HALF_KEY = GROUPS * HEAD_WIDTH
CHUNKS = 3
BLOCKS = 4

low_type = jnp.bfloat16
eps_norm = 1e-05
masked_score = -1e30
lowest_peak = -1e20
LOG2E = math.log2(math.e)
SCORE_SCALE = HEAD_WIDTH ** (-0.5)
VMEM_LIMIT = 58 * 1024 * 1024

PAIR = [(0, 1), (1, 0)]
ANY = pl.BlockSpec(memory_space=pl.ANY)
SCALARS = pl.BlockSpec(memory_space=pltpu.SMEM)


def inverse_freq():
    return 10000.0 ** (-(jnp.arange(TURN, dtype=jnp.float32) * 2.0) / HEAD_WIDTH)


def norm_scale(value):
    return lax.rsqrt(jnp.mean(value * value, axis=-1, keepdims=True) + eps_norm)


def norm_back(scaled, value, scale):
    return scale * scaled - value * scale**3 * jnp.mean(scaled * value, axis=-1, keepdims=True)


def dot(left, right, over=(1, 0)):
    return lax.dot_general(
        left, right, (((over[0],), (over[1],)), ((), ())), preferred_element_type=jnp.float32
    )


def swap_core(value):
    return lax.ppermute(value, "core", PAIR)


def params():
    return pltpu.CompilerParams(vmem_limit_bytes=VMEM_LIMIT)


def cost(flops, moved, special=0):
    return pl.CostEstimate(flops=int(flops), bytes_accessed=int(moved), transcendentals=int(special))


def shape(dims, kind=low_type):
    return jax.ShapeDtypeStruct(tuple(dims), kind)


def pack_attn_kernel(info, q_ref, k_ref, v_ref, o_ref, own_ref, *piece_ref):
    def half(ref):
        size = ref.shape[1] // 2
        value = ref[...].astype(low_type)
        return jnp.where(info[0] == 0, value[:, :size], value[:, size:])

    own_ref[...] = jnp.concatenate([half(r) for r in (q_ref, k_ref, v_ref, o_ref)], axis=1)
    for ref in piece_ref:
        part = ref.shape[1]
        ref[...] = own_ref[:, pl.ds(pl.multiple_of(info[1] * part, part), part)]


def pack_attn(info, arrays, tuned):
    rows = arrays[0].shape[0]
    width = sum(a.shape[1] for a in arrays) // 2
    outs = [shape((rows, width))] + [shape((rows, width // BLOCKS))] * tuned
    return pl.pallas_call(
        pack_attn_kernel,
        in_specs=[SCALARS] + [pl.BlockSpec()] * 4,
        out_specs=[pl.BlockSpec()] * len(outs),
        out_shape=outs,
        compiler_params=params(),
        cost_estimate=cost(0, rows * width * 10),
    )(info, *arrays)


def pack_ffn_kernel(info, gate_ref, up_ref, down_ref, own_ref, *piece_ref):
    step, steps = pl.program_id(0), pl.num_programs(0)
    part = gate_ref.shape[1] // CHUNKS
    rows = gate_ref.shape[0]
    blocks = own_ref.shape[2] // part // 3
    for c in range(CHUNKS):
        at = slice(c * part, (c + 1) * part)
        here = pl.ds(pl.multiple_of(step * part, part), part)
        own_ref[c, :, here] = gate_ref[:, at].astype(low_type)
        there = pl.ds(pl.multiple_of((blocks + step) * part, part), part)
        own_ref[c, :, there] = up_ref[:, at].astype(low_type)

    @pl.when(step == 0)
    def _():
        turned = down_ref[...].astype(low_type).T
        for c in range(CHUNKS):
            for q in range(blocks):
                own_ref[c, :, (2 * blocks + q) * part : (2 * blocks + q + 1) * part] = turned[
                    q * rows : (q + 1) * rows, c * part : (c + 1) * part
                ]

    @pl.when(step == steps - 1)
    def _():
        for c, ref in enumerate(piece_ref):
            size = ref.shape[1]
            ref[...] = own_ref[c, :, pl.ds(pl.multiple_of(info[1] * size, size), size)]


def pack_ffn(info, gate, up, down, tuned):
    rows, hidden = gate.shape
    hidden_rows, width = down.shape
    steps = hidden // hidden_rows
    half = hidden_rows // 2
    packed = 3 * steps * (half // CHUNKS)
    outs = [shape((CHUNKS, rows, packed))] + [shape((rows, packed // BLOCKS))] * (CHUNKS * tuned)
    columns = pl.BlockSpec((rows, half), lambda z, info: (0, 2 * z + info[0]))
    return pl.pallas_call(
        pack_ffn_kernel,
        grid_spec=pltpu.PrefetchScalarGridSpec(
            num_scalar_prefetch=1,
            grid=(steps,),
            in_specs=[columns, columns, pl.BlockSpec((half, width), lambda z, info: (info[0], 0))],
            out_specs=[pl.BlockSpec((CHUNKS, rows, packed), lambda z, info: (0, 0, 0))]
            + [pl.BlockSpec((rows, packed // BLOCKS), lambda z, info: (0, 0))] * (CHUNKS * tuned),
        ),
        out_shape=outs,
        compiler_params=params(),
        cost_estimate=cost(0, rows * packed * CHUNKS * 6),
    )(info, gate, up, down)


def ring(count, step):
    return [(i, (i + step) % count) for i in range(count)]


def assemble_kernel(count, info, own_ref, *refs):
    pieces, out_ref, sems = refs[:-2], refs[-2], refs[-1]
    rows = own_ref.shape[0]
    part = out_ref.shape[2]
    copies = []

    def begin(source, block, row):
        target = out_ref.at[block, pl.ds(pl.multiple_of(row * rows, rows), rows), :]
        copies.append(pltpu.make_async_copy(source, target, sems.at[len(copies)]))
        copies[-1].start()

    for b in range(BLOCKS):
        begin(own_ref.at[:, b * part : (b + 1) * part], b, info[2])
    for flip in range(BLOCKS):
        for k in range(1, count):
            begin(
                pieces[flip * (count - 1) + k - 1],
                jnp.bitwise_xor(info[1], flip),
                lax.rem(info[2] + count - k, count),
            )
    for copy in copies:
        copy.wait()


def assemble(info, own, pieces, count):
    rows, width = own.shape
    out = shape((BLOCKS, rows * count, width // BLOCKS))

    def kernel(*refs):
        assemble_kernel(count, *refs)

    return pl.pallas_call(
        kernel,
        in_specs=[SCALARS] + [ANY] * (1 + len(pieces)),
        out_specs=pl.BlockSpec(),
        out_shape=out,
        scratch_shapes=[pltpu.SemaphoreType.DMA((BLOCKS * count,))],
        compiler_params=params(),
        cost_estimate=cost(0, rows * width * count * 4),
    )(info, own, *pieces)


def gather_weights(info, own, piece, sizes, turn):
    nz = sizes[2]
    if piece is None:
        full = lax.all_gather(own, "z", axis=0, tiled=True)
        return full.reshape(full.shape[0], BLOCKS, -1).transpose(1, 0, 2)
    slots = [lax.ppermute(piece, "z", ring(nz, k)) for k in range(1, nz)]
    by_x = [lax.ppermute(s, "x", PAIR) for s in slots]
    by_y = [lax.ppermute(s, "y", PAIR) for s in slots]
    far = [
        lax.ppermute(by_x[k], "y", PAIR) if (k + turn) % 2 else lax.ppermute(by_y[k], "x", PAIR)
        for k in range(nz - 1)
    ]
    return assemble(info, own, slots + by_x + by_y + far, nz)


def send_out(info, packed, outs, sems):
    copies = []

    def begin(source, target):
        copies.append(pltpu.make_async_copy(source, target, sems.at[len(copies)]))
        copies[-1].start()

    if len(outs) == 1:
        begin(packed, outs[0])
    else:
        keep_one, send_one, keep_two, send_two = outs
        cut = packed.shape[1] // 2
        y, x = lax.div(info[1], 2), lax.rem(info[1], 2)
        for i in range(2):
            at_y, at_x = jnp.bitwise_xor(y, i), jnp.bitwise_xor(x, i)
            begin(packed.at[at_y * 2 + x, :cut], keep_one.at[i])
            begin(packed.at[at_y * 2 + 1 - x, :cut], send_one.at[i])
            begin(packed.at[y * 2 + at_x, cut:], keep_two.at[i])
            begin(packed.at[(1 - y) * 2 + at_x, cut:], send_two.at[i])
    for copy in copies:
        copy.wait()


def sent_shapes(rows, part, tuned):
    if tuned:
        return [shape((2, rows // 2, part))] * 4
    return [shape((BLOCKS, rows, part))]


def sum_over(value, axis, count):
    if count & (count - 1):
        return lax.psum(value, axis)
    step = 1
    while step < count:
        value = value + lax.ppermute(value, axis, [(i, i ^ step) for i in range(count)])
        step *= 2
    return value


def add_low(kept, came):
    return (kept.astype(jnp.float32) + came.astype(jnp.float32)).astype(low_type)


def scatter_gradients(outs, sizes):
    ny, nx, nz = sizes
    if len(outs) == 1:
        packed = outs[0]
        total = packed.shape[1]
        split = packed.transpose(1, 0, 2).reshape(total, ny * nx, -1).transpose(1, 0, 2)
        mine = lax.psum_scatter(split, ("y", "x"), scatter_dimension=0, tiled=True)[0]
    else:
        keep_one, send_one, keep_two, send_two = outs
        came_one = lax.ppermute(send_one, "x", PAIR)
        came_two = lax.ppermute(send_two, "y", PAIR)
        one = lax.ppermute(add_low(keep_one[1], came_one[1]), "y", PAIR)
        two = lax.ppermute(add_low(keep_two[1], came_two[1]), "x", PAIR)
        one = add_low(add_low(keep_one[0], came_one[0]), one)
        two = add_low(add_low(keep_two[0], came_two[0]), two)
        mine = jnp.concatenate([one, two])
    return lax.psum_scatter(mine, "z", scatter_dimension=0, tiled=True)


def spread(mine, sizes):
    everyone = lax.all_gather(mine, ("core", "y", "x"), axis=0)
    both = everyone.reshape((2, sizes[0] * sizes[1]) + mine.shape)
    if sizes[0] * sizes[1] == BLOCKS:
        return both
    both = jnp.moveaxis(both, 1, -2).reshape((2,) + mine.shape[:2] + (BLOCKS, -1))
    return jnp.moveaxis(both, -2, 1)


def turn_heads(ref, value, cosine, sine, start):
    for h in range(value.shape[0] // HEAD_WIDTH):
        former = value[h * HEAD_WIDTH : h * HEAD_WIDTH + TURN]
        latter = value[h * HEAD_WIDTH + TURN : (h + 1) * HEAD_WIDTH]
        at = start + h * HEAD_WIDTH
        ref[at : at + TURN, :] = (former * cosine - latter * sine).astype(ref.dtype)
        ref[at + TURN : at + HEAD_WIDTH, :] = (latter * cosine + former * sine).astype(ref.dtype)


def project_kernel(mine_ref, other_ref, gain_ref, w_ref, cos_ref, sin_ref, normed_ref, q_ref, kv_ref):
    rows = mine_ref.shape[0]
    hk, part = HALF_KEY, w_ref.shape[2]
    for i, ref in enumerate((mine_ref, other_ref)):
        value = ref[...].astype(jnp.float32)
        normed = (value * norm_scale(value) * gain_ref[...]).astype(low_type)
        at = slice(i * rows, (i + 1) * rows)
        normed_ref[:, at] = normed.T
    weights = [w_ref[0].T, w_ref[1].T, w_ref[2].T[:hk]]
    for i in range(2):
        at = slice(i * rows, (i + 1) * rows)
        normed = normed_ref[:, at]
        cosine, sine = cos_ref[:, at], sin_ref[:, at]
        first = dot(weights[0], normed)
        turn_heads(q_ref.at[:, at], first, cosine, sine, 0)
        second = dot(weights[1], normed)
        turn_heads(q_ref.at[:, at], second[: part - hk], cosine, sine, part)
        turn_heads(kv_ref.at[0, :, at], second[part - hk :], cosine, sine, 0)
        kv_ref[1, :, at] = dot(weights[2], normed).astype(low_type)


def project(mine, other, gain, weights, cosine, sine):
    rows, width = mine.shape
    return pl.pallas_call(
        project_kernel,
        in_specs=[pl.BlockSpec()] * 6,
        out_specs=[pl.BlockSpec()] * 3,
        out_shape=[
            shape((width, 2 * rows)), shape((HALF_QUERY, 2 * rows)), shape((2, HALF_KEY, 2 * rows))
        ],
        compiler_params=params(),
        cost_estimate=cost(4 * rows * width * 960, 14 << 20),
    )(mine, other, gain, weights, cosine, sine)


def tile_mask(first, place0, key0, size, causal):
    key_place = key0 + lax.broadcasted_iota(jnp.int32, (size, size), 0)
    allowed = key_place >= first
    if causal:
        place = place0 + lax.broadcasted_iota(jnp.int32, (size, size), 1)
        allowed = allowed & (key_place <= place)
    return jnp.concatenate([allowed] * GROUP, axis=1)


def heads_of(ref):
    return jnp.concatenate(
        [ref[r * HEAD_WIDTH : (r + 1) * HEAD_WIDTH, :] for r in range(GROUP)], axis=1
    )


def over_tiles(info, size, rows, turn):
    per = rows // size
    half = pl.program_id(2)
    own = info[3] * per
    hi = own + half
    lo = info[4 + pl.program_id(0) * per + half]

    def columns(b):
        return pl.ds(pl.multiple_of(lax.rem(b, per) * size, size), size)

    def earlier(b, _):
        turn(hi, b, lax.div(b, per), columns(b))
        return 0

    def here(b, _):
        turn(hi, b, None, columns(b))
        return 0

    lax.fori_loop(lo, own, earlier, 0)
    lax.fori_loop(jnp.maximum(lo, own), hi + 1, here, 0)


def attend_kernel(info, q_ref, kv_ref, past_ref, first_ref, o_ref, total_ref, peak_s, sum_s, acc_s):
    size, rows = q_ref.shape[1], kv_ref.shape[2]
    q = heads_of(q_ref)
    peak_s[...] = jnp.full(peak_s.shape, lowest_peak, jnp.float32)
    sum_s[...] = jnp.zeros(sum_s.shape, jnp.float32)
    acc_s[...] = jnp.zeros(acc_s.shape, jnp.float32)

    def turn(hi, b, past, at):
        k = kv_ref[0, :, at] if past is None else past_ref[past, 0, :, at]
        v = kv_ref[1, :, at] if past is None else past_ref[past, 1, :, at]
        allowed = tile_mask(first_ref[0], hi * size, b * size, size, past is None)
        scores = dot(k, q, (0, 0)) * (SCORE_SCALE * LOG2E)
        scores = jnp.where(allowed, scores, masked_score)
        peak = peak_s[...]
        fresh = jnp.maximum(peak, jnp.max(scores, axis=0, keepdims=True))
        shrink = jnp.exp2(peak - fresh)
        terms = jnp.exp2(scores - fresh)
        peak_s[...] = fresh
        sum_s[...] = sum_s[...] * shrink + jnp.sum(terms, axis=0, keepdims=True)
        acc_s[...] = acc_s[...] * shrink + dot(v, terms.astype(low_type))

    over_tiles(info, size, rows, turn)
    total = sum_s[...]
    mixed = acc_s[...] / total
    log_total = peak_s[...] + jnp.log2(total)
    for r in range(GROUP):
        o_ref[r * HEAD_WIDTH : (r + 1) * HEAD_WIDTH, :] = mixed[:, r * size : (r + 1) * size]
        total_ref[0, r : r + 1, :] = log_total[:, r * size : (r + 1) * size]


def attend_back_kernel(
    info, q_ref, kv_ref, past_ref, g_ref, first_ref, total_ref, delta_ref, dq_ref, dkv_ref, dpast_ref,
    acc_s, past_s,
):
    size, rows = q_ref.shape[1], kv_ref.shape[2]
    q = heads_of(q_ref)
    g = heads_of(g_ref)
    total = jnp.concatenate([total_ref[0, r : r + 1, :] for r in range(GROUP)], axis=1)
    delta = jnp.concatenate([delta_ref[0, r : r + 1, :] for r in range(GROUP)], axis=1)
    acc_s[...] = jnp.zeros(acc_s.shape, jnp.float32)

    @pl.when(pl.program_id(2) == 0)
    def _():
        dkv_ref[...] = jnp.zeros(dkv_ref.shape, jnp.float32)
        past_s[...] = jnp.zeros(past_s.shape, jnp.float32)

    def turn(hi, b, past, at):
        k = kv_ref[0, :, at] if past is None else past_ref[past, 0, :, at]
        v = kv_ref[1, :, at] if past is None else past_ref[past, 1, :, at]
        allowed = tile_mask(first_ref[0], hi * size, b * size, size, past is None)
        scores = dot(k, q, (0, 0)) * (SCORE_SCALE * LOG2E)
        weights = jnp.exp2(jnp.where(allowed, scores - total, masked_score))
        grad_weights = dot(v, g, (0, 0))
        grad_scores = (weights * (grad_weights - delta) * SCORE_SCALE).astype(low_type)
        dk = dot(q, grad_scores, (1, 1))
        dv = dot(g, weights.astype(low_type), (1, 1))
        if past is None:
            dkv_ref[0, :, at] += dk
            dkv_ref[1, :, at] += dv
        else:
            past_s[past, 0, :, at] += dk
            past_s[past, 1, :, at] += dv
        acc_s[...] += dot(k, grad_scores)

    over_tiles(info, size, rows, turn)
    acc = acc_s[...]
    for r in range(GROUP):
        dq_ref[r * HEAD_WIDTH : (r + 1) * HEAD_WIDTH, :] = acc[:, r * size : (r + 1) * size]

    @pl.when(pl.program_id(2) == pl.num_programs(2) - 1)
    def _():
        dpast_ref[...] = past_s[...].astype(low_type)


def attention_specs(parts, rows, size):
    per = rows // size
    wide = pl.BlockSpec((GROUP * HEAD_WIDTH, size), lambda s, g, h: (g, s * per + h))
    own = pl.BlockSpec((2, HEAD_WIDTH, rows), lambda s, g, h: (0, g, s))
    past = pl.BlockSpec((parts, 2, HEAD_WIDTH, rows), lambda s, g, h: (0, 0, g, s))
    first = pl.BlockSpec((1, 1, size), lambda s, g, h: (s, 0, h))
    stat = pl.BlockSpec((1, 8, size), lambda s, g, h: (g, 0, s * per + h))
    return (2, GROUPS, per), wide, own, past, first, stat


def attend(info, query, keyvalue, past, first, size):
    both = keyvalue.shape[2]
    rows = both // 2
    grid, wide, own, past_spec, first_spec, stat = attention_specs(past.shape[0], rows, size)
    pairs = 2 * rows * rows * 3 // 2
    return pl.pallas_call(
        attend_kernel,
        grid=grid,
        in_specs=[SCALARS, wide, own, past_spec, first_spec],
        out_specs=[wide, stat],
        out_shape=[shape(query.shape, jnp.float32), shape((GROUPS, 8, both), jnp.float32)],
        scratch_shapes=[
            pltpu.VMEM((1, GROUP * size), jnp.float32),
            pltpu.VMEM((1, GROUP * size), jnp.float32),
            pltpu.VMEM((HEAD_WIDTH, GROUP * size), jnp.float32),
        ],
        compiler_params=params(),
        cost_estimate=cost(pairs * 9 * 64 * 4 * 5, 8 << 20, pairs * 9),
    )(info, query, keyvalue, past, first)


def attend_back(info, query, keyvalue, past, grad, first, log_total, delta, size):
    both = keyvalue.shape[2]
    rows = both // 2
    grid, wide, own, past_spec, first_spec, stat = attention_specs(past.shape[0], rows, size)
    pairs = 2 * rows * rows * 3 // 2
    return pl.pallas_call(
        attend_back_kernel,
        grid=grid,
        in_specs=[SCALARS, wide, own, past_spec, wide, first_spec, stat, stat],
        out_specs=[wide, own, past_spec],
        out_shape=[
            shape(query.shape, jnp.float32), shape(keyvalue.shape, jnp.float32), shape(past.shape)
        ],
        scratch_shapes=[
            pltpu.VMEM((HEAD_WIDTH, GROUP * size), jnp.float32),
            pltpu.VMEM((past.shape[0], 2, HEAD_WIDTH, rows), jnp.float32),
        ],
        compiler_params=params(),
        cost_estimate=cost(pairs * 9 * 64 * 10 * 3, 12 << 20, pairs * 9),
    )(info, query, keyvalue, past, grad, first, log_total, delta)


def place_out(core, mine_ref, other_ref, out_ref):
    cut, part = HALF_KEY, mine_ref.shape[2]
    mine = jnp.concatenate([mine_ref[0][:, cut:], mine_ref[1]], axis=1)
    other = jnp.concatenate([other_ref[0][:, cut:], other_ref[1]], axis=1)
    out_ref[...] = jnp.where(
        core == 0,
        jnp.concatenate([mine, other], axis=1),
        jnp.concatenate([other, mine], axis=1),
    )


def out_kernel(
    info, mine_ref, came_ref, w_ref, w_other_ref, tokens_ref, gain_ref, middle_ref, normed_ref,
    turned_ref, rows_ref, w_s,
):
    place_out(info[0], w_ref, w_other_ref, w_s)
    hq = HALF_QUERY
    mine = w_s[pl.ds(pl.multiple_of(info[0] * hq, hq), hq), :]
    other = w_s[pl.ds(pl.multiple_of((1 - info[0]) * hq, hq), hq), :]
    rows_ref[...] = mine
    middle = (
        tokens_ref[...].astype(jnp.float32)
        + dot(mine_ref[...].astype(low_type).T, mine)
        + dot(came_ref[...].T, other)
    )
    middle_ref[...] = middle
    normed = (middle * norm_scale(middle) * gain_ref[...]).astype(low_type)
    normed_ref[...] = normed
    turned_ref[...] = normed.T


def project_out(info, attended, came, weights, weights_other, tokens, gain):
    rows, width = tokens.shape
    hq = HALF_QUERY
    part = weights.shape[2]
    return pl.pallas_call(
        out_kernel,
        grid=(1,),
        in_specs=[
            SCALARS,
            pl.BlockSpec((hq, rows), lambda i: (0, 0)),
            pl.BlockSpec((hq, rows), lambda i: (0, 0)),
            pl.BlockSpec((2, width, part), lambda i: (1, 0, 0)),
            pl.BlockSpec((2, width, part), lambda i: (0, 0, 0)),
            pl.BlockSpec((rows, width), lambda i: (0, 0)),
            pl.BlockSpec((1, width), lambda i: (0, 0)),
        ],
        out_specs=[
            pl.BlockSpec((rows, width), lambda i: (0, 0)),
            pl.BlockSpec((rows, width), lambda i: (0, 0)),
            pl.BlockSpec((width, rows), lambda i: (0, 0)),
            pl.BlockSpec((hq, width), lambda i: (0, 0)),
        ],
        out_shape=[
            shape((rows, width), jnp.float32), shape((rows, width)), shape((width, rows)),
            shape((hq, width)),
        ],
        scratch_shapes=[pltpu.VMEM((width, width), low_type)],
        compiler_params=params(),
        cost_estimate=cost(2 * rows * width * width, 16 << 20),
    )(info, attended, came, weights, weights_other, tokens, gain)


def ffn_kernel(held, info, *refs):
    x_refs, c_refs, xt_refs, ct_refs, w_ref = refs[0:2], refs[2:4], refs[4:6], refs[6:8], refs[8]
    sums = refs[9 : 9 + 2 * held]
    refs = refs[9 + 2 * held :]
    result_ref, grad_ref, outs = refs[0], refs[1], refs[2:-9]
    gate_s, up_s, down_s, hidden_s, dgate_s, dup_s, packed_s, _, sems = refs[-9:]
    step = pl.program_id(0)
    size = result_ref.shape[0]
    half = 2
    block = gate_s.shape[1]
    part = w_ref.shape[2]
    width = gate_s.shape[0]
    lane = block // BLOCKS
    rows = width // BLOCKS

    @pl.when(step == 0)
    def _():
        gate_s[:, :part] = w_ref[0]
        gate_s[:, part:] = w_ref[1, :, : block - part]
        up_s[:, : 2 * part - block] = w_ref[1, :, block - part :]
        up_s[:, 2 * part - block :] = w_ref[2, :, : 2 * block - 2 * part]
        for q in range(BLOCKS):
            for z in range(BLOCKS):
                column = 2 * block + q * lane
                b, at = column // part, column % part
                down_s[q * rows : (q + 1) * rows, z * lane : (z + 1) * lane] = w_ref[
                    b, z * rows : (z + 1) * rows, at : at + lane
                ]

    @pl.when(step < 2 * half)
    def _():
        mine = step < half
        x = jnp.where(mine, x_refs[0][...], x_refs[1][...])
        c = jnp.where(mine, c_refs[0][...], c_refs[1][...])
        gate = dot(x, gate_s[...])
        upward = dot(x, up_s[...])
        grad_hidden = dot(c, down_s[...])
        sigmoid = 1.0 / (1.0 + jnp.exp(-gate))
        silu = gate * sigmoid
        hidden = (silu * upward).astype(low_type)
        grad_gate = (grad_hidden * upward * sigmoid * (1.0 + gate * (1.0 - sigmoid))).astype(low_type)
        grad_up = (grad_hidden * silu).astype(low_type)
        at = pl.ds(pl.multiple_of(step * size, size), size)
        hidden_s[at, :] = hidden
        dgate_s[at, :] = grad_gate
        dup_s[at, :] = grad_up
        result = dot(hidden, down_s[...], (1, 1))
        grad = dot(grad_gate, gate_s[...], (1, 1)) + dot(grad_up, up_s[...], (1, 1))
        if held:
            result = result + sums[0][...]
            grad = grad + sums[1][...]
        result_ref[...] = result
        grad_ref[...] = grad

    @pl.when(step >= 2 * half)
    def _():
        q = step - 2 * half
        cut = half * size
        at = pl.ds(pl.multiple_of(q * rows, rows), rows)
        gate = dot(xt_refs[0][...], dgate_s[:cut]) + dot(xt_refs[1][...], dgate_s[cut:])
        up = dot(xt_refs[0][...], dup_s[:cut]) + dot(xt_refs[1][...], dup_s[cut:])
        down = dot(ct_refs[0][...], hidden_s[:cut]) + dot(ct_refs[1][...], hidden_s[cut:])
        gate, up, down = gate.astype(low_type), up.astype(low_type), down.astype(low_type)
        packed_s[0, at, :] = gate[:, :part]
        packed_s[1, at, : block - part] = gate[:, part:]
        packed_s[1, at, block - part :] = up[:, : 2 * part - block]
        packed_s[2, at, : 2 * block - 2 * part] = up[:, 2 * part - block :]
        column = 2 * block + q * lane
        b = lax.div(column, part)
        there = pl.ds(pl.multiple_of(lax.rem(column, part), lane), lane)
        for z in range(BLOCKS):
            packed_s[b, z * rows : (z + 1) * rows, there] = down[:, z * lane : (z + 1) * lane]

    @pl.when(step == pl.num_programs(0) - 1)
    def _():
        send_out(info, packed_s, outs, sems)


def ffn_chunk(info, xs, cs, xts, cts, weights, sums, tuned):
    rows, width = xs[0].shape
    size = rows // 2
    part = weights.shape[2]
    block = BLOCKS * part // 3
    turned = width // BLOCKS

    def first(i):
        return (jnp.minimum(i, 1), 0)

    def second(i):
        return (jnp.clip(i - 2, 0, 1), 0)

    def either(i):
        return (jnp.minimum(i, 3), 0)

    def later(i):
        return (jnp.maximum(i - 4, 0), 0)

    token = [pl.BlockSpec((size, width), first), pl.BlockSpec((size, width), second)]
    across = [pl.BlockSpec((turned, rows), later)] * 2
    total = [pl.BlockSpec((size, width), either)] * 2
    held = len(sums) > 0
    sent = sent_shapes(width, part, tuned)

    def kernel(info, *refs):
        ffn_kernel(held, info, *refs)

    return pl.pallas_call(
        kernel,
        grid=(8,),
        in_specs=[SCALARS] + token + token + across + across
        + [pl.BlockSpec(weights.shape, lambda i: (0, 0, 0))] + (total if held else []),
        out_specs=total + [ANY] * len(sent),
        out_shape=[shape((2 * rows, width), jnp.float32)] * 2 + sent,
        scratch_shapes=[
            pltpu.VMEM((width, block), low_type),
            pltpu.VMEM((width, block), low_type),
            pltpu.VMEM((width, block), low_type),
            pltpu.VMEM((2 * rows, block), low_type),
            pltpu.VMEM((2 * rows, block), low_type),
            pltpu.VMEM((2 * rows, block), low_type),
            pltpu.VMEM((BLOCKS, width, part), low_type),
            pltpu.VMEM((8, 128), jnp.float32),
            pltpu.SemaphoreType.DMA((8,)),
        ],
        compiler_params=params(),
        cost_estimate=cost(18 * 2 * rows * width * block, 40 << 20, 2 * rows * block),
    )(info, *xs, *cs, *xts, *cts, weights, *sums)


def branch_kernel(g_ref, g_other_ref, w_ref, attended_ref, grad_ref, delta_ref, rows_ref):
    rows = g_ref.shape[0]
    delta_ref[...] = jnp.zeros(delta_ref.shape, jnp.float32)
    for i, ref in enumerate((g_ref, g_other_ref)):
        at = slice(i * rows, (i + 1) * rows)
        grad = dot(w_ref[...], ref[...], (1, 1)).astype(low_type)
        grad_ref[:, at] = grad
        product = grad.astype(jnp.float32) * attended_ref[:, at]
        for h in range(GROUP * GROUPS):
            delta_ref[h // GROUP, h % GROUP : h % GROUP + 1, at] = jnp.sum(
                product[h * HEAD_WIDTH : (h + 1) * HEAD_WIDTH], axis=0, keepdims=True
            )
    attended = attended_ref[...].astype(low_type)
    rows_ref[...] = (
        dot(attended[:, :rows], g_ref[...]) + dot(attended[:, rows:], g_other_ref[...])
    ).astype(low_type)


def branch(grad, grad_other, out_rows, attended):
    rows, width = grad.shape
    return pl.pallas_call(
        branch_kernel,
        in_specs=[pl.BlockSpec()] * 4,
        out_specs=[pl.BlockSpec()] * 3,
        out_shape=[
            shape(attended.shape), shape((GROUPS, 8, 2 * rows), jnp.float32),
            shape((HALF_QUERY, width)),
        ],
        compiler_params=params(),
        cost_estimate=cost(8 * rows * width * HALF_QUERY, 12 << 20),
    )(grad, grad_other, out_rows, attended)


def attn_grad_kernel(
    info, dq_ref, dkv_ref, came_ref, cos_ref, sin_ref, normed_ref, mine_ref, other_ref, d_ref, *refs
):
    outs, packed_s, sems = refs[:-2], refs[-2], refs[-1]
    hq, hk = HALF_QUERY, HALF_KEY
    part = packed_s.shape[2]
    cosine, sine = cos_ref[...], -sin_ref[...]
    turn_heads(d_ref, dq_ref[...], cosine, sine, 0)
    whole = dkv_ref[...] + came_ref[...].astype(jnp.float32)
    turn_heads(d_ref, whole[0], cosine, sine, hq)
    d_ref[hq + hk :, :] = whole[1].astype(low_type)
    normed = normed_ref[...]
    packed_s[0] = dot(normed, d_ref[:part, :], (1, 1)).astype(low_type)
    packed_s[1] = dot(normed, d_ref[part : 2 * part, :], (1, 1)).astype(low_type)
    last = dot(normed, d_ref[2 * part :, :], (1, 1)).astype(low_type)
    mine, other = mine_ref[...], other_ref[...]
    low = info[0] == 0
    out = jnp.concatenate(
        [jnp.where(low, mine, other), jnp.where(low, other, mine)], axis=0
    )
    packed_s[2] = jnp.concatenate([last, out[:, : part - hk]], axis=1)
    packed_s[3] = out[:, part - hk :]
    send_out(info, packed_s, outs, sems)


def attn_grads(info, grad_query, grad_kv, came, cosine, sine, normed, mine, other, tuned):
    width, both = normed.shape
    part = (2 * HALF_QUERY + 2 * HALF_KEY) // BLOCKS
    sent = sent_shapes(width, part, tuned)
    return pl.pallas_call(
        attn_grad_kernel,
        in_specs=[SCALARS] + [pl.BlockSpec()] * 8,
        out_specs=[pl.BlockSpec()] + [ANY] * len(sent),
        out_shape=[shape((HALF_QUERY + 2 * HALF_KEY, both))] + sent,
        scratch_shapes=[
            pltpu.VMEM((BLOCKS, width, part), low_type),
            pltpu.SemaphoreType.DMA((8,)),
        ],
        compiler_params=params(),
        cost_estimate=cost(2 * both * width * 960, 20 << 20),
    )(info, grad_query, grad_kv, came, cosine, sine, normed, mine, other)


def normed_grad_kernel(d_ref, w_ref, mine_ref, other_ref):
    rows = mine_ref.shape[0]
    hk, part = HALF_KEY, w_ref.shape[2]
    for i, ref in enumerate((other_ref, mine_ref)):
        at = slice((1 - i) * rows, (2 - i) * rows)
        d = d_ref[:, at].T
        value = dot(d[:, :part], w_ref[0], (1, 1)) + dot(d[:, part : 2 * part], w_ref[1], (1, 1))
        value = value + dot(d[:, 2 * part :], w_ref[2][:, :hk], (1, 1))
        ref[...] = value.astype(ref.dtype)


def normed_grad(d, weights):
    width = weights.shape[1]
    rows = d.shape[1] // 2
    return pl.pallas_call(
        normed_grad_kernel,
        in_specs=[pl.BlockSpec()] * 2,
        out_specs=[pl.BlockSpec()] * 2,
        out_shape=[shape((rows, width), jnp.float32), shape((rows, width))],
        compiler_params=params(),
        cost_estimate=cost(4 * rows * width * 960, 9 << 20),
    )(d, weights)


def unpack_attn_kernel(all_ref, q_ref, k_ref, v_ref, o_ref):
    hq, hk = HALF_QUERY, HALF_KEY
    both = [
        jnp.concatenate([all_ref[h, b, 0] for b in range(BLOCKS)], axis=1).astype(jnp.float32)
        for h in range(2)
    ]
    start = 0
    for ref, size in ((q_ref, hq), (k_ref, hk), (v_ref, hk), (o_ref, hq)):
        ref[...] = jnp.concatenate([v[:, start : start + size] for v in both], axis=1)
        start += size


def unpack_attn(everyone):
    rows = everyone.shape[3]
    return pl.pallas_call(
        unpack_attn_kernel,
        in_specs=[pl.BlockSpec()],
        out_specs=[pl.BlockSpec()] * 4,
        out_shape=[
            shape((rows, 2 * n), jnp.float32) for n in (HALF_QUERY, HALF_KEY, HALF_KEY, HALF_QUERY)
        ],
        compiler_params=params(),
        cost_estimate=cost(0, 6 << 20),
    )(everyone)


def unpack_ffn_kernel(all_ref, gate_ref, up_ref, down_ref):
    rows, part = all_ref.shape[3], all_ref.shape[4]
    block = BLOCKS * part // 3
    lane = block // BLOCKS
    half = CHUNKS * lane
    for h in range(2):
        for c in range(CHUNKS):
            value = jnp.concatenate([all_ref[h, b, c] for b in range(BLOCKS)], axis=1)
            value = value.astype(jnp.float32)
            for z in range(BLOCKS):
                at = z * 2 * half + h * half + c * lane
                gate_ref[:, at : at + lane] = value[:, z * lane : (z + 1) * lane]
                up_ref[:, at : at + lane] = value[:, block + z * lane : block + (z + 1) * lane]
            down = jnp.concatenate(
                [value[:, 2 * block + q * lane : 2 * block + (q + 1) * lane] for q in range(BLOCKS)],
                axis=0,
            )
            down_ref[h * half + c * lane : h * half + (c + 1) * lane, :] = down.T


def unpack_ffn(everyone):
    rows, part = everyone.shape[3:]
    lane = part // 3
    return pl.pallas_call(
        unpack_ffn_kernel,
        in_specs=[pl.BlockSpec()],
        out_specs=[pl.BlockSpec()] * 3,
        out_shape=[
            shape((rows, 2 * BLOCKS * CHUNKS * lane), jnp.float32),
            shape((rows, 2 * BLOCKS * CHUNKS * lane), jnp.float32),
            shape((2 * CHUNKS * lane, BLOCKS * rows), jnp.float32),
        ],
        compiler_params=params(),
        cost_estimate=cost(0, 16 << 20),
    )(everyone)


def shards(sizes, *arrays):
    (
        tokens, segments, cotangent, attn_gain, w_query, key_matrix, value_matrix, w_out, ffn_gain,
        w_gate, w_up, w_down,
    ) = arrays
    ny, nx, nz = sizes
    tuned = (ny, nx) == (2, 2)
    core, xi = lax.axis_index("core"), lax.axis_index("x")
    place = lax.axis_index("y") * nx + xi
    info = jnp.stack([core, place, lax.axis_index("z"), xi]).astype(jnp.int32)
    tokens, cotangent, ids = tokens[0], cotangent[0], segments[0]
    rows, width = tokens.shape
    own_rows = w_query.shape[0]

    attn_own, *attn_piece = pack_attn(info, (w_query, key_matrix, value_matrix, w_out), tuned)
    ffn_own, *ffn_piece = pack_ffn(info, w_gate, w_up, w_down, tuned)
    weights = gather_weights(info, attn_own, attn_piece[0] if tuned else None, sizes, 0)
    ffn_weights = [
        gather_weights(info, ffn_own[c], ffn_piece[c] if tuned else None, sizes, c + 1)
        for c in range(CHUNKS)
    ]
    weights_other = swap_core(weights[2:])

    all_ids = lax.all_gather(ids, "x", axis=0, tiled=True)
    first = jnp.sum((all_ids[:, None] < ids[None, :]).astype(jnp.int32), axis=0)
    firsts = jnp.concatenate([first[None], swap_core(first[None])])
    token_place = xi * rows + jnp.arange(rows, dtype=jnp.int32)
    positions = (token_place[None] - firsts).reshape(-1)
    angles = inverse_freq()[:, None] * positions.astype(jnp.float32)[None, :]
    cosine, sine = jnp.cos(angles), jnp.sin(angles)
    size = rows // 2
    starts = firsts.reshape(2, rows // size, size)[:, :, 0] // size
    info = jnp.concatenate([info, starts.reshape(-1)])
    firsts = firsts[:, None, :]

    gains = lax.all_gather(jnp.stack([attn_gain, ffn_gain]).astype(low_type), "z", axis=1, tiled=True)
    gain_one, gain_two = gains[:1].astype(jnp.float32), gains[1:].astype(jnp.float32)

    turned = cotangent.T
    cs, cts = (cotangent, swap_core(cotangent)), (turned, swap_core(turned))

    normed, query, keyvalue = project(
        tokens, swap_core(tokens), gain_one, weights, cosine, sine
    )
    if nx == 2:
        past = lax.ppermute(keyvalue, "x", [(0, 1)])[None]
    else:
        past = lax.all_gather(keyvalue, "x", axis=0)
    attended, log_total = attend(info, query, keyvalue, past, firsts, size)
    came = swap_core(attended[:, rows:].astype(low_type))
    middle, normed_two, normed_turned, out_rows = project_out(
        info, attended, came, weights, weights_other, tokens, gain_two
    )

    xs, xts = (normed_two, swap_core(normed_two)), (normed_turned, swap_core(normed_turned))
    sums, ffn_sent = (), []
    for c in range(CHUNKS):
        *sums, = ffn_chunk(info, xs, cs, xts, cts, ffn_weights[c], sums, tuned)
        sums, sent = sums[:2], sums[2:]
        ffn_sent.append(sent)
    result, grad_normed_two = sums

    def pair_sum(value):
        return value[:rows] + swap_core(value[rows:].astype(low_type)).astype(jnp.float32)

    grad_normed_two = pair_sum(grad_normed_two)
    scale_two = norm_scale(middle)
    grad_gain_two = jnp.sum(grad_normed_two * middle * scale_two, axis=0)
    grad_middle = cotangent.astype(jnp.float32) + norm_back(
        grad_normed_two * gain_two, middle, scale_two
    )
    grad_branch = grad_middle.astype(low_type)
    output = (middle + pair_sum(result)).astype(low_type)

    grad_other = swap_core(grad_branch)
    grad_attended, delta, grad_rows = branch(grad_branch, grad_other, out_rows, attended)
    hq = HALF_QUERY
    mine = lax.dynamic_slice_in_dim(grad_rows, core * hq, hq, 1)
    other = swap_core(lax.dynamic_slice_in_dim(grad_rows, (1 - core) * hq, hq, 1))
    grad_query, grad_kv, grad_past = attend_back(
        info, query, keyvalue, past, grad_attended, firsts, log_total, delta, size
    )
    if nx == 2:
        came = lax.ppermute(grad_past[0], "x", [(1, 0)])
    else:
        came = lax.psum_scatter(grad_past, "x", scatter_dimension=0, tiled=True)[0]
    grad_projected, *attn_sent = attn_grads(
        info, grad_query, grad_kv, came, cosine, sine, normed, mine, other, tuned
    )
    normed_mine, normed_other = normed_grad(grad_projected, weights)
    grad_normed = normed_mine + swap_core(normed_other).astype(jnp.float32)
    inputs = tokens.astype(jnp.float32)
    scale_one = norm_scale(inputs)
    grad_gain_one = jnp.sum(grad_normed * inputs * scale_one, axis=0)
    grad_inputs = (
        grad_middle + norm_back(grad_normed * gain_one, inputs, scale_one)
    ).astype(low_type)

    gain_grads = jnp.stack([grad_gain_one, grad_gain_two])
    for axis, count in (("core", 2), ("x", nx), ("y", ny), ("z", nz)):
        gain_grads = sum_over(gain_grads, axis, count)
    gain_grads = lax.dynamic_slice_in_dim(gain_grads, lax.axis_index("z") * own_rows, own_rows, 1)

    ffn_sums = jnp.stack([scatter_gradients(sent, sizes) for sent in ffn_sent])
    attn_sum = scatter_gradients(attn_sent, sizes)
    grad_w_gate, grad_w_up, grad_w_down = unpack_ffn(spread(ffn_sums, sizes))
    attn_out = unpack_attn(spread(attn_sum[None], sizes))
    return (
        output[None], grad_inputs[None], gain_grads[0], *attn_out, gain_grads[1], grad_w_gate,
        grad_w_up, grad_w_down,
    )


def solution(mesh):
    dp, ctx, fsdp = (mesh.shape[name] for name in ("dp", "ctx", "fsdp"))
    fine = Mesh(mesh.devices.reshape(dp // 2, 2, ctx, fsdp), ("y", "core", "x", "z"))
    sizes = (dp // 2, ctx, fsdp)
    wide = P(("y", "core", "z"), "x", None)
    matrix, vector = P("z", None), P("z")
    in_specs = (
        wide, P(("y", "core", "z"), "x"), wide, vector, matrix, matrix, matrix, matrix, vector,
        matrix, matrix, matrix,
    )
    out_specs = (
        wide, wide, vector, matrix, matrix, matrix, matrix, vector, matrix, matrix, matrix
    )

    def layer(*arrays):
        return shards(sizes, *arrays)

    return jax.shard_map(
        layer, mesh=fine, in_specs=in_specs, out_specs=out_specs, check_vma=False
    )
```

time: 1380 us -> 653 us (0.47)
  waiting for transfers between devices: 969 us -> 261 us
  Pallas kernels: 0 us -> 182 us
  matrix products: 169 us -> 0 us
  starting transfers between devices: 1.2 us -> 119 us
  blocking collectives: 117 us -> 22.4 us
  other arithmetic: 63.5 us -> 31.8 us
    reduce_scatter x9 -> x4, waiting for transfers between devices: 568 us -> 35.6 us  [scatter_gradients(): return lax.psum_scatter(mine, 'z', scatter_dimension=0, tiled=True)]
    all_gather x5 -> x2, waiting for transfers between devices: 334 us -> 31.6 us  [spread(): everyone = lax.all_gather(mine, ('core', 'y', 'x'), axis=0)]
    ppermute x0 -> x84, waiting for transfers between devices: none -> 193 us  [the longest x4 64.2 us: scatter_gradients(): came_one = lax.ppermute(send_one, 'x', PAIR)]
    pallas_call x0 -> x18, Pallas kernels: none -> 182 us  [the longest x3 66.7 us: ffn_chunk(): pl.pallas_call(kernel, grid=(8,), in_specs=[SCALARS] + token + token + ac...]
    dot_general x28 -> x0, matrix products: 169 us -> none  [the longest x7 40.3 us: outer_sum(): lax.dot_general(left, right, (((0,), (0,)), ((), ())), preferred_element_...]
    ppermute x0 -> x84, starting transfers between devices: none -> 119 us  [the longest x12 37.8 us: gather_weights(): slots = [lax.ppermute(piece, 'z', ring(nz, k)) for k in range(1, nz)]]
    psum x1 -> x0, waiting for transfers between devices: 65.9 us -> none  [shards(): lax.psum(attn_shards[1].astype(jnp.bfloat16), ('dp', 'ctx'))]
    all_gather x5 -> x2, blocking collectives: 77.3 us -> 22.4 us  [the longest x1 18.1 us: shards(): lax.all_gather(jnp.stack([attn_gain, ffn_gain]).astype(low_type), 'z', ax...]
  transfers between devices with their start and end apart: 15 -> 90, of which waited for: 12 -> 40; matrix products, arithmetic and copies ran while one was open for 12% -> 6% of each run, Pallas kernels for 0% -> 11%
where the time goes in v1:
time: 653 us; the launch traced here: 652 us
  waiting for transfers between devices  261 us (40%)
  Pallas kernels  182 us (28%)
  starting transfers between devices  119 us (18%)
  other arithmetic  31.8 us (5%)
  blocking collectives  22.4 us (3%)
  local copies, waits for them, and re-layouts  19.4 us (3%)
  between operations  15.5 us (2%)
    pallas_call x3, Pallas kernels, ffn_chunk(): pl.pallas_call(kernel, grid=(8,), in_specs=[SCALARS] + token + token + ac...  66.7 us
    ppermute x4, waiting for transfers between devices, scatter_gradients(): came_one = lax.ppermute(send_one, 'x', PAIR)  64.2 us
    ppermute x12, starting transfers between devices, gather_weights(): slots = [lax.ppermute(piece, 'z', ring(nz, k)) for k in range(1, nz)]  37.8 us
    reduce_scatter x4, waiting for transfers between devices, scatter_gradients(): return lax.psum_scatter(mine, 'z', scatter_dimension=0, tiled=True)  35.6 us
    all_gather x2, waiting for transfers between devices, spread(): everyone = lax.all_gather(mine, ('core', 'y', 'x'), axis=0)  31.6 us
    ppermute x4, waiting for transfers between devices, scatter_gradients(): one = lax.ppermute(add_low(keep_one[1], came_one[1]), 'y', PAIR)  31.2 us
    ppermute x12, waiting for transfers between devices, gather_weights(): by_x = [lax.ppermute(s, 'x', PAIR) for s in slots]  27.9 us
    ppermute x1, waiting for transfers between devices, shards(): came = lax.ppermute(grad_past[0], 'x', [(1, 0)])  26.1 us
  transfers between devices with their start and end apart: 90, of which 40 were waited for; matrix products, arithmetic and copies ran while one was open for 6% of the time, Pallas kernels for 11%

profile of v1, /device:TPU:0, one launch (start us, length us, event | category | flops | bytes accessed | tf_op | source)
XLA Modules:
  0.0 651.6 jit_solution(14397548885999594349)
XLA Ops:
  23.6 18.1 %all-gather.3 = bf16[4,288,2]{1,2,0:T(2,128)(2,1)S(1)} all-gather(bf16[1,288,2]{1,2,0:T(2,128)(2,1)S(1)} %maximum_bitcast_fusion), channel_id=1, replica_groups=mesh['y'=2,'core'=2,'x'=2,'z'=4] {'z'}, dimensions={0}, use_global_device_ids=true | all-gather | bytes 5760 | tf_op jit(solution)/shard_map/all_gather | solution.py:876
  54.2 10.6 %collective-permute-done.6.refs_6_ = bf16[288,384]{1,0:T(8,128)(2,1)S(1)} collective-permute-done((bf16[288,384]{1,0:T(8,128)(2,1)S(1)}, bf16[288,384]{1,0:T(8,128)(2,1)S(1)}, u32[]{:S(2)}, u32[]{:S(2)}) %collective-permute-start.6) | collective-permute-done | bytes 221216 | tf_op jit(solution)/shard_map/ppermute | solution.py:198
  81.8 9.3 %collective-permute-start.34 = (bf16[288,384]{1,0:T(8,128)(2,1)}, bf16[288,384]{1,0:T(8,128)(2,1)S(1)}, u32[]{:S(2)}, u32[]{:S(2)}) collective-permute-start(bf16[288,384]{1,0:T(8,128)(2,1)} %get-tuple-element.74), channel_id=1, source_target_pairs={{0,2},{1,3},{2,0},{3,1},{4,6},{5,7},{6,4},{7,5},{8,10},{9,11},{10,... | collective-permute-start | bytes 663560 | tf_op jit(solution)/shard_map/ppermute | solution.py:197
  91.5 7.8 %collective-permute-start.35 = (bf16[288,384]{1,0:T(8,128)(2,1)}, bf16[288,384]{1,0:T(8,128)(2,1)S(1)}, u32[]{:S(2)}, u32[]{:S(2)}) collective-permute-start(bf16[288,384]{1,0:T(8,128)(2,1)} %get-tuple-element.74), channel_id=1, source_target_pairs={{0,3},{1,0},{2,1},{3,2},{4,7},{5,4},{6,5},{7,6},{8,11},{9,8},{10,9... | collective-permute-start | bytes 663560 | tf_op jit(solution)/shard_map/ppermute | solution.py:197
  126.2 9.5 %collective-permute-done.48.refs_5_ = bf16[288,384]{1,0:T(8,128)(2,1)S(1)} collective-permute-done((bf16[288,384]{1,0:T(8,128)(2,1)S(1)}, bf16[288,384]{1,0:T(8,128)(2,1)S(1)}, u32[]{:S(2)}, u32[]{:S(2)}) %collective-permute-start.48) | collective-permute-done | bytes 221216 | tf_op jit(solution)/shard_map/ppermute | solution.py:198
  156.1 15.7 %shard_map.206 = (f32[576,1024]{1,0:T(8,128)}, f32[3,8,1024]{2,1,0:T(8,128)}) custom-call(s32[8]{0:T(128)} %concatenate.29.info, bf16[576,1024]{1,0:T(8,128)(2,1)} %get-tuple-element.66.q_ref, bf16[2,192,1024]{2,1,0:T(8,128)(2,1)} %get-tuple-element.67.kv_ref, bf16[1,2,192,1024]{3,2,1,0:T(8,128)(2,1)} %bitcast.11.past_ref, ...), custom_call_target="tpu_custom_call" | custom-call | flops 9059696640 | bytes 8388608 | tf_op jit(solution)/shard_map/pallas_call | solution.py:448
  173.6 8.3 %collective-permute-start.26 = (bf16[288,384]{1,0:T(8,128)(2,1)S(1)}, bf16[288,384]{1,0:T(8,128)(2,1)S(1)}, u32[]{:S(2)}, u32[]{:S(2)}) collective-permute-start(bf16[288,384]{1,0:T(8,128)(2,1)S(1)} %copy-done.33), channel_id=1, source_target_pairs={{0,4},{4,0},{1,5},{5,1},{2,6},{6,2},{3,7},{7,3},{8,12},{12,8},{9,1... | collective-permute-start | bytes 663560 | tf_op jit(solution)/shard_map/ppermute | solution.py:198
  208.8 9.5 %shard_map.207 = (f32[512,1152]{1,0:T(8,128)}, bf16[512,1152]{1,0:T(8,128)(2,1)}, bf16[1152,512]{1,0:T(8,128)(2,1)}, bf16[576,1152]{1,0:T(8,128)(2,1)}) custom-call(s32[8]{0:T(128)} %concatenate.29.info, f32[576,1024]{1,0:T(8,128)} %get-tuple-element.68.mine_ref.attended_ref, bf16[576,512]{1,0:T(8,128)(2,1)} %copy-done.24, ...), custom_call_target="tpu_custom_call" | custom-call | flops 1358954496 | bytes 16777216 | tf_op jit(solution)/shard_map/pallas_call | solution.py:521
  254.5 21.2 %shard_map.212 = (f32[1024,1152]{1,0:T(8,128)}, f32[1024,1152]{1,0:T(8,128)}, bf16[2,576,384]{2,1,0:T(8,128)(2,1)}, bf16[2,576,384]{2,1,0:T(8,128)(2,1)}, bf16[2...) custom-call(s32[8]{0:T(128)} %concatenate.29.info, bf16[512,1152]{1,0:T(8,128)(2,1)} %get-tuple-element.70.refs_0_, ...), custom_call_target="tpu_custom_call" | custom-call | flops 10871635968 | bytes 41943040 | tf_op jit(solution)/shard_map/pallas_call | solution.py:655
  275.7 22.8 %shard_map.213 = (f32[1024,1152]{1,0:T(8,128)}, f32[1024,1152]{1,0:T(8,128)}, bf16[2,576,384]{2,1,0:T(8,128)(2,1)}, bf16[2,576,384]{2,1,0:T(8,128)(2,1)}, bf16[2...) custom-call(s32[8]{0:T(128)} %concatenate.29.info, bf16[512,1152]{1,0:T(8,128)(2,1)} %get-tuple-element.70.refs_0_, ...), custom_call_target="tpu_custom_call" | custom-call | flops 10871635968 | bytes 41943040 | tf_op jit(solution)/shard_map/pallas_call | solution.py:655
  298.5 22.7 %shard_map.214 = (f32[1024,1152]{1,0:T(8,128)}, f32[1024,1152]{1,0:T(8,128)}, bf16[2,576,384]{2,1,0:T(8,128)(2,1)}, bf16[2,576,384]{2,1,0:T(8,128)(2,1)}, bf16[2...) custom-call(s32[8]{0:T(128)} %concatenate.29.info, bf16[512,1152]{1,0:T(8,128)(2,1)} %get-tuple-element.70.refs_0_, ...), custom_call_target="tpu_custom_call" | custom-call | flops 10871635968 | bytes 41943040 | tf_op jit(solution)/shard_map/pallas_call | solution.py:655
  342.7 18.5 %shard_map.216 = (f32[576,1024]{1,0:T(8,128)}, f32[2,192,1024]{2,1,0:T(8,128)}, bf16[1,2,192,1024]{3,2,1,0:T(8,128)(2,1)}) custom-call(s32[8]{0:T(128)} %concatenate.29.info, bf16[576,1024]{1,0:T(8,128)(2,1)} %get-tuple-element.66.q_ref, bf16[2,192,1024]{2,1,0:T(8,128)(2,1)} %get-tuple-element.67.kv_ref, bf16[1,2,192,1024]{3,2,1,0:T(8,128)(2,1)} %bitcast.11.past_ref, ...), custom_call_target="tpu_custom_call" | custom-call | flops 13589544960 | bytes 12582912 | tf_op jit(solution)/shard_map/pallas_call | solution.py:469
  366.2 26.1 %collective-permute-done.60.came_ref = bf16[2,192,1024]{2,1,0:T(8,128)(2,1)S(1)} collective-permute-done((bf16[2,192,1024]{2,1,0:T(8,128)(2,1)}, bf16[2,192,1024]{2,1,0:T(8,128)(2,1)S(1)}, u32[]{:S(2)}, u32[]{:S(2)}) %collective-permute-start.60) | collective-permute-done | bytes 786464 | tf_op jit(solution)/shard_map/ppermute | solution.py:924
  393.3 10.1 %shard_map.217 = (bf16[960,1024]{1,0:T(8,128)(2,1)}, bf16[2,576,384]{2,1,0:T(8,128)(2,1)}, bf16[2,576,384]{2,1,0:T(8,128)(2,1)}, bf16[2,576,384]{2,1,0:T(8,128)(2,1)}, bf16[2,576,384]{2,1,0:T(8,128)(2,1)}) custom-call(s32[8]{0:T(128)} %concatenate.29.info, f32[576,1024]{1,0:T(8,128)} %get-tuple-element.86.dq_ref, f32[2,192,1024]{2,1,0:T(8,128)} %get-tuple-element.87.dkv_ref, ...), custom_call_target="tpu_custom_call" | custom-call | flops 2264924160 | bytes 20971520 | tf_op jit(solution)/shard_map/pallas_call | solution.py:740
  403.5 21.5 %collective-permute-done.68 = bf16[2,576,384]{2,1,0:T(8,128)(2,1)S(1)} collective-permute-done((bf16[2,576,384]{2,1,0:T(8,128)(2,1)}, bf16[2,576,384]{2,1,0:T(8,128)(2,1)S(1)}, u32[]{:S(2)}, u32[]{:S(2)}) %collective-permute-start.68) | collective-permute-done | bytes 884768 | tf_op jit(solution)/shard_map/ppermute | solution.py:259
  431.4 7.9 %collective-permute-done.69 = bf16[576,384]{1,0:T(8,128)(2,1)S(1)} collective-permute-done((bf16[576,384]{1,0:T(8,128)(2,1)S(1)}, bf16[576,384]{1,0:T(8,128)(2,1)S(1)}, u32[]{:S(2)}, u32[]{:S(2)}) %collective-permute-start.69) | collective-permute-done | bytes 442400 | tf_op jit(solution)/shard_map/ppermute | solution.py:261
  441.8 15.6 %collective-permute-done.72 = bf16[2,576,384]{2,1,0:T(8,128)(2,1)S(1)} collective-permute-done((bf16[2,576,384]{2,1,0:T(8,128)(2,1)}, bf16[2,576,384]{2,1,0:T(8,128)(2,1)S(1)}, u32[]{:S(2)}, u32[]{:S(2)}) %collective-permute-start.72) | collective-permute-done | bytes 884768 | tf_op jit(solution)/shard_map/ppermute | solution.py:259
  461.8 8.9 %collective-permute-done.73 = bf16[576,384]{1,0:T(8,128)(2,1)S(1)} collective-permute-done((bf16[576,384]{1,0:T(8,128)(2,1)S(1)}, bf16[576,384]{1,0:T(8,128)(2,1)S(1)}, u32[]{:S(2)}, u32[]{:S(2)}) %collective-permute-start.73) | collective-permute-done | bytes 442400 | tf_op jit(solution)/shard_map/ppermute | solution.py:261
  473.8 14.2 %collective-permute-done.76 = bf16[2,576,384]{2,1,0:T(8,128)(2,1)} collective-permute-done((bf16[2,576,384]{2,1,0:T(8,128)(2,1)}, bf16[2,576,384]{2,1,0:T(8,128)(2,1)}, u32[]{:S(2)}, u32[]{:S(2)}) %collective-permute-start.76) | collective-permute-done | bytes 884768 | tf_op jit(solution)/shard_map/ppermute | solution.py:259
  493.5 8.9 %collective-permute-done.77 = bf16[576,384]{1,0:T(8,128)(2,1)S(1)} collective-permute-done((bf16[576,384]{1,0:T(8,128)(2,1)S(1)}, bf16[576,384]{1,0:T(8,128)(2,1)S(1)}, u32[]{:S(2)}, u32[]{:S(2)}) %collective-permute-start.77) | collective-permute-done | bytes 442400 | tf_op jit(solution)/shard_map/ppermute | solution.py:261
  504.8 12.9 %collective-permute-done.80 = bf16[2,576,384]{2,1,0:T(8,128)(2,1)} collective-permute-done((bf16[2,576,384]{2,1,0:T(8,128)(2,1)}, bf16[2,576,384]{2,1,0:T(8,128)(2,1)}, u32[]{:S(2)}, u32[]{:S(2)}) %collective-permute-start.80) | collective-permute-done | bytes 884768 | tf_op jit(solution)/shard_map/ppermute | solution.py:259
  530.6 9.2 %reduce-scatter.9.cloned.1.call-done = bf16[288,384]{1,0:T(8,128)(2,1)} async-done(((bf16[1152,384]{1,0:T(8,128)(2,1)}), bf16[288,384]{1,0:T(8,128)(2,1)}) %reduce-scatter.9.cloned.1.call-update) | async-done | bytes 221200 | tf_op jit(solution)/shard_map/reduce_scatter | solution.py:266
  539.8 26.4 %reduce-scatter.11.cloned.1.call-done = bf16[288,384]{1,0:T(8,128)(2,1)} async-done(((bf16[1152,384]{1,0:T(8,128)(2,1)}), bf16[288,384]{1,0:T(8,128)(2,1)}) %reduce-scatter.11.cloned.1.call-update) | async-done | bytes 221200 | tf_op jit(solution)/shard_map/reduce_scatter | solution.py:266
  605.4 31.6 %all-gather.9.cloned.1.call-done = bf16[24,288,384]{2,1,0:T(8,128)(2,1)} async-done(((bf16[3,288,384]{2,1,0:T(8,128)(2,1)}), bf16[24,288,384]{2,1,0:T(8,128)(2,1)}) %all-gather.9.cloned.1.call-update) | async-done | bytes 5308432 | tf_op jit(solution)/shard_map/all_gather | solution.py:270
  (391 shorter events, 268.9 us)
Async XLA Ops:
  7.2 522.6 %reduce-scatter.5.cloned.1.call-start = ((), (), s32[]{:S(2)}) async-start(), calls=%async_computation.4 | async-start | bytes 1105920 | tf_op jit(solution)/shard_map/reduce_scatter | solution.py:266
  11.4 30.4 %collective-permute-start.2 = (bf16[288,384]{1,0:T(8,128)(2,1)}, bf16[288,384]{1,0:T(8,128)(2,1)S(1)}, u32[]{:S(2)}, u32[]{:S(2)}) collective-permute-start(bf16[288,384]{1,0:T(8,128)(2,1)} %get-tuple-element.65), channel_id=1, source_target_pairs={{0,1},{1,2},{2,3},{3,0},{4,5},{5,6},{6,7},{7,4},{8,9},{9,10},{10,1... | collective-permute-start | bytes 663560 | tf_op jit(solution)/shard_map/ppermute | solution.py:197
  14.4 37.8 %collective-permute-start.3 = (bf16[288,384]{1,0:T(8,128)(2,1)}, bf16[288,384]{1,0:T(8,128)(2,1)S(1)}, u32[]{:S(2)}, u32[]{:S(2)}) collective-permute-start(bf16[288,384]{1,0:T(8,128)(2,1)} %get-tuple-element.65), channel_id=1, source_target_pairs={{0,2},{1,3},{2,0},{3,1},{4,6},{5,7},{6,4},{7,5},{8,10},{9,11},{10,... | collective-permute-start | bytes 663560 | tf_op jit(solution)/shard_map/ppermute | solution.py:197
  17.0 34.7 %collective-permute-start.4 = (bf16[288,384]{1,0:T(8,128)(2,1)}, bf16[288,384]{1,0:T(8,128)(2,1)S(1)}, u32[]{:S(2)}, u32[]{:S(2)}) collective-permute-start(bf16[288,384]{1,0:T(8,128)(2,1)} %get-tuple-element.65), channel_id=1, source_target_pairs={{0,3},{1,0},{2,1},{3,2},{4,7},{5,4},{6,5},{7,6},{8,11},{9,8},{10,9... | collective-permute-start | bytes 663560 | tf_op jit(solution)/shard_map/ppermute | solution.py:197
  23.0 82.6 %collective-permute-start.1 = (bf16[512,1152]{1,0:T(8,128)(2,1)S(1)}, bf16[512,1152]{1,0:T(8,128)(2,1)}, u32[]{:S(2)}, u32[]{:S(2)}) collective-permute-start(bf16[512,1152]{1,0:T(8,128)(2,1)S(1)} %bitcast.102), channel_id=1, source_target_pairs={{0,8},{8,0},{1,9},{9,1},{2,10},{10,2},{3,11},{11,3},{4,12},{12,4},... | collective-permute-start | bytes 3538952 | tf_op jit(solution)/shard_map/ppermute | solution.py:54
  75.6 37.5 %collective-permute-start.33 = (bf16[288,384]{1,0:T(8,128)(2,1)}, bf16[288,384]{1,0:T(8,128)(2,1)S(1)}, u32[]{:S(2)}, u32[]{:S(2)}) collective-permute-start(bf16[288,384]{1,0:T(8,128)(2,1)} %get-tuple-element.74), channel_id=1, source_target_pairs={{0,1},{1,2},{2,3},{3,0},{4,5},{5,6},{6,7},{7,4},{8,9},{9,10},{10,1... | collective-permute-start | bytes 663560 | tf_op jit(solution)/shard_map/ppermute | solution.py:197
  81.8 38.0 %collective-permute-start.34 = (bf16[288,384]{1,0:T(8,128)(2,1)}, bf16[288,384]{1,0:T(8,128)(2,1)S(1)}, u32[]{:S(2)}, u32[]{:S(2)}) collective-permute-start(bf16[288,384]{1,0:T(8,128)(2,1)} %get-tuple-element.74), channel_id=1, source_target_pairs={{0,2},{1,3},{2,0},{3,1},{4,6},{5,7},{6,4},{7,5},{8,10},{9,11},{10,... | collective-permute-start | bytes 663560 | tf_op jit(solution)/shard_map/ppermute | solution.py:197
  91.5 30.6 %collective-permute-start.35 = (bf16[288,384]{1,0:T(8,128)(2,1)}, bf16[288,384]{1,0:T(8,128)(2,1)S(1)}, u32[]{:S(2)}, u32[]{:S(2)}) collective-permute-start(bf16[288,384]{1,0:T(8,128)(2,1)} %get-tuple-element.74), channel_id=1, source_target_pairs={{0,3},{1,0},{2,1},{3,2},{4,7},{5,4},{6,5},{7,6},{8,11},{9,8},{10,9... | collective-permute-start | bytes 663560 | tf_op jit(solution)/shard_map/ppermute | solution.py:197
  113.1 40.6 %collective-permute-start.14 = (bf16[2,192,1024]{2,1,0:T(8,128)(2,1)}, bf16[2,192,1024]{2,1,0:T(8,128)(2,1)}, u32[]{:S(2)}, u32[]{:S(2)}) collective-permute-start(bf16[2,192,1024]{2,1,0:T(8,128)(2,1)} %get-tuple-element.67.kv_ref), channel_id=1, source_target_pairs={{0,4},{1,5},{2,6},{3,7},{8,12},{9,13},{10,14},{11,15},{16,20},{17,... | collective-permute-start | bytes 2359304 | tf_op jit(solution)/shard_map/ppermute | solution.py:886
  138.2 69.5 %collective-permute-start.16 = (bf16[2,1152,384]{2,1,0:T(8,128)(2,1)S(1)}, bf16[2,1152,384]{2,1,0:T(8,128)(2,1)}, u32[]{:S(2)}, u32[]{:S(2)}) collective-permute-start(bf16[2,1152,384]{2,1,0:T(8,128)(2,1)S(1)} %slice.189), channel_id=1, source_target_pairs={{0,8},{8,0},{1,9},{9,1},{2,10},{10,2},{3,11},{11,3},{4,12},{12,4},... | collective-permute-start | bytes 5308424 | tf_op jit(solution)/shard_map/ppermute | solution.py:54
  153.6 28.4 %collective-permute-start.24 = (bf16[288,384]{1,0:T(8,128)(2,1)}, bf16[288,384]{1,0:T(8,128)(2,1)S(1)}, u32[]{:S(2)}, u32[]{:S(2)}) collective-permute-start(bf16[288,384]{1,0:T(8,128)(2,1)} %collective-permute-done.21.refs_2_), channel_id=1, source_target_pairs={{0,4},{4,0},{1,5},{5,1},{2,6},{6,2},{3,7},{7,3},{8,12},{12,8},{9,1... | collective-permute-start | bytes 663560 | tf_op jit(solution)/shard_map/ppermute | solution.py:198
  173.2 34.8 %collective-permute-start.15 = (bf16[576,512]{1,0:T(8,128)(2,1)S(1)}, bf16[576,512]{1,0:T(8,128)(2,1)S(1)}, u32[]{:S(2)}, u32[]{:S(2)}) collective-permute-start(bf16[576,512]{1,0:T(8,128)(2,1)S(1)} %slice.269), channel_id=1, source_target_pairs={{0,8},{8,0},{1,9},{9,1},{2,10},{10,2},{3,11},{11,3},{4,12},{12,4},... | collective-permute-start | bytes 1769480 | tf_op jit(solution)/shard_map/ppermute | solution.py:54
  218.3 36.2 %collective-permute-start.18 = (bf16[512,1152]{1,0:T(8,128)(2,1)S(1)}, bf16[512,1152]{1,0:T(8,128)(2,1)}, u32[]{:S(2)}, u32[]{:S(2)}) collective-permute-start(bf16[512,1152]{1,0:T(8,128)(2,1)S(1)} %bitcast.107), channel_id=1, source_target_pairs={{0,8},{8,0},{1,9},{9,1},{2,10},{10,2},{3,11},{11,3},{4,12},{12,4},... | collective-permute-start | bytes 3538952 | tf_op jit(solution)/shard_map/ppermute | solution.py:54
  218.4 34.6 %collective-permute-start.20 = (bf16[1152,512]{0,1:T(8,128)(2,1)S(1)}, bf16[1152,512]{0,1:T(8,128)(2,1)S(1)}, u32[]{:S(2)}, u32[]{:S(2)}) collective-permute-start(bf16[1152,512]{0,1:T(8,128)(2,1)S(1)} %bitcast.108), channel_id=1, source_target_pairs={{0,8},{8,0},{1,9},{9,1},{2,10},{10,2},{3,11},{11,3},{4,12},{12,4},... | collective-permute-start | bytes 3538952 | tf_op jit(solution)/shard_map/ppermute | solution.py:54
  218.9 35.6 %collective-permute-start.17 = (bf16[512,1152]{1,0:T(8,128)(2,1)}, bf16[512,1152]{1,0:T(8,128)(2,1)}, u32[]{:S(2)}, u32[]{:S(2)}) collective-permute-start(bf16[512,1152]{1,0:T(8,128)(2,1)} %get-tuple-element.70.refs_0_), channel_id=1, source_target_pairs={{0,8},{8,0},{1,9},{9,1},{2,10},{10,2},{3,11},{11,3},{4,12},{12,4},... | collective-permute-start | bytes 3538952 | tf_op jit(solution)/shard_map/ppermute | solution.py:54
  219.0 35.5 %collective-permute-start.19 = (bf16[1152,512]{1,0:T(8,128)(2,1)}, bf16[1152,512]{1,0:T(8,128)(2,1)}, u32[]{:S(2)}, u32[]{:S(2)}) collective-permute-start(bf16[1152,512]{1,0:T(8,128)(2,1)} %get-tuple-element.71.refs_4_), channel_id=1, source_target_pairs={{0,8},{8,0},{1,9},{9,1},{2,10},{10,2},{3,11},{11,3},{4,12},{12,4},... | collective-permute-start | bytes 3538952 | tf_op jit(solution)/shard_map/ppermute | solution.py:54
  361.2 31.2 %collective-permute-start.60 = (bf16[2,192,1024]{2,1,0:T(8,128)(2,1)}, bf16[2,192,1024]{2,1,0:T(8,128)(2,1)S(1)}, u32[]{:S(2)}, u32[]{:S(2)}) collective-permute-start(bf16[2,192,1024]{2,1,0:T(8,128)(2,1)} %bitcast.121), channel_id=1, source_target_pairs={{4,0},{5,1},{6,2},{7,3},{12,8},{13,9},{14,10},{15,11},{20,16},{21,... | collective-permute-start | bytes 2359304 | tf_op jit(solution)/shard_map/ppermute | solution.py:924
  427.9 29.4 %collective-permute-start.72 = (bf16[2,576,384]{2,1,0:T(8,128)(2,1)}, bf16[2,576,384]{2,1,0:T(8,128)(2,1)S(1)}, u32[]{:S(2)}, u32[]{:S(2)}) collective-permute-start(bf16[2,576,384]{2,1,0:T(8,128)(2,1)} %get-tuple-element.103), channel_id=1, source_target_pairs={{0,4},{4,0},{1,5},{5,1},{2,6},{6,2},{3,7},{7,3},{8,12},{12,8},{9,1... | collective-permute-start | bytes 2654216 | tf_op jit(solution)/shard_map/ppermute | solution.py:259
  429.4 29.8 %collective-permute-start.74 = (bf16[2,576,384]{2,1,0:T(8,128)(2,1)}, bf16[2,576,384]{2,1,0:T(8,128)(2,1)S(1)}, u32[]{:S(2)}, u32[]{:S(2)}) collective-permute-start(bf16[2,576,384]{2,1,0:T(8,128)(2,1)} %get-tuple-element.105), channel_id=1, source_target_pairs={{0,16},{16,0},{1,17},{17,1},{2,18},{18,2},{3,19},{19,3},{4,20},{20... | collective-permute-start | bytes 2654216 | tf_op jit(solution)/shard_map/ppermute | solution.py:260
  441.7 88.9 %reduce-scatter.7.cloned.1.call-start = ((), (), s32[]{:S(2)}) async-start(), calls=%async_computation.5 | async-start | bytes 1105920 | tf_op jit(solution)/shard_map/reduce_scatter | solution.py:266
  473.8 66.0 %reduce-scatter.9.cloned.1.call-start = ((), (), s32[]{:S(2)}) async-start(), calls=%async_computation.6 | async-start | bytes 1105920 | tf_op jit(solution)/shard_map/reduce_scatter | solution.py:266
  504.8 61.5 %reduce-scatter.11.cloned.1.call-start = ((), (), s32[]{:S(2)}) async-start(), calls=%async_computation.7 | async-start | bytes 1105920 | tf_op jit(solution)/shard_map/reduce_scatter | solution.py:266
  529.7 72.0 %all-gather.7.cloned.1.call-start = ((), (), s32[]{:S(2)}) async-start(), calls=%async_computation.8 | async-start | bytes 1990656 | tf_op jit(solution)/shard_map/all_gather | solution.py:270
  530.3 106.7 %all-gather.9.cloned.1.call-start = ((), (), s32[]{:S(2)}) async-start(), calls=%async_computation.9 | async-start | bytes 5971968 | tf_op jit(solution)/shard_map/all_gather | solution.py:270
  (134 other events, 1915.1 us)
Sparse Core Ops, SparseCore 0:
  441.8 34.9 reduce-scatter.4
  479.7 28.6 reduce-scatter.6
  511.3 28.4 reduce-scatter.8
  542.5 23.6 reduce-scatter.10
  567.9 25.7 all-gather.6
  595.5 41.4 all-gather.8

commit v2 on v1

--- a/solution.py
+++ b/solution.py
@@ -18,6 +18,7 @@
 HALF_KEY = GROUPS * HEAD_WIDTH
 CHUNKS = 3
 BLOCKS = 4
+GAIN_ROWS = 16
 
 low_type = jnp.bfloat16
 eps_norm = 1e-05
@@ -54,6 +55,17 @@
     return lax.ppermute(value, "core", PAIR)
 
 
+def behind(value, others):
+    return lax.optimization_barrier((value, *others))[0]
+
+
+def ignoring(kernel, given, after):
+    def wrapped(*refs):
+        kernel(*refs[:given], *refs[given + len(after) :])
+
+    return wrapped
+
+
 def params():
     return pltpu.CompilerParams(vmem_limit_bytes=VMEM_LIMIT)
 
@@ -66,30 +78,34 @@
     return jax.ShapeDtypeStruct(tuple(dims), kind)
 
 
-def pack_attn_kernel(info, q_ref, k_ref, v_ref, o_ref, own_ref, *piece_ref):
+def pack_attn_kernel(info, q_ref, k_ref, v_ref, o_ref, gain_ref, own_ref, *piece_ref):
     def half(ref):
         size = ref.shape[1] // 2
         value = ref[...].astype(low_type)
         return jnp.where(info[0] == 0, value[:, :size], value[:, size:])
 
     own_ref[...] = jnp.concatenate([half(r) for r in (q_ref, k_ref, v_ref, o_ref)], axis=1)
+    rows = own_ref.shape[0]
     for ref in piece_ref:
         part = ref.shape[1]
-        ref[...] = own_ref[:, pl.ds(pl.multiple_of(info[1] * part, part), part)]
-
-
-def pack_attn(info, arrays, tuned):
+        ref[:rows, :] = own_ref[:, pl.ds(pl.multiple_of(info[1] * part, part), part)]
+        gains = jnp.concatenate([gain_ref[...], jnp.zeros((GAIN_ROWS - 2, rows), jnp.float32)], axis=0)
+        gains = jnp.concatenate([gains, jnp.zeros((GAIN_ROWS, part - rows), jnp.float32)], axis=1)
+        ref[rows:, :] = gains.astype(low_type)
+
+
+def pack_attn(info, arrays, gains, tuned):
     rows = arrays[0].shape[0]
     width = sum(a.shape[1] for a in arrays) // 2
-    outs = [shape((rows, width))] + [shape((rows, width // BLOCKS))] * tuned
+    outs = [shape((rows, width))] + [shape((rows + GAIN_ROWS, width // BLOCKS))] * tuned
     return pl.pallas_call(
         pack_attn_kernel,
-        in_specs=[SCALARS] + [pl.BlockSpec()] * 4,
+        in_specs=[SCALARS] + [pl.BlockSpec()] * 5,
         out_specs=[pl.BlockSpec()] * len(outs),
         out_shape=outs,
         compiler_params=params(),
         cost_estimate=cost(0, rows * width * 10),
-    )(info, *arrays)
+    )(info, *arrays, gains)
 
 
 def pack_ffn_kernel(info, gate_ref, up_ref, down_ref, own_ref, *piece_ref):
@@ -115,9 +131,12 @@
 
     @pl.when(step == steps - 1)
     def _():
-        for c, ref in enumerate(piece_ref):
-            size = ref.shape[1]
-            ref[...] = own_ref[c, :, pl.ds(pl.multiple_of(info[1] * size, size), size)]
+        if piece_ref:
+            one, rest = piece_ref
+            size = one.shape[1]
+            at = pl.ds(pl.multiple_of(info[1] * size, size), size)
+            one[...] = own_ref[0, :, at]
+            rest[...] = own_ref[1:, :, at]
 
 
 def pack_ffn(info, gate, up, down, tuned):
@@ -126,7 +145,10 @@
     steps = hidden // hidden_rows
     half = hidden_rows // 2
     packed = 3 * steps * (half // CHUNKS)
-    outs = [shape((CHUNKS, rows, packed))] + [shape((rows, packed // BLOCKS))] * (CHUNKS * tuned)
+    part = packed // BLOCKS
+    outs = [shape((CHUNKS, rows, packed))]
+    if tuned:
+        outs += [shape((rows, part)), shape((CHUNKS - 1, rows, part))]
     columns = pl.BlockSpec((rows, half), lambda z, info: (0, 2 * z + info[0]))
     return pl.pallas_call(
         pack_ffn_kernel,
@@ -134,8 +156,9 @@
             num_scalar_prefetch=1,
             grid=(steps,),
             in_specs=[columns, columns, pl.BlockSpec((half, width), lambda z, info: (info[0], 0))],
-            out_specs=[pl.BlockSpec((CHUNKS, rows, packed), lambda z, info: (0, 0, 0))]
-            + [pl.BlockSpec((rows, packed // BLOCKS), lambda z, info: (0, 0))] * (CHUNKS * tuned),
+            out_specs=[
+                pl.BlockSpec(o.shape, lambda z, info, n=len(o.shape): (0,) * n) for o in outs
+            ],
         ),
         out_shape=outs,
         compiler_params=params(),
@@ -147,10 +170,8 @@
     return [(i, (i + step) % count) for i in range(count)]
 
 
-def assemble_kernel(count, info, own_ref, *refs):
-    pieces, out_ref, sems = refs[:-2], refs[-2], refs[-1]
-    rows = own_ref.shape[0]
-    part = out_ref.shape[2]
+def place_pieces(info, count, own, stacks, forward, out_ref, sems):
+    rows, part = own.shape[0], out_ref.shape[2]
     copies = []
 
     def begin(source, block, row):
@@ -159,49 +180,66 @@
         copies[-1].start()
 
     for b in range(BLOCKS):
-        begin(own_ref.at[:, b * part : (b + 1) * part], b, info[2])
-    for flip in range(BLOCKS):
+        begin(own.at[:, b * part : (b + 1) * part], b, info[2])
+    for flip, stack in enumerate(stacks):
         for k in range(1, count):
-            begin(
-                pieces[flip * (count - 1) + k - 1],
-                jnp.bitwise_xor(info[1], flip),
-                lax.rem(info[2] + count - k, count),
-            )
-    for copy in copies:
-        copy.wait()
-
-
-def assemble(info, own, pieces, count):
+            row = lax.rem(info[2] + (k if forward else count - k), count)
+            begin(stack.at[k - 1], jnp.bitwise_xor(info[1], flip), row)
+    return copies
+
+
+def assemble(info, own, stacks, count):
     rows, width = own.shape
     out = shape((BLOCKS, rows * count, width // BLOCKS))
 
-    def kernel(*refs):
-        assemble_kernel(count, *refs)
+    def kernel(info, own_ref, *refs):
+        for copy in place_pieces(info, count, own_ref, refs[:-2], False, refs[-2], refs[-1]):
+            copy.wait()
 
     return pl.pallas_call(
         kernel,
-        in_specs=[SCALARS] + [ANY] * (1 + len(pieces)),
+        in_specs=[SCALARS] + [ANY] * (1 + len(stacks)),
         out_specs=pl.BlockSpec(),
         out_shape=out,
         scratch_shapes=[pltpu.SemaphoreType.DMA((BLOCKS * count,))],
         compiler_params=params(),
         cost_estimate=cost(0, rows * width * count * 4),
-    )(info, own, *pieces)
-
-
-def gather_weights(info, own, piece, sizes, turn):
-    nz = sizes[2]
-    if piece is None:
-        full = lax.all_gather(own, "z", axis=0, tiled=True)
-        return full.reshape(full.shape[0], BLOCKS, -1).transpose(1, 0, 2)
-    slots = [lax.ppermute(piece, "z", ring(nz, k)) for k in range(1, nz)]
-    by_x = [lax.ppermute(s, "x", PAIR) for s in slots]
-    by_y = [lax.ppermute(s, "y", PAIR) for s in slots]
-    far = [
-        lax.ppermute(by_x[k], "y", PAIR) if (k + turn) % 2 else lax.ppermute(by_y[k], "x", PAIR)
-        for k in range(nz - 1)
-    ]
-    return assemble(info, own, slots + by_x + by_y + far, nz)
+    )(info, own, *stacks)
+
+
+def pick_kernel(info, all_ref, *refs):
+    outs, sems = refs[:-1], refs[-1]
+    count = all_ref.shape[0]
+    copies = []
+    for c, out in enumerate(outs):
+        for k in range(1, count):
+            source = all_ref.at[lax.rem(info[2] + k, count), c]
+            copies.append(pltpu.make_async_copy(source, out.at[k - 1], sems.at[len(copies)]))
+            copies[-1].start()
+    for copy in copies:
+        copy.wait()
+
+
+def pick(info, everyone):
+    count, chunks, rows, part = everyone.shape
+    return pl.pallas_call(
+        pick_kernel,
+        in_specs=[SCALARS, ANY],
+        out_specs=[pl.BlockSpec()] * chunks,
+        out_shape=[shape((count - 1, rows, part))] * chunks,
+        scratch_shapes=[pltpu.SemaphoreType.DMA((chunks * (count - 1),))],
+        compiler_params=params(),
+        cost_estimate=cost(0, count * chunks * rows * part * 4),
+    )(info, everyone)
+
+
+def travel_z(piece, sizes):
+    return [lax.ppermute(piece, "z", ring(sizes[2], k)) for k in range(1, sizes[2])]
+
+
+def gather_whole(own):
+    full = lax.all_gather(own, "z", axis=0, tiled=True)
+    return full.reshape(full.shape[0], BLOCKS, -1).transpose(1, 0, 2)
 
 
 def send_out(info, packed, outs, sems):
@@ -247,22 +285,39 @@
     return (kept.astype(jnp.float32) + came.astype(jnp.float32)).astype(low_type)
 
 
-def scatter_gradients(outs, sizes):
+def scatter_first(outs):
+    if len(outs) == 1:
+        return ()
+    return lax.ppermute(outs[1], "x", PAIR), lax.ppermute(outs[3], "y", PAIR)
+
+
+def scatter_sums(outs, came, last):
+    if len(outs) == 1:
+        return ()
+    came = lax.optimization_barrier((*came, *last))
+    return add_low(outs[0][1], came[0][1]), add_low(outs[2][1], came[1][1])
+
+
+def scatter_second(sums):
+    if len(sums) == 0:
+        return ()
+    return lax.ppermute(sums[0], "y", PAIR), lax.ppermute(sums[1], "x", PAIR)
+
+
+def scatter_mine(outs, first, second, last, sizes):
     ny, nx, nz = sizes
     if len(outs) == 1:
         packed = outs[0]
         total = packed.shape[1]
         split = packed.transpose(1, 0, 2).reshape(total, ny * nx, -1).transpose(1, 0, 2)
-        mine = lax.psum_scatter(split, ("y", "x"), scatter_dimension=0, tiled=True)[0]
-    else:
-        keep_one, send_one, keep_two, send_two = outs
-        came_one = lax.ppermute(send_one, "x", PAIR)
-        came_two = lax.ppermute(send_two, "y", PAIR)
-        one = lax.ppermute(add_low(keep_one[1], came_one[1]), "y", PAIR)
-        two = lax.ppermute(add_low(keep_two[1], came_two[1]), "x", PAIR)
-        one = add_low(add_low(keep_one[0], came_one[0]), one)
-        two = add_low(add_low(keep_two[0], came_two[0]), two)
-        mine = jnp.concatenate([one, two])
+        return lax.psum_scatter(split, ("y", "x"), scatter_dimension=0, tiled=True)[0]
+    second = lax.optimization_barrier((*second, *last))
+    one = add_low(add_low(outs[0][0], first[0][0]), second[0])
+    two = add_low(add_low(outs[2][0], first[1][0]), second[1])
+    return jnp.concatenate([one, two])
+
+
+def scatter_rows(mine):
     return lax.psum_scatter(mine, "z", scatter_dimension=0, tiled=True)
 
 
@@ -440,15 +495,15 @@
     return (2, GROUPS, per), wide, own, past, first, stat
 
 
-def attend(info, query, keyvalue, past, first, size):
+def attend(info, query, keyvalue, past, first, size, after):
     both = keyvalue.shape[2]
     rows = both // 2
     grid, wide, own, past_spec, first_spec, stat = attention_specs(past.shape[0], rows, size)
     pairs = 2 * rows * rows * 3 // 2
     return pl.pallas_call(
-        attend_kernel,
+        ignoring(attend_kernel, 5, after),
         grid=grid,
-        in_specs=[SCALARS, wide, own, past_spec, first_spec],
+        in_specs=[SCALARS, wide, own, past_spec, first_spec] + [ANY] * len(after),
         out_specs=[wide, stat],
         out_shape=[shape(query.shape, jnp.float32), shape((GROUPS, 8, both), jnp.float32)],
         scratch_shapes=[
@@ -458,18 +513,18 @@
         ],
         compiler_params=params(),
         cost_estimate=cost(pairs * 9 * 64 * 4 * 5, 8 << 20, pairs * 9),
-    )(info, query, keyvalue, past, first)
-
-
-def attend_back(info, query, keyvalue, past, grad, first, log_total, delta, size):
+    )(info, query, keyvalue, past, first, *after)
+
+
+def attend_back(info, query, keyvalue, past, grad, first, log_total, delta, size, after):
     both = keyvalue.shape[2]
     rows = both // 2
     grid, wide, own, past_spec, first_spec, stat = attention_specs(past.shape[0], rows, size)
     pairs = 2 * rows * rows * 3 // 2
     return pl.pallas_call(
-        attend_back_kernel,
+        ignoring(attend_back_kernel, 8, after),
         grid=grid,
-        in_specs=[SCALARS, wide, own, past_spec, wide, first_spec, stat, stat],
+        in_specs=[SCALARS, wide, own, past_spec, wide, first_spec, stat, stat] + [ANY] * len(after),
         out_specs=[wide, own, past_spec],
         out_shape=[
             shape(query.shape, jnp.float32), shape(keyvalue.shape, jnp.float32), shape(past.shape)
@@ -480,7 +535,7 @@
         ],
         compiler_params=params(),
         cost_estimate=cost(pairs * 9 * 64 * 10 * 3, 12 << 20, pairs * 9),
-    )(info, query, keyvalue, past, grad, first, log_total, delta)
+    )(info, query, keyvalue, past, grad, first, log_total, delta, *after)
 
 
 def place_out(core, mine_ref, other_ref, out_ref):
@@ -514,12 +569,12 @@
     turned_ref[...] = normed.T
 
 
-def project_out(info, attended, came, weights, weights_other, tokens, gain):
+def project_out(info, attended, came, weights, weights_other, tokens, gain, after):
     rows, width = tokens.shape
     hq = HALF_QUERY
     part = weights.shape[2]
     return pl.pallas_call(
-        out_kernel,
+        ignoring(out_kernel, 7, after),
         grid=(1,),
         in_specs=[
             SCALARS,
@@ -529,7 +584,8 @@
             pl.BlockSpec((2, width, part), lambda i: (0, 0, 0)),
             pl.BlockSpec((rows, width), lambda i: (0, 0)),
             pl.BlockSpec((1, width), lambda i: (0, 0)),
-        ],
+        ]
+        + [ANY] * len(after),
         out_specs=[
             pl.BlockSpec((rows, width), lambda i: (0, 0)),
             pl.BlockSpec((rows, width), lambda i: (0, 0)),
@@ -543,35 +599,46 @@
         scratch_shapes=[pltpu.VMEM((width, width), low_type)],
         compiler_params=params(),
         cost_estimate=cost(2 * rows * width * width, 16 << 20),
-    )(info, attended, came, weights, weights_other, tokens, gain)
-
-
-def ffn_kernel(held, info, *refs):
+    )(info, attended, came, weights, weights_other, tokens, gain, *after)
+
+
+def ffn_kernel(chunk, pieces, held, after, info, *refs):
     x_refs, c_refs, xt_refs, ct_refs, w_ref = refs[0:2], refs[2:4], refs[4:6], refs[6:8], refs[8]
-    sums = refs[9 : 9 + 2 * held]
-    refs = refs[9 + 2 * held :]
+    others = refs[9 : 9 + pieces]
+    refs = refs[9 + pieces :]
+    sums = refs[: 2 * held]
+    refs = refs[2 * held + after :]
     result_ref, grad_ref, outs = refs[0], refs[1], refs[2:-9]
-    gate_s, up_s, down_s, hidden_s, dgate_s, dup_s, packed_s, _, sems = refs[-9:]
+    gate_s, up_s, down_s, hidden_s, dgate_s, dup_s, packed_s, sems, place_sems = refs[-9:]
     step = pl.program_id(0)
     size = result_ref.shape[0]
     half = 2
     block = gate_s.shape[1]
-    part = w_ref.shape[2]
+    part = packed_s.shape[2]
     width = gate_s.shape[0]
     lane = block // BLOCKS
     rows = width // BLOCKS
 
     @pl.when(step == 0)
     def _():
-        gate_s[:, :part] = w_ref[0]
-        gate_s[:, part:] = w_ref[1, :, : block - part]
-        up_s[:, : 2 * part - block] = w_ref[1, :, block - part :]
-        up_s[:, 2 * part - block :] = w_ref[2, :, : 2 * block - 2 * part]
+        if pieces:
+            copies = place_pieces(
+                info, BLOCKS, w_ref.at[chunk], others, chunk > 0, packed_s, place_sems
+            )
+        else:
+            copies = [pltpu.make_async_copy(w_ref, packed_s, place_sems.at[0])]
+            copies[0].start()
+        for copy in copies:
+            copy.wait()
+        gate_s[:, :part] = packed_s[0]
+        gate_s[:, part:] = packed_s[1, :, : block - part]
+        up_s[:, : 2 * part - block] = packed_s[1, :, block - part :]
+        up_s[:, 2 * part - block :] = packed_s[2, :, : 2 * block - 2 * part]
         for q in range(BLOCKS):
             for z in range(BLOCKS):
                 column = 2 * block + q * lane
                 b, at = column // part, column % part
-                down_s[q * rows : (q + 1) * rows, z * lane : (z + 1) * lane] = w_ref[
+                down_s[q * rows : (q + 1) * rows, z * lane : (z + 1) * lane] = packed_s[
                     b, z * rows : (z + 1) * rows, at : at + lane
                 ]
 
@@ -624,10 +691,10 @@
         send_out(info, packed_s, outs, sems)
 
 
-def ffn_chunk(info, xs, cs, xts, cts, weights, sums, tuned):
+def ffn_chunk(chunk, info, xs, cs, xts, cts, weights, pieces, sums, after, tuned):
     rows, width = xs[0].shape
     size = rows // 2
-    part = weights.shape[2]
+    part = weights.shape[2] // (BLOCKS if tuned else 1)
     block = BLOCKS * part // 3
     turned = width // BLOCKS
 
@@ -650,13 +717,13 @@
     sent = sent_shapes(width, part, tuned)
 
     def kernel(info, *refs):
-        ffn_kernel(held, info, *refs)
+        ffn_kernel(chunk, len(pieces), held, len(after), info, *refs)
 
     return pl.pallas_call(
         kernel,
         grid=(8,),
-        in_specs=[SCALARS] + token + token + across + across
-        + [pl.BlockSpec(weights.shape, lambda i: (0, 0, 0))] + (total if held else []),
+        in_specs=[SCALARS] + token + token + across + across + [ANY] * (1 + len(pieces))
+        + (total if held else []) + [ANY] * len(after),
         out_specs=total + [ANY] * len(sent),
         out_shape=[shape((2 * rows, width), jnp.float32)] * 2 + sent,
         scratch_shapes=[
@@ -667,12 +734,12 @@
             pltpu.VMEM((2 * rows, block), low_type),
             pltpu.VMEM((2 * rows, block), low_type),
             pltpu.VMEM((BLOCKS, width, part), low_type),
-            pltpu.VMEM((8, 128), jnp.float32),
             pltpu.SemaphoreType.DMA((8,)),
+            pltpu.SemaphoreType.DMA((BLOCKS * BLOCKS,)),
         ],
         compiler_params=params(),
         cost_estimate=cost(18 * 2 * rows * width * block, 40 << 20, 2 * rows * block),
-    )(info, *xs, *cs, *xts, *cts, weights, *sums)
+    )(info, *xs, *cs, *xts, *cts, weights, *pieces, *sums, *after)
 
 
 def branch_kernel(g_ref, g_other_ref, w_ref, attended_ref, grad_ref, delta_ref, rows_ref):
@@ -693,11 +760,11 @@
     ).astype(low_type)
 
 
-def branch(grad, grad_other, out_rows, attended):
+def branch(grad, grad_other, out_rows, attended, after):
     rows, width = grad.shape
     return pl.pallas_call(
-        branch_kernel,
-        in_specs=[pl.BlockSpec()] * 4,
+        ignoring(branch_kernel, 4, after),
+        in_specs=[pl.BlockSpec()] * 4 + [ANY] * len(after),
         out_specs=[pl.BlockSpec()] * 3,
         out_shape=[
             shape(attended.shape), shape((GROUPS, 8, 2 * rows), jnp.float32),
@@ -705,7 +772,7 @@
         ],
         compiler_params=params(),
         cost_estimate=cost(8 * rows * width * HALF_QUERY, 12 << 20),
-    )(grad, grad_other, out_rows, attended)
+    )(grad, grad_other, out_rows, attended, *after)
 
 
 def attn_grad_kernel(
@@ -733,13 +800,13 @@
     send_out(info, packed_s, outs, sems)
 
 
-def attn_grads(info, grad_query, grad_kv, came, cosine, sine, normed, mine, other, tuned):
+def attn_grads(info, grad_query, grad_kv, came, cosine, sine, normed, mine, other, after, tuned):
     width, both = normed.shape
     part = (2 * HALF_QUERY + 2 * HALF_KEY) // BLOCKS
     sent = sent_shapes(width, part, tuned)
     return pl.pallas_call(
-        attn_grad_kernel,
-        in_specs=[SCALARS] + [pl.BlockSpec()] * 8,
+        ignoring(attn_grad_kernel, 9, after),
+        in_specs=[SCALARS] + [pl.BlockSpec()] * 8 + [ANY] * len(after),
         out_specs=[pl.BlockSpec()] + [ANY] * len(sent),
         out_shape=[shape((HALF_QUERY + 2 * HALF_KEY, both))] + sent,
         scratch_shapes=[
@@ -748,7 +815,7 @@
         ],
         compiler_params=params(),
         cost_estimate=cost(2 * both * width * 960, 20 << 20),
-    )(info, grad_query, grad_kv, came, cosine, sine, normed, mine, other)
+    )(info, grad_query, grad_kv, came, cosine, sine, normed, mine, other, *after)
 
 
 def normed_grad_kernel(d_ref, w_ref, mine_ref, other_ref):
@@ -762,17 +829,17 @@
         ref[...] = value.astype(ref.dtype)
 
 
-def normed_grad(d, weights):
+def normed_grad(d, weights, after):
     width = weights.shape[1]
     rows = d.shape[1] // 2
     return pl.pallas_call(
-        normed_grad_kernel,
-        in_specs=[pl.BlockSpec()] * 2,
+        ignoring(normed_grad_kernel, 2, after),
+        in_specs=[pl.BlockSpec()] * 2 + [ANY] * len(after),
         out_specs=[pl.BlockSpec()] * 2,
         out_shape=[shape((rows, width), jnp.float32), shape((rows, width))],
         compiler_params=params(),
         cost_estimate=cost(4 * rows * width * 960, 9 << 20),
-    )(d, weights)
+    )(d, weights, *after)
 
 
 def unpack_attn_kernel(all_ref, q_ref, k_ref, v_ref, o_ref):
@@ -801,14 +868,15 @@
     )(everyone)
 
 
-def unpack_ffn_kernel(all_ref, gate_ref, up_ref, down_ref):
-    rows, part = all_ref.shape[3], all_ref.shape[4]
+def unpack_ffn_kernel(*refs):
+    all_refs, (gate_ref, up_ref, down_ref) = refs[:CHUNKS], refs[CHUNKS:]
+    rows, part = all_refs[0].shape[3], all_refs[0].shape[4]
     block = BLOCKS * part // 3
     lane = block // BLOCKS
     half = CHUNKS * lane
     for h in range(2):
         for c in range(CHUNKS):
-            value = jnp.concatenate([all_ref[h, b, c] for b in range(BLOCKS)], axis=1)
+            value = jnp.concatenate([all_refs[c][h, b, 0] for b in range(BLOCKS)], axis=1)
             value = value.astype(jnp.float32)
             for z in range(BLOCKS):
                 at = z * 2 * half + h * half + c * lane
@@ -822,11 +890,11 @@
 
 
 def unpack_ffn(everyone):
-    rows, part = everyone.shape[3:]
+    rows, part = everyone[0].shape[3:]
     lane = part // 3
     return pl.pallas_call(
         unpack_ffn_kernel,
-        in_specs=[pl.BlockSpec()],
+        in_specs=[pl.BlockSpec()] * CHUNKS,
         out_specs=[pl.BlockSpec()] * 3,
         out_shape=[
             shape((rows, 2 * BLOCKS * CHUNKS * lane), jnp.float32),
@@ -835,7 +903,7 @@
         ],
         compiler_params=params(),
         cost_estimate=cost(0, 16 << 20),
-    )(everyone)
+    )(*everyone)
 
 
 def shards(sizes, *arrays):
@@ -852,13 +920,36 @@
     rows, width = tokens.shape
     own_rows = w_query.shape[0]
 
-    attn_own, *attn_piece = pack_attn(info, (w_query, key_matrix, value_matrix, w_out), tuned)
+    gains = jnp.stack([attn_gain, ffn_gain])
+    attn_own, *attn_piece = pack_attn(
+        info, (w_query, key_matrix, value_matrix, w_out), gains, tuned
+    )
     ffn_own, *ffn_piece = pack_ffn(info, w_gate, w_up, w_down, tuned)
-    weights = gather_weights(info, attn_own, attn_piece[0] if tuned else None, sizes, 0)
-    ffn_weights = [
-        gather_weights(info, ffn_own[c], ffn_piece[c] if tuned else None, sizes, c + 1)
-        for c in range(CHUNKS)
-    ]
+    if tuned:
+        slots = travel_z(attn_piece[0], sizes)
+        stack = jnp.stack([s[:own_rows] for s in slots])
+        ffn_slots = travel_z(behind(ffn_piece[0], (stack,)), sizes)
+        ffn_stacks = [jnp.stack(ffn_slots)]
+        rest = lax.all_gather(behind(ffn_piece[1], ffn_slots), "z", axis=0)
+        ffn_stacks += pick(info, rest)
+        stacks = (
+            stack,
+            lax.ppermute(stack, "x", PAIR),
+            lax.ppermute(stack, "y", PAIR),
+            lax.ppermute(stack, ("y", "x"), [(i, 3 - i) for i in range(4)]),
+        )
+        weights = assemble(info, attn_own, stacks, nz)
+        ffn_weights = [ffn_own] * CHUNKS
+        gains = [gains.astype(low_type)] + [s[own_rows : own_rows + 2, :own_rows] for s in slots]
+        gains = jnp.stack(gains[::-1] + gains[::-1])
+        gains = lax.dynamic_slice_in_dim(gains, nz - 1 - lax.axis_index("z"), nz, 0)
+        gains = gains.transpose(1, 0, 2).reshape(2, width)
+    else:
+        weights = gather_whole(attn_own)
+        ffn_pieces = [()] * CHUNKS
+        before_attend = before_out = ()
+        ffn_weights = [gather_whole(ffn_own[c]) for c in range(CHUNKS)]
+        gains = lax.all_gather(gains.astype(low_type), "z", axis=1, tiled=True)
     weights_other = swap_core(weights[2:])
 
     all_ids = lax.all_gather(ids, "x", axis=0, tiled=True)
@@ -873,7 +964,6 @@
     info = jnp.concatenate([info, starts.reshape(-1)])
     firsts = firsts[:, None, :]
 
-    gains = lax.all_gather(jnp.stack([attn_gain, ffn_gain]).astype(low_type), "z", axis=1, tiled=True)
     gain_one, gain_two = gains[:1].astype(jnp.float32), gains[1:].astype(jnp.float32)
 
     turned = cotangent.T
@@ -882,22 +972,40 @@
     normed, query, keyvalue = project(
         tokens, swap_core(tokens), gain_one, weights, cosine, sine
     )
-    if nx == 2:
-        past = lax.ppermute(keyvalue, "x", [(0, 1)])[None]
+    if tuned:
+        by_x = [lax.ppermute(s, "x", PAIR) for s in ffn_stacks]
+        by_y = [lax.ppermute(s, "y", PAIR) for s in ffn_stacks]
+        far = [
+            lax.ppermute(by_x[0], "y", PAIR),
+            lax.ppermute(by_x[1], "y", PAIR),
+            lax.ppermute(by_y[2], "x", PAIR),
+        ]
+        ffn_pieces = list(zip(ffn_stacks, by_x, by_y, far))
+        past = lax.ppermute(behind(keyvalue, (by_x[0],)), "x", [(0, 1)])[None]
+        before_attend = (by_y[0], *ffn_stacks[1:])
+        before_out = (by_x[1], by_y[1], far[0])
     else:
         past = lax.all_gather(keyvalue, "x", axis=0)
-    attended, log_total = attend(info, query, keyvalue, past, firsts, size)
+    attended, log_total = attend(info, query, keyvalue, past, firsts, size, before_attend)
     came = swap_core(attended[:, rows:].astype(low_type))
     middle, normed_two, normed_turned, out_rows = project_out(
-        info, attended, came, weights, weights_other, tokens, gain_two
+        info, attended, came, weights, weights_other, tokens, gain_two, before_out
     )
 
     xs, xts = (normed_two, swap_core(normed_two)), (normed_turned, swap_core(normed_turned))
-    sums, ffn_sent = (), []
+    sums, ready = (), ()
+    sent, first, send, second, mine_ffn = ([None] * (CHUNKS + 1) for _ in range(5))
     for c in range(CHUNKS):
-        *sums, = ffn_chunk(info, xs, cs, xts, cts, ffn_weights[c], sums, tuned)
-        sums, sent = sums[:2], sums[2:]
-        ffn_sent.append(sent)
+        *sums, = ffn_chunk(
+            c, info, xs, cs, xts, cts, ffn_weights[c], ffn_pieces[c], sums, ready, tuned
+        )
+        sums, sent[c] = sums[:2], sums[2:]
+        first[c] = scatter_first(sent[c])
+        if c >= 1:
+            ready = send[c - 1] = scatter_sums(sent[c - 1], first[c - 1], sums[:1])
+            second[c - 1] = scatter_second(send[c - 1])
+        if c >= 2:
+            mine_ffn[c - 2] = scatter_mine(sent[c - 2], first[c - 2], second[c - 2], sums[:1], sizes)
     result, grad_normed_two = sums
 
     def pair_sum(value):
@@ -913,21 +1021,32 @@
     output = (middle + pair_sum(result)).astype(low_type)
 
     grad_other = swap_core(grad_branch)
-    grad_attended, delta, grad_rows = branch(grad_branch, grad_other, out_rows, attended)
+    grad_attended, delta, grad_rows = branch(
+        grad_branch, grad_other, out_rows, attended, (mine_ffn[0], *send[1])
+    )
     hq = HALF_QUERY
     mine = lax.dynamic_slice_in_dim(grad_rows, core * hq, hq, 1)
     other = swap_core(lax.dynamic_slice_in_dim(grad_rows, (1 - core) * hq, hq, 1))
+    last = (grad_attended,)
+    send[2] = scatter_sums(sent[2], first[2], last)
+    second[2] = scatter_second(send[2])
+    mine_ffn[1] = scatter_mine(sent[1], first[1], second[1], last, sizes)
     grad_query, grad_kv, grad_past = attend_back(
-        info, query, keyvalue, past, grad_attended, firsts, log_total, delta, size
-    )
-    if nx == 2:
+        info, query, keyvalue, past, grad_attended, firsts, log_total, delta, size,
+        (*send[2], mine_ffn[1]),
+    )
+    mine_ffn[2] = scatter_mine(sent[2], first[2], second[2], (grad_past,), sizes)
+    ffn_sums = [scatter_rows(mine) for mine in mine_ffn[:CHUNKS]]
+    ffn_all = [spread(total[None], sizes) for total in ffn_sums]
+    if tuned:
         came = lax.ppermute(grad_past[0], "x", [(1, 0)])
     else:
         came = lax.psum_scatter(grad_past, "x", scatter_dimension=0, tiled=True)[0]
     grad_projected, *attn_sent = attn_grads(
-        info, grad_query, grad_kv, came, cosine, sine, normed, mine, other, tuned
-    )
-    normed_mine, normed_other = normed_grad(grad_projected, weights)
+        info, grad_query, grad_kv, came, cosine, sine, normed, mine, other,
+        (ffn_sums[0], mine_ffn[2]), tuned,
+    )
+    normed_mine, normed_other = normed_grad(grad_projected, weights, ())
     grad_normed = normed_mine + swap_core(normed_other).astype(jnp.float32)
     inputs = tokens.astype(jnp.float32)
     scale_one = norm_scale(inputs)
@@ -941,9 +1060,12 @@
         gain_grads = sum_over(gain_grads, axis, count)
     gain_grads = lax.dynamic_slice_in_dim(gain_grads, lax.axis_index("z") * own_rows, own_rows, 1)
 
-    ffn_sums = jnp.stack([scatter_gradients(sent, sizes) for sent in ffn_sent])
-    attn_sum = scatter_gradients(attn_sent, sizes)
-    grad_w_gate, grad_w_up, grad_w_down = unpack_ffn(spread(ffn_sums, sizes))
+    sent[3], first[3] = attn_sent, scatter_first(attn_sent)
+    send[3] = scatter_sums(attn_sent, first[3], (normed_mine, ffn_all[0]))
+    second[3] = scatter_second(send[3])
+    mine_attn = scatter_mine(attn_sent, first[3], second[3], (ffn_all[1],), sizes)
+    attn_sum = scatter_rows(mine_attn)
+    grad_w_gate, grad_w_up, grad_w_down = unpack_ffn(ffn_all)
     attn_out = unpack_attn(spread(attn_sum[None], sizes))
     return (
         output[None], grad_inputs[None], gain_grads[0], *attn_out, gain_grads[1], grad_w_gate,

time: 653 us -> 521 us (0.80)
  waiting for transfers between devices: 261 us -> 181 us
  starting transfers between devices: 119 us -> 68.6 us
  blocking collectives: 22.4 us -> 4.33 us
  local copies, waits for them, and re-layouts: 19.4 us -> 31.8 us
  Pallas kernels: 182 us -> 170 us
  other arithmetic: 31.8 us -> 43 us
    ppermute x65 -> x35, waiting for transfers between devices: 150 us -> 98.8 us  [the longest x8 38.1 us: scatter_first(): return (lax.ppermute(outs[1], 'x', PAIR), lax.ppermute(outs[3], 'y', PAIR))]
    ppermute x65 -> x35, starting transfers between devices: 110 us -> 60 us  [the longest x8 11 us: scatter_first(): return (lax.ppermute(outs[1], 'x', PAIR), lax.ppermute(outs[3], 'y', PAIR))]
    all_gather x1 -> x0, blocking collectives: 18.1 us -> none  [shards(): lax.all_gather(jnp.stack([attn_gain, ffn_gain]).astype(low_type), 'z', ax...]
    pallas_call x11 -> x9, Pallas kernels: 94.6 us -> 79.6 us  [the longest x1 16.2 us: attend_back(): pl.pallas_call(ignoring(attend_back_kernel, 8, after), grid=grid, in_spec...]
    reduce_scatter x4, waiting for transfers between devices: 35.6 us -> 21.2 us  [scatter_rows(): return lax.psum_scatter(mine, 'z', scatter_dimension=0, tiled=True)]
    all_gather x2 -> x4, waiting for transfers between devices: 31.6 us -> 24.7 us  [spread(): everyone = lax.all_gather(mine, ('core', 'y', 'x'), axis=0)]
    convert_element_type x16 -> x15, other arithmetic: 9.3 us -> 16 us  [add_low(): (kept.astype(jnp.float32) + came.astype(jnp.float32)).astype(low_type)]
    ppermute x13, waiting for transfers between devices: 7.58 us -> 0.95 us  [swap_core(): return lax.ppermute(value, 'core', PAIR)]
  transfers between devices with their start and end apart: 90 -> 63, of which waited for: 40 -> 30; matrix products, arithmetic and copies ran while one was open for 6% -> 12% of each run, Pallas kernels for 11% -> 27%
where the time goes in v2:
time: 521 us; the launch traced here: 514 us
  waiting for transfers between devices  181 us (35%)
  Pallas kernels  170 us (33%)
  starting transfers between devices  68.6 us (13%)
  other arithmetic  43 us (8%)
  local copies, waits for them, and re-layouts  31.8 us (6%)
  between operations  14.7 us (3%)
    pallas_call x3, Pallas kernels, ffn_chunk(): pl.pallas_call(kernel, grid=(8,), in_specs=[SCALARS] + token + token + ac...  70.3 us
    ppermute x8, waiting for transfers between devices, scatter_first(): return (lax.ppermute(outs[1], 'x', PAIR), lax.ppermute(outs[3], 'y', PAIR))  38.1 us
    all_gather x4, waiting for transfers between devices, spread(): everyone = lax.all_gather(mine, ('core', 'y', 'x'), axis=0)  24.7 us
    ppermute x1, waiting for transfers between devices, shards(): came = lax.ppermute(grad_past[0], 'x', [(1, 0)])  23.7 us
    reduce_scatter x4, waiting for transfers between devices, scatter_rows(): return lax.psum_scatter(mine, 'z', scatter_dimension=0, tiled=True)  21.2 us
    ppermute x8, waiting for transfers between devices, scatter_second(): return (lax.ppermute(sums[0], 'y', PAIR), lax.ppermute(sums[1], 'x', PAIR))  19.9 us
    ppermute x6, waiting for transfers between devices, travel_z(): lax.ppermute(piece, 'z', ring(sizes[2], k))  18 us
    pallas_call x1, Pallas kernels, attend_back(): pl.pallas_call(ignoring(attend_back_kernel, 8, after), grid=grid, in_spec...  16.2 us
  transfers between devices with their start and end apart: 63, of which 30 were waited for; matrix products, arithmetic and copies ran while one was open for 12% of the time, Pallas kernels for 27%

profile of v2, /device:TPU:0, one launch (start us, length us, event | category | flops | bytes accessed | tf_op | source)
XLA Modules:
  0.0 513.8 jit_solution(2422059359191233253)
XLA Ops:
  24.6 6.1 %shard_map.206 = (bf16[3,288,1536]{2,1,0:T(8,128)(2,1)}, bf16[288,384]{1,0:T(8,128)(2,1)}, bf16[2,288,384]{2,1,0:T(8,128)(2,1)}) custom-call(s32[4]{0:T(128)} %pad_add_fusion.2.info, f32[288,3072]{1,0:T(8,128)} %gate_ref.1, f32[288,3072]{1,0:T(8,128)} %up_ref.1, f32[768,1152]{1,0:T(8,128)} %down_ref.1), custom_call_target="tpu_custom_call" | custom-call | bytes 7962624 | tf_op jit(solution)/shard_map/pallas_call | solution.py:153
  32.1 6.4 %collective-permute-done.3 = bf16[304,384]{1,0:T(8,128)(2,1)S(1)} collective-permute-done((bf16[304,384]{1,0:T(8,128)(2,1)}, bf16[304,384]{1,0:T(8,128)(2,1)S(1)}, u32[]{:S(2)}, u32[]{:S(2)}) %collective-permute-start.3) | collective-permute-done | bytes 233504 | tf_op jit(solution)/shard_map/ppermute | solution.py:237
  82.1 7.4 %shard_map.205 = (bf16[1152,1024]{1,0:T(8,128)(2,1)}, bf16[576,1024]{1,0:T(8,128)(2,1)}, bf16[2,192,1024]{2,1,0:T(8,128)(2,1)}) custom-call(bf16[512,1152]{1,0:T(8,128)(2,1)} %bitcast.116, bf16[512,1152]{1,0:T(8,128)(2,1)} %collective-permute-done.1.other_ref, f32[1,1152]{1,0:T(1,128)} %reshape.257.gain_ref, ...), custom_call_target="tpu_custom_call" | custom-call | flops 2264924160 | bytes 14680064 | tf_op jit(solution)/shard_map/pallas_call | solution.py:365
  112.7 13.9 %shard_map.208 = (f32[576,1024]{1,0:T(8,128)}, f32[3,8,1024]{2,1,0:T(8,128)}) custom-call(s32[8]{0:T(128)} %concatenate.37.refs_0_.info, bf16[576,1024]{1,0:T(8,128)(2,1)} %get-tuple-element.86.refs_1_, bf16[2,192,1024]{2,1,0:T(8,128)(2,1)} %get-tuple-element.90.refs_2_, bf16[1,2,192,1024]{3,2,1,0:T(8,128)(2,1)} %bitcast.136, ...), custom_call_target="tpu_custom_call" | custom-call | flops 9059696640 | bytes 8388608 | tf_op jit(solution)/shard_map/pallas_call | solution.py:503
  134.4 9.4 %shard_map.209 = (f32[512,1152]{1,0:T(8,128)}, bf16[512,1152]{1,0:T(8,128)(2,1)}, bf16[1152,512]{1,0:T(8,128)(2,1)}, bf16[576,1152]{1,0:T(8,128)(2,1)}) custom-call(s32[8]{0:T(128)} %concatenate.37.refs_0_.info, f32[576,1024]{1,0:T(8,128)} %get-tuple-element.95.refs_1_.refs_3_, bf16[576,512]{1,0:T(8,128)(2,1)} %copy-done.27, ...), custom_call_target="tpu_custom_call" | custom-call | flops 1358954496 | bytes 16777216 | tf_op jit(solution)/shard_map/pallas_call | solution.py:576
  149.6 6.4 %collective-permute-start.23 = (bf16[3,288,384]{2,1,0:T(8,128)(2,1)}, bf16[3,288,384]{2,1,0:T(8,128)(2,1)}, u32[]{:S(2)}, u32[]{:S(2)}) collective-permute-start(bf16[3,288,384]{2,1,0:T(8,128)(2,1)} %get-tuple-element.94.refs_7_.refs_9_), channel_id=1, source_target_pairs={{0,4},{4,0},{1,5},{5,1},{2,6},{6,2},{3,7},{7,3},{8,12},{12,8},{9,1... | collective-permute-start | bytes 1990664 | tf_op jit(solution)/shard_map/ppermute | solution.py:976
  156.1 6.3 %collective-permute-done.24.refs_11_ = bf16[3,288,384]{2,1,0:T(8,128)(2,1)} collective-permute-done((bf16[3,288,384]{2,1,0:T(8,128)(2,1)}, bf16[3,288,384]{2,1,0:T(8,128)(2,1)}, u32[]{:S(2)}, u32[]{:S(2)}) %collective-permute-start.24) | collective-permute-done | bytes 663584 | tf_op jit(solution)/shard_map/ppermute | solution.py:977
  169.3 22.2 %shard_map.210 = (f32[1024,1152]{1,0:T(8,128)}, f32[1024,1152]{1,0:T(8,128)}, bf16[2,576,384]{2,1,0:T(8,128)(2,1)}, bf16[2,576,384]{2,1,0:T(8,128)(2,1)}, bf16[2...) custom-call(s32[8]{0:T(128)} %concatenate.37.refs_0_.info, bf16[512,1152]{1,0:T(8,128)(2,1)} %get-tuple-element.97.refs_0_, ...), custom_call_target="tpu_custom_call" | custom-call | flops 10871635968 | bytes 41943040 | tf_op jit(solution)/shard_map/pallas_call | solution.py:722
  194.5 24.3 %shard_map.211 = (f32[1024,1152]{1,0:T(8,128)}, f32[1024,1152]{1,0:T(8,128)}, bf16[2,576,384]{2,1,0:T(8,128)(2,1)}, bf16[2,576,384]{2,1,0:T(8,128)(2,1)}, bf16[2...) custom-call(s32[8]{0:T(128)} %concatenate.37.refs_0_.info, bf16[512,1152]{1,0:T(8,128)(2,1)} %get-tuple-element.97.refs_0_, ...), custom_call_target="tpu_custom_call" | custom-call | flops 10871635968 | bytes 41943040 | tf_op jit(solution)/shard_map/pallas_call | solution.py:722
  221.6 23.8 %shard_map.212 = (f32[1024,1152]{1,0:T(8,128)}, f32[1024,1152]{1,0:T(8,128)}, bf16[2,576,384]{2,1,0:T(8,128)(2,1)}, bf16[2,576,384]{2,1,0:T(8,128)(2,1)}, bf16[2...) custom-call(s32[8]{0:T(128)} %concatenate.37.refs_0_.info, bf16[512,1152]{1,0:T(8,128)(2,1)} %get-tuple-element.97.refs_0_, ...), custom_call_target="tpu_custom_call" | custom-call | flops 10871635968 | bytes 41943040 | tf_op jit(solution)/shard_map/pallas_call | solution.py:722
  254.8 10.2 %collective-permute-done.33 = bf16[576,384]{1,0:T(8,128)(2,1)} collective-permute-done((bf16[576,384]{1,0:T(8,128)(2,1)}, bf16[576,384]{1,0:T(8,128)(2,1)}, u32[]{:S(2)}, u32[]{:S(2)}) %collective-permute-start.33) | collective-permute-done | bytes 442400 | tf_op jit(solution)/shard_map/ppermute | solution.py:304
  276.8 6.5 %collective-permute-done.34 = bf16[2,576,384]{2,1,0:T(8,128)(2,1)} collective-permute-done((bf16[2,576,384]{2,1,0:T(8,128)(2,1)}, bf16[2,576,384]{2,1,0:T(8,128)(2,1)}, u32[]{:S(2)}, u32[]{:S(2)}) %collective-permute-start.34) | collective-permute-done | bytes 884768 | tf_op jit(solution)/shard_map/ppermute | solution.py:291
  290.8 7.2 %shard_map.213 = (bf16[576,1024]{1,0:T(8,128)(2,1)}, f32[3,8,1024]{2,1,0:T(8,128)}, bf16[576,1152]{1,0:T(8,128)(2,1)}) custom-call(bf16[512,1152]{1,0:T(8,128)(2,1)} %get-tuple-element.165.refs_0_, bf16[512,1152]{1,0:T(8,128)(2,1)} %copy-done.40, bf16[576,1152]{1,0:T(8,128)(2,1)} %get-tuple-element.112.refs_2_, ...), custom_call_target="tpu_custom_call" | custom-call | flops 2717908992 | bytes 12582912 | tf_op jit(solution)/shard_map/pallas_call | solution.py:765
  304.4 16.8 %collective-permute-done.36 = bf16[2,576,384]{2,1,0:T(8,128)(2,1)S(1)} collective-permute-done((bf16[2,576,384]{2,1,0:T(8,128)(2,1)}, bf16[2,576,384]{2,1,0:T(8,128)(2,1)S(1)}, u32[]{:S(2)}, u32[]{:S(2)}) %collective-permute-start.36) | collective-permute-done | bytes 884768 | tf_op jit(solution)/shard_map/ppermute | solution.py:291
  326.2 16.2 %shard_map.214 = (f32[576,1024]{1,0:T(8,128)}, f32[2,192,1024]{2,1,0:T(8,128)}, bf16[1,2,192,1024]{3,2,1,0:T(8,128)(2,1)}) custom-call(s32[8]{0:T(128)} %concatenate.37.refs_0_.info, bf16[576,1024]{1,0:T(8,128)(2,1)} %get-tuple-element.86.refs_1_, bf16[2,192,1024]{2,1,0:T(8,128)(2,1)} %get-tuple-element.90.refs_2_, bf16[1,2,192,1024]{3,2,1,0:T(8,128)(2,1)} %bitcast.137, ...), custom_call_target="tpu_custom_call" | custom-call | flops 13589544960 | bytes 12582912 | tf_op jit(solution)/shard_map/pallas_call | solution.py:524
  348.9 23.7 %collective-permute-done.40.refs_3_ = bf16[2,192,1024]{2,1,0:T(8,128)(2,1)} collective-permute-done((bf16[2,192,1024]{2,1,0:T(8,128)(2,1)}, bf16[2,192,1024]{2,1,0:T(8,128)(2,1)}, u32[]{:S(2)}, u32[]{:S(2)}) %collective-permute-start.40) | collective-permute-done | bytes 786464 | tf_op jit(solution)/shard_map/ppermute | solution.py:1042
  372.6 9.9 %shard_map.215 = (bf16[960,1024]{1,0:T(8,128)(2,1)}, bf16[2,576,384]{2,1,0:T(8,128)(2,1)}, bf16[2,576,384]{2,1,0:T(8,128)(2,1)}, bf16[2,576,384]{2,1,0:T(8,128)(2,1)}, bf16[2,576,384]{2,1,0:T(8,128)(2,1)}) custom-call(s32[8]{0:T(128)} %concatenate.37.refs_0_.info, f32[576,1024]{1,0:T(8,128)} %get-tuple-element.132.refs_1_, ...), custom_call_target="tpu_custom_call" | custom-call | flops 2264924160 | bytes 20971520 | tf_op jit(solution)/shard_map/pallas_call | solution.py:807
  382.7 6.9 %collective-permute-start.51 = (bf16[2,576,384]{2,1,0:T(8,128)(2,1)}, bf16[2,576,384]{2,1,0:T(8,128)(2,1)}, u32[]{:S(2)}, u32[]{:S(2)}) collective-permute-start(bf16[2,576,384]{2,1,0:T(8,128)(2,1)} %get-tuple-element.144), channel_id=1, source_target_pairs={{0,16},{16,0},{1,17},{17,1},{2,18},{18,2},{3,19},{19,3},{4,20},{20... | collective-permute-start | bytes 2654216 | tf_op jit(solution)/shard_map/ppermute | solution.py:291
  389.8 7.6 %shard_map.216 = (f32[512,1152]{1,0:T(8,128)}, bf16[512,1152]{1,0:T(8,128)(2,1)}) custom-call(bf16[960,1024]{1,0:T(8,128)(2,1)} %get-tuple-element.139.refs_0_, bf16[4,1152,384]{2,1,0:T(8,128)(2,1)} %shard_map.204.w_ref.refs_3_.refs_1_), custom_call_target="tpu_custom_call" | custom-call | flops 2264924160 | bytes 9437184 | tf_op jit(solution)/shard_map/pallas_call | solution.py:835
  397.4 6.5 %collective-permute-done.50 = bf16[2,576,384]{2,1,0:T(8,128)(2,1)S(1)} collective-permute-done((bf16[2,576,384]{2,1,0:T(8,128)(2,1)}, bf16[2,576,384]{2,1,0:T(8,128)(2,1)S(1)}, u32[]{:S(2)}, u32[]{:S(2)}) %collective-permute-start.50) | collective-permute-done | bytes 884768 | tf_op jit(solution)/shard_map/ppermute | solution.py:291
  413.6 7.0 %collective-permute-done.53 = bf16[576,384]{1,0:T(8,128)(2,1)S(1)} collective-permute-done((bf16[576,384]{1,0:T(8,128)(2,1)S(1)}, bf16[576,384]{1,0:T(8,128)(2,1)S(1)}, u32[]{:S(2)}, u32[]{:S(2)}) %collective-permute-start.53) | collective-permute-done | bytes 442400 | tf_op jit(solution)/shard_map/ppermute | solution.py:304
  426.3 21.2 %reduce-scatter.9.cloned.1.call-done = bf16[288,384]{1,0:T(8,128)(2,1)} async-done(((bf16[1152,384]{1,0:T(8,128)(2,1)}), bf16[288,384]{1,0:T(8,128)(2,1)}) %reduce-scatter.9.cloned.1.call-update) | async-done | bytes 221200 | tf_op jit(solution)/shard_map/reduce_scatter | solution.py:321
  475.1 7.4 %shard_map.218 = (f32[288,3072]{1,0:T(8,128)}, f32[288,3072]{1,0:T(8,128)}, f32[768,1152]{1,0:T(8,128)}) custom-call(bf16[2,4,1,288,384]{4,3,2,1,0:T(8,128)(2,1)} %bitcast.127, bf16[2,4,1,288,384]{4,3,2,1,0:T(8,128)(2,1)} %bitcast.128, bf16[2,4,1,288,384]{4,3,2,1,0:T(8,128)(2,1)} %bitcast.129), custom_call_target="tpu_custom_call" | custom-call | bytes 16777216 | tf_op jit(solution)/shard_map/pallas_call | solution.py:895
  482.5 21.0 %all-gather.18.cloned.1.call-done = bf16[2304,384]{1,0:T(8,128)(2,1)} async-done(((bf16[288,384]{1,0:T(8,128)(2,1)}), bf16[2304,384]{1,0:T(8,128)(2,1)}) %all-gather.18.cloned.1.call-update) | async-done | bytes 1769488 | tf_op jit(solution)/shard_map/all_gather | solution.py:325
  (307 shorter events, 204.8 us)
Async XLA Ops:
  7.2 93.6 %all-gather.12.cloned.1.call-start = ((), (), s32[]{:S(2)}) async-start(), calls=%async_computation.8 | async-start | bytes 2211840 | tf_op jit(solution)/shard_map/all_gather | solution.py:933
  24.1 58.0 %collective-permute-start.1 = (bf16[512,1152]{1,0:T(8,128)(2,1)S(1)}, bf16[512,1152]{1,0:T(8,128)(2,1)}, u32[]{:S(2)}, u32[]{:S(2)}) collective-permute-start(bf16[512,1152]{1,0:T(8,128)(2,1)S(1)} %bitcast.118), channel_id=1, source_target_pairs={{0,8},{8,0},{1,9},{9,1},{2,10},{10,2},{3,11},{11,3},{4,12},{12,4},... | collective-permute-start | bytes 3538952 | tf_op jit(solution)/shard_map/ppermute | solution.py:55
  44.1 25.0 %collective-permute-start.5 = (bf16[3,288,384]{2,1,0:T(8,128)(2,1)S(1)}, bf16[3,288,384]{2,1,0:T(8,128)(2,1)S(1)}, u32[]{:S(2)}, u32[]{:S(2)}) collective-permute-start(bf16[3,288,384]{2,1,0:T(8,128)(2,1)S(1)} %pad_maximum_fusion.4.refs_0_), channel_id=1, source_target_pairs={{0,4},{4,0},{1,5},{5,1},{2,6},{6,2},{3,7},{7,3},{8,12},{12,8},{9,1... | collective-permute-start | bytes 1990664 | tf_op jit(solution)/shard_map/ppermute | solution.py:937
  48.0 25.5 %collective-permute-start.6 = (bf16[3,288,384]{2,1,0:T(8,128)(2,1)S(1)}, bf16[3,288,384]{2,1,0:T(8,128)(2,1)S(1)}, u32[]{:S(2)}, u32[]{:S(2)}) collective-permute-start(bf16[3,288,384]{2,1,0:T(8,128)(2,1)S(1)} %pad_maximum_fusion.4.refs_0_), channel_id=1, source_target_pairs={{0,16},{16,0},{1,17},{17,1},{2,18},{18,2},{3,19},{19,3},{4,20},{20... | collective-permute-start | bytes 1990664 | tf_op jit(solution)/shard_map/ppermute | solution.py:938
  61.3 240.8 %reduce-scatter.5.cloned.1.call-start = ((), (), s32[]{:S(2)}) async-start(), calls=%async_computation.4 | async-start | bytes 1105920 | tf_op jit(solution)/shard_map/reduce_scatter | solution.py:321
  95.1 34.7 %collective-permute-start.15 = (bf16[2,1152,384]{2,1,0:T(8,128)(2,1)}, bf16[2,1152,384]{2,1,0:T(8,128)(2,1)S(1)}, u32[]{:S(2)}, u32[]{:S(2)}) collective-permute-start(bf16[2,1152,384]{2,1,0:T(8,128)(2,1)} %slice.209), channel_id=1, source_target_pairs={{0,8},{8,0},{1,9},{9,1},{2,10},{10,2},{3,11},{11,3},{4,12},{12,4},... | collective-permute-start | bytes 5308424 | tf_op jit(solution)/shard_map/ppermute | solution.py:55
  97.8 31.6 %collective-permute-start.18 = (bf16[3,288,384]{2,1,0:T(8,128)(2,1)}, bf16[3,288,384]{2,1,0:T(8,128)(2,1)}, u32[]{:S(2)}, u32[]{:S(2)}) collective-permute-start(bf16[3,288,384]{2,1,0:T(8,128)(2,1)} %collective-permute-done.11.refs_10_), channel_id=1, source_target_pairs={{0,16},{16,0},{1,17},{17,1},{2,18},{18,2},{3,19},{19,3},{4,20},{20... | collective-permute-start | bytes 1990664 | tf_op jit(solution)/shard_map/ppermute | solution.py:979
  104.1 26.8 %collective-permute-start.16 = (bf16[3,288,384]{2,1,0:T(8,128)(2,1)}, bf16[3,288,384]{2,1,0:T(8,128)(2,1)}, u32[]{:S(2)}, u32[]{:S(2)}) collective-permute-start(bf16[3,288,384]{2,1,0:T(8,128)(2,1)} %get-tuple-element.93.refs_6_.refs_9_), channel_id=1, source_target_pairs={{0,4},{4,0},{1,5},{5,1},{2,6},{6,2},{3,7},{7,3},{8,12},{12,8},{9,1... | collective-permute-start | bytes 1990664 | tf_op jit(solution)/shard_map/ppermute | solution.py:976
  129.4 26.7 %collective-permute-start.20 = (bf16[512,1152]{1,0:T(8,128)(2,1)S(1)}, bf16[512,1152]{1,0:T(8,128)(2,1)}, u32[]{:S(2)}, u32[]{:S(2)}) collective-permute-start(bf16[512,1152]{1,0:T(8,128)(2,1)S(1)} %bitcast.122), channel_id=1, source_target_pairs={{0,8},{8,0},{1,9},{9,1},{2,10},{10,2},{3,11},{11,3},{4,12},{12,4},... | collective-permute-start | bytes 3538952 | tf_op jit(solution)/shard_map/ppermute | solution.py:55
  149.6 71.1 %collective-permute-start.23 = (bf16[3,288,384]{2,1,0:T(8,128)(2,1)}, bf16[3,288,384]{2,1,0:T(8,128)(2,1)}, u32[]{:S(2)}, u32[]{:S(2)}) collective-permute-start(bf16[3,288,384]{2,1,0:T(8,128)(2,1)} %get-tuple-element.94.refs_7_.refs_9_), channel_id=1, source_target_pairs={{0,4},{4,0},{1,5},{5,1},{2,6},{6,2},{3,7},{7,3},{8,12},{12,8},{9,1... | collective-permute-start | bytes 1990664 | tf_op jit(solution)/shard_map/ppermute | solution.py:976
  156.1 37.5 %collective-permute-start.26 = (bf16[3,288,384]{2,1,0:T(8,128)(2,1)}, bf16[3,288,384]{2,1,0:T(8,128)(2,1)S(1)}, u32[]{:S(2)}, u32[]{:S(2)}) collective-permute-start(bf16[3,288,384]{2,1,0:T(8,128)(2,1)} %collective-permute-done.16.refs_7_.refs_10_), channel_id=1, source_target_pairs={{0,16},{16,0},{1,17},{17,1},{2,18},{18,2},{3,19},{19,3},{4,20},{20... | collective-permute-start | bytes 1990664 | tf_op jit(solution)/shard_map/ppermute | solution.py:980
  162.4 58.4 %collective-permute-start.25 = (bf16[3,288,384]{2,1,0:T(8,128)(2,1)}, bf16[3,288,384]{2,1,0:T(8,128)(2,1)S(1)}, u32[]{:S(2)}, u32[]{:S(2)}) collective-permute-start(bf16[3,288,384]{2,1,0:T(8,128)(2,1)} %collective-permute-done.24.refs_11_), channel_id=1, source_target_pairs={{0,4},{4,0},{1,5},{5,1},{2,6},{6,2},{3,7},{7,3},{8,12},{12,8},{9,1... | collective-permute-start | bytes 1990664 | tf_op jit(solution)/shard_map/ppermute | solution.py:981
  191.4 27.3 %collective-permute-start.27 = (bf16[2,576,384]{2,1,0:T(8,128)(2,1)}, bf16[2,576,384]{2,1,0:T(8,128)(2,1)S(1)}, u32[]{:S(2)}, u32[]{:S(2)}) collective-permute-start(bf16[2,576,384]{2,1,0:T(8,128)(2,1)} %get-tuple-element.105), channel_id=1, source_target_pairs={{0,4},{4,0},{1,5},{5,1},{2,6},{6,2},{3,7},{7,3},{8,12},{12,8},{9,1... | collective-permute-start | bytes 2654216 | tf_op jit(solution)/shard_map/ppermute | solution.py:291
  191.5 27.3 %collective-permute-start.28 = (bf16[2,576,384]{2,1,0:T(8,128)(2,1)}, bf16[2,576,384]{2,1,0:T(8,128)(2,1)S(1)}, u32[]{:S(2)}, u32[]{:S(2)}) collective-permute-start(bf16[2,576,384]{2,1,0:T(8,128)(2,1)} %get-tuple-element.106), channel_id=1, source_target_pairs={{0,16},{16,0},{1,17},{17,1},{2,18},{18,2},{3,19},{19,3},{4,20},{20... | collective-permute-start | bytes 2654216 | tf_op jit(solution)/shard_map/ppermute | solution.py:291
  254.7 28.6 %collective-permute-start.34 = (bf16[2,576,384]{2,1,0:T(8,128)(2,1)}, bf16[2,576,384]{2,1,0:T(8,128)(2,1)}, u32[]{:S(2)}, u32[]{:S(2)}) collective-permute-start(bf16[2,576,384]{2,1,0:T(8,128)(2,1)} %get-tuple-element.116), channel_id=1, source_target_pairs={{0,4},{4,0},{1,5},{5,1},{2,6},{6,2},{3,7},{7,3},{8,12},{12,8},{9,1... | collective-permute-start | bytes 2654216 | tf_op jit(solution)/shard_map/ppermute | solution.py:291
  276.3 49.8 %reduce-scatter.7.cloned.1.call-start = ((), (), s32[]{:S(2)}) async-start(), calls=%async_computation.5 | async-start | bytes 1105920 | tf_op jit(solution)/shard_map/reduce_scatter | solution.py:321
  302.0 106.7 %all-gather.14.cloned.1.call-start = ((), (), s32[]{:S(2)}) async-start(), calls=%async_computation.9 | async-start | bytes 1990656 | tf_op jit(solution)/shard_map/all_gather | solution.py:325
  302.6 119.3 %all-gather.16.cloned.1.call-start = ((), (), s32[]{:S(2)}) async-start(), calls=%async_computation.10 | async-start | bytes 1990656 | tf_op jit(solution)/shard_map/all_gather | solution.py:325
  326.2 99.3 %reduce-scatter.11.cloned.1.call-start = ((), (), s32[]{:S(2)}) async-start(), calls=%async_computation.7 | async-start | bytes 1105920 | tf_op jit(solution)/shard_map/reduce_scatter | solution.py:321
  342.4 30.2 %collective-permute-start.40 = (bf16[2,192,1024]{2,1,0:T(8,128)(2,1)}, bf16[2,192,1024]{2,1,0:T(8,128)(2,1)}, u32[]{:S(2)}, u32[]{:S(2)}) collective-permute-start(bf16[2,192,1024]{2,1,0:T(8,128)(2,1)} %bitcast.138), channel_id=1, source_target_pairs={{4,0},{5,1},{6,2},{7,3},{12,8},{13,9},{14,10},{15,11},{20,16},{21,... | collective-permute-start | bytes 2359304 | tf_op jit(solution)/shard_map/ppermute | solution.py:1042
  382.7 26.1 %collective-permute-start.51 = (bf16[2,576,384]{2,1,0:T(8,128)(2,1)}, bf16[2,576,384]{2,1,0:T(8,128)(2,1)}, u32[]{:S(2)}, u32[]{:S(2)}) collective-permute-start(bf16[2,576,384]{2,1,0:T(8,128)(2,1)} %get-tuple-element.144), channel_id=1, source_target_pairs={{0,16},{16,0},{1,17},{17,1},{2,18},{18,2},{3,19},{19,3},{4,20},{20... | collective-permute-start | bytes 2654216 | tf_op jit(solution)/shard_map/ppermute | solution.py:291
  389.6 57.9 %reduce-scatter.9.cloned.1.call-start = ((), (), s32[]{:S(2)}) async-start(), calls=%async_computation.6 | async-start | bytes 1105920 | tf_op jit(solution)/shard_map/reduce_scatter | solution.py:321
  425.4 49.6 %all-gather.20.cloned.1.call-start = ((), (), s32[]{:S(2)}) async-start(), calls=%async_computation.12 | async-start | bytes 1990656 | tf_op jit(solution)/shard_map/all_gather | solution.py:325
  426.2 77.3 %all-gather.18.cloned.1.call-start = ((), (), s32[]{:S(2)}) async-start(), calls=%async_computation.11 | async-start | bytes 1990656 | tf_op jit(solution)/shard_map/all_gather | solution.py:325
  (85 other events, 1181.0 us)
Sparse Core Ops, SparseCore 0:
  61.4 39.3 all-gather.11
  276.4 23.1 reduce-scatter.4
  302.5 23.6 reduce-scatter.6
  327.9 25.6 all-gather.13
  355.2 32.2 all-gather.15
  390.3 28.2 reduce-scatter.10
  425.6 21.8 reduce-scatter.8
  449.4 25.6 all-gather.19
  477.0 26.5 all-gather.17

commit v3 on v2

--- a/solution.py
+++ b/solution.py
@@ -19,6 +19,8 @@
 CHUNKS = 3
 BLOCKS = 4
 GAIN_ROWS = 16
+FFN_ROWS = 512
+COST = 0.1
 
 low_type = jnp.bfloat16
 eps_norm = 1e-05
@@ -71,7 +73,9 @@
 
 
 def cost(flops, moved, special=0):
-    return pl.CostEstimate(flops=int(flops), bytes_accessed=int(moved), transcendentals=int(special))
+    return pl.CostEstimate(
+        flops=int(flops * COST), bytes_accessed=int(moved * COST), transcendentals=int(special * COST)
+    )
 
 
 def shape(dims, kind=low_type):
@@ -132,11 +136,13 @@
     @pl.when(step == steps - 1)
     def _():
         if piece_ref:
-            one, rest = piece_ref
-            size = one.shape[1]
+            one, two = piece_ref
+            size, cut = one.shape[1], rows // 2
             at = pl.ds(pl.multiple_of(info[1] * size, size), size)
-            one[...] = own_ref[0, :, at]
-            rest[...] = own_ref[1:, :, at]
+            one[:rows, :] = own_ref[0, :, at]
+            one[rows:, :] = own_ref[1, :cut, at]
+            two[:cut, :] = own_ref[1, cut:, at]
+            two[cut:, :] = own_ref[2, :, at]
 
 
 def pack_ffn(info, gate, up, down, tuned):
@@ -148,7 +154,7 @@
     part = packed // BLOCKS
     outs = [shape((CHUNKS, rows, packed))]
     if tuned:
-        outs += [shape((rows, part)), shape((CHUNKS - 1, rows, part))]
+        outs += [shape((rows + rows // 2, part))] * 2
     columns = pl.BlockSpec((rows, half), lambda z, info: (0, 2 * z + info[0]))
     return pl.pallas_call(
         pack_ffn_kernel,
@@ -188,7 +194,7 @@
     return copies
 
 
-def assemble(info, own, stacks, count):
+def assemble(info, own, stacks, count, after):
     rows, width = own.shape
     out = shape((BLOCKS, rows * count, width // BLOCKS))
 
@@ -197,40 +203,47 @@
             copy.wait()
 
     return pl.pallas_call(
-        kernel,
-        in_specs=[SCALARS] + [ANY] * (1 + len(stacks)),
+        ignoring(kernel, 2 + len(stacks), after),
+        in_specs=[SCALARS] + [ANY] * (1 + len(stacks) + len(after)),
         out_specs=pl.BlockSpec(),
         out_shape=out,
         scratch_shapes=[pltpu.SemaphoreType.DMA((BLOCKS * count,))],
         compiler_params=params(),
         cost_estimate=cost(0, rows * width * count * 4),
-    )(info, own, *stacks)
-
-
-def pick_kernel(info, all_ref, *refs):
-    outs, sems = refs[:-1], refs[-1]
-    count = all_ref.shape[0]
+    )(info, own, *stacks, *after)
+
+
+def pick_kernel(parts, info, *refs):
+    ins = refs[: -1 - len({p[0] for p in parts})]
+    outs, sems = refs[len(ins) : -1], refs[-1]
     copies = []
-    for c, out in enumerate(outs):
+    for out, source, start, stop, at in parts:
+        count = ins[source].shape[0]
         for k in range(1, count):
-            source = all_ref.at[lax.rem(info[2] + k, count), c]
-            copies.append(pltpu.make_async_copy(source, out.at[k - 1], sems.at[len(copies)]))
+            rows = ins[source].at[lax.rem(info[2] + k, count), start:stop]
+            target = outs[out].at[k - 1, at : at + stop - start]
+            copies.append(pltpu.make_async_copy(rows, target, sems.at[len(copies)]))
             copies[-1].start()
     for copy in copies:
         copy.wait()
 
 
-def pick(info, everyone):
-    count, chunks, rows, part = everyone.shape
-    return pl.pallas_call(
-        pick_kernel,
-        in_specs=[SCALARS, ANY],
-        out_specs=[pl.BlockSpec()] * chunks,
-        out_shape=[shape((count - 1, rows, part))] * chunks,
-        scratch_shapes=[pltpu.SemaphoreType.DMA((chunks * (count - 1),))],
-        compiler_params=params(),
-        cost_estimate=cost(0, count * chunks * rows * part * 4),
-    )(info, everyone)
+def pick(info, arrays, parts, rows):
+    count, _, part = arrays[0].shape
+    outs = [shape((count - 1, rows, part))] * len({p[0] for p in parts})
+
+    def kernel(*refs):
+        pick_kernel(parts, *refs)
+
+    return pl.pallas_call(
+        kernel,
+        in_specs=[SCALARS] + [ANY] * len(arrays),
+        out_specs=[pl.BlockSpec()] * len(outs),
+        out_shape=outs,
+        scratch_shapes=[pltpu.SemaphoreType.DMA((len(parts) * (count - 1),))],
+        compiler_params=params(),
+        cost_estimate=cost(0, len(outs) * count * rows * part * 4),
+    )(info, *arrays)
 
 
 def travel_z(piece, sizes):
@@ -242,15 +255,20 @@
     return full.reshape(full.shape[0], BLOCKS, -1).transpose(1, 0, 2)
 
 
-def send_out(info, packed, outs, sems):
+def send_out(info, packed, outs, way, sems):
     copies = []
 
     def begin(source, target):
         copies.append(pltpu.make_async_copy(source, target, sems.at[len(copies)]))
         copies[-1].start()
 
-    if len(outs) == 1:
+    if way == "whole":
         begin(packed, outs[0])
+    elif way == "z":
+        count, _, rows, _ = outs[0].shape
+        for z in range(count):
+            for b in range(BLOCKS):
+                begin(packed.at[b, z * rows : (z + 1) * rows], outs[0].at[z, b])
     else:
         keep_one, send_one, keep_two, send_two = outs
         cut = packed.shape[1] // 2
@@ -261,14 +279,66 @@
             begin(packed.at[at_y * 2 + 1 - x, :cut], send_one.at[i])
             begin(packed.at[y * 2 + at_x, cut:], keep_two.at[i])
             begin(packed.at[(1 - y) * 2 + at_x, cut:], send_two.at[i])
-    for copy in copies:
+    return copies
+
+
+def sent_shapes(rows, part, way):
+    if way == "xy":
+        return [shape((2, rows // 2, part))] * 4
+    if way == "z":
+        return [shape((BLOCKS, BLOCKS, rows // BLOCKS, part))]
+    return [shape((BLOCKS, rows, part))]
+
+
+def split_kernel(info, packed_ref, *refs):
+    for copy in send_out(info, packed_ref, refs[:-1], "xy", refs[-1]):
         copy.wait()
 
 
-def sent_shapes(rows, part, tuned):
-    if tuned:
-        return [shape((2, rows // 2, part))] * 4
-    return [shape((BLOCKS, rows, part))]
+def split(info, packed):
+    _, rows, part = packed.shape
+    return pl.pallas_call(
+        split_kernel,
+        in_specs=[SCALARS, pl.BlockSpec()],
+        out_specs=[ANY] * 4,
+        out_shape=sent_shapes(rows, part, "xy"),
+        scratch_shapes=[pltpu.SemaphoreType.DMA((8,))],
+        compiler_params=params(),
+        cost_estimate=cost(0, 4 * BLOCKS * rows * part),
+    )(info, packed)
+
+
+def sum_over(value, axis, count):
+    if count & (count - 1):
+        return lax.psum(value, axis)
+    step = 1
+    while step < count:
+        value = value + lax.ppermute(value, axis, [(i, i ^ step) for i in range(count)])
+        step *= 2
+    return value
+
+
+def add_low(kept, came):
+    return (kept.astype(jnp.float32) + came.astype(jnp.float32)).astype(low_type)
+
+
+def scatter_first(outs):
+    if len(outs) == 1:
+        return ()
+    return lax.ppermute(outs[1], "x", PAIR), lax.ppermute(outs[3], "y", PAIR)
+
+
+def scatter_sums(outs, came, last):
+    if len(outs) == 1:
+        return ()
+    came = lax.optimization_barrier((*came, *last))
+    return add_low(outs[0][1], came[0][1]), add_low(outs[2][1], came[1][1])
+
+
+def scatter_second(sums):
+    if len(sums) == 0:
+        return ()
+    return lax.ppermute(sums[0], "y", PAIR), lax.ppermute(sums[1], "x", PAIR)
 
 
 def sum_over(value, axis, count):
@@ -317,17 +387,69 @@
     return jnp.concatenate([one, two])
 
 
+def merge_kernel(*refs):
+    parts, out = refs[:6], refs[6]
+    cut = out.shape[0] // 2
+    for i in range(2):
+        kept, came, second = (ref[...].astype(jnp.float32) for ref in parts[3 * i : 3 * i + 3])
+        out[i * cut : (i + 1) * cut, :] = (kept[0] + came[0] + second).astype(low_type)
+
+
+def merge(outs, first, second):
+    cut, part = second[0].shape
+    half = pl.BlockSpec((1, cut, part), lambda i: (0, 0, 0))
+    whole = pl.BlockSpec((cut, part), lambda i: (0, 0))
+    return pl.pallas_call(
+        merge_kernel,
+        grid=(1,),
+        in_specs=[half, half, whole] * 2,
+        out_specs=pl.BlockSpec((2 * cut, part), lambda i: (0, 0)),
+        out_shape=shape((2 * cut, part)),
+        compiler_params=params(),
+        cost_estimate=cost(0, 16 * cut * part),
+    )(outs[0], first[0], second[0], outs[2], first[1], second[1])
+
+
+def scatter_mine(outs, first, second, last, sizes):
+    ny, nx, nz = sizes
+    if len(outs) == 1:
+        packed = outs[0]
+        total = packed.shape[1]
+        split = packed.transpose(1, 0, 2).reshape(total, ny * nx, -1).transpose(1, 0, 2)
+        return lax.psum_scatter(split, ("y", "x"), scatter_dimension=0, tiled=True)[0]
+    return merge(outs, first, lax.optimization_barrier((*second, *last))[: len(second)])
+
+
 def scatter_rows(mine):
     return lax.psum_scatter(mine, "z", scatter_dimension=0, tiled=True)
 
 
-def spread(mine, sizes):
-    everyone = lax.all_gather(mine, ("core", "y", "x"), axis=0)
-    both = everyone.reshape((2, sizes[0] * sizes[1]) + mine.shape)
+def spread(total, sizes):
     if sizes[0] * sizes[1] == BLOCKS:
-        return both
-    both = jnp.moveaxis(both, 1, -2).reshape((2,) + mine.shape[:2] + (BLOCKS, -1))
-    return jnp.moveaxis(both, -2, 1)
+        mine = [
+            total,
+            lax.ppermute(total, "x", PAIR),
+            lax.ppermute(total, "y", PAIR),
+            lax.ppermute(total, ("y", "x"), [(i, 3 - i) for i in range(4)]),
+        ]
+        return mine, [swap_core(value) for value in mine]
+    everyone = jnp.moveaxis(lax.all_gather(total, ("y", "x"), axis=0), 0, -2)
+    everyone = jnp.moveaxis(everyone.reshape(total.shape[:2] + (BLOCKS, -1)), -2, 0)
+    place = lax.axis_index("y") * sizes[1] + lax.axis_index("x")
+    mine = [
+        lax.dynamic_index_in_dim(everyone, (place % BLOCKS) ^ i, 0, False) for i in range(BLOCKS)
+    ]
+    return mine, [swap_core(value) for value in mine]
+
+
+def gather_all(total, sizes):
+    everyone = lax.all_gather(total, ("core", "y", "x"), axis=0)
+    count = sizes[0] * sizes[1]
+    if count == BLOCKS:
+        return (everyone,)
+    both = jnp.moveaxis(everyone.reshape((2, count) + total.shape), 1, -2)
+    both = jnp.moveaxis(both.reshape((2,) + total.shape[:2] + (BLOCKS, -1)), -2, 1)
+    return (both.reshape((2 * BLOCKS,) + both.shape[2:]),)
 
 
 def turn_heads(ref, value, cosine, sine, start):
@@ -602,144 +724,156 @@
     )(info, attended, came, weights, weights_other, tokens, gain, *after)
 
 
-def ffn_kernel(chunk, pieces, held, after, info, *refs):
-    x_refs, c_refs, xt_refs, ct_refs, w_ref = refs[0:2], refs[2:4], refs[4:6], refs[6:8], refs[8]
-    others = refs[9 : 9 + pieces]
-    refs = refs[9 + pieces :]
-    sums = refs[: 2 * held]
-    refs = refs[2 * held + after :]
-    result_ref, grad_ref, outs = refs[0], refs[1], refs[2:-9]
-    gate_s, up_s, down_s, hidden_s, dgate_s, dup_s, packed_s, sems, place_sems = refs[-9:]
-    step = pl.program_id(0)
-    size = result_ref.shape[0]
-    half = 2
-    block = gate_s.shape[1]
-    part = packed_s.shape[2]
+def ffn_kernel(tuned, ways, info, *refs):
+    xs, cs, xts, cts, w_ref, refs = refs[0:2], refs[2:4], refs[4:6], refs[6:8], refs[8], refs[9:]
+    stacks = [()] * CHUNKS
+    if tuned:
+        stacks, refs = [refs[4 * j : 4 * j + 4] for j in range(CHUNKS)], refs[4 * CHUNKS :]
+    totals, outs, scratch = refs[:4], list(refs[4:-17]), refs[-17:]
+    (
+        x_s, c_s, xt_s, ct_s, result_s, grad_s, result_low, grad_low, land_s, gate_s, up_s, down_s,
+        hidden_s, dgate_s, dup_s, packed_s, sems,
+    ) = scratch
+    rows = xs[0].shape[0]
+    size = FFN_ROWS
+    block, part = gate_s.shape[1], packed_s.shape[3]
     width = gate_s.shape[0]
-    lane = block // BLOCKS
-    rows = width // BLOCKS
-
-    @pl.when(step == 0)
-    def _():
-        if pieces:
-            copies = place_pieces(
-                info, BLOCKS, w_ref.at[chunk], others, chunk > 0, packed_s, place_sems
-            )
-        else:
-            copies = [pltpu.make_async_copy(w_ref, packed_s, place_sems.at[0])]
-            copies[0].start()
-        for copy in copies:
+    lane, turned = block // BLOCKS, width // BLOCKS
+
+    def begin(source, target, sem):
+        copy = pltpu.make_async_copy(source, target, sem)
+        copy.start()
+        return copy
+
+    def weights_in(j):
+        target = land_s.at[j % 2]
+        if tuned:
+            return place_pieces(info, BLOCKS, w_ref.at[j], stacks[j], True, target, sems.at[j])
+        return [begin(w_ref.at[j], target, sems.at[j, 0])]
+
+    coming = weights_in(0)
+    there = [begin(ref, x_s.at[i * rows : (i + 1) * rows], sems.at[3, i]) for i, ref in enumerate(xs)]
+    there += [begin(ref, c_s.at[i * rows : (i + 1) * rows], sems.at[3, 2 + i]) for i, ref in enumerate(cs)]
+    across = [begin(ref, xt_s.at[:, i * rows : (i + 1) * rows], sems.at[3, 4 + i]) for i, ref in enumerate(xts)]
+    across += [begin(ref, ct_s.at[:, i * rows : (i + 1) * rows], sems.at[3, 6 + i]) for i, ref in enumerate(cts)]
+    going = [[] for _ in range(CHUNKS + 1)]
+    for j in range(CHUNKS):
+        for copy in coming:
             copy.wait()
-        gate_s[:, :part] = packed_s[0]
-        gate_s[:, part:] = packed_s[1, :, : block - part]
-        up_s[:, : 2 * part - block] = packed_s[1, :, block - part :]
-        up_s[:, 2 * part - block :] = packed_s[2, :, : 2 * block - 2 * part]
+        land = land_s.at[j % 2]
+        gate_s[:, :part] = land[0]
+        gate_s[:, part:] = land[1, :, : block - part]
+        up_s[:, : 2 * part - block] = land[1, :, block - part :]
+        up_s[:, 2 * part - block :] = land[2, :, : 2 * block - 2 * part]
         for q in range(BLOCKS):
             for z in range(BLOCKS):
                 column = 2 * block + q * lane
                 b, at = column // part, column % part
-                down_s[q * rows : (q + 1) * rows, z * lane : (z + 1) * lane] = packed_s[
-                    b, z * rows : (z + 1) * rows, at : at + lane
+                down_s[q * turned : (q + 1) * turned, z * lane : (z + 1) * lane] = land[
+                    b, z * turned : (z + 1) * turned, at : at + lane
                 ]
-
-    @pl.when(step < 2 * half)
-    def _():
-        mine = step < half
-        x = jnp.where(mine, x_refs[0][...], x_refs[1][...])
-        c = jnp.where(mine, c_refs[0][...], c_refs[1][...])
-        gate = dot(x, gate_s[...])
-        upward = dot(x, up_s[...])
-        grad_hidden = dot(c, down_s[...])
-        sigmoid = 1.0 / (1.0 + jnp.exp(-gate))
-        silu = gate * sigmoid
-        hidden = (silu * upward).astype(low_type)
-        grad_gate = (grad_hidden * upward * sigmoid * (1.0 + gate * (1.0 - sigmoid))).astype(low_type)
-        grad_up = (grad_hidden * silu).astype(low_type)
-        at = pl.ds(pl.multiple_of(step * size, size), size)
-        hidden_s[at, :] = hidden
-        dgate_s[at, :] = grad_gate
-        dup_s[at, :] = grad_up
-        result = dot(hidden, down_s[...], (1, 1))
-        grad = dot(grad_gate, gate_s[...], (1, 1)) + dot(grad_up, up_s[...], (1, 1))
-        if held:
-            result = result + sums[0][...]
-            grad = grad + sums[1][...]
-        result_ref[...] = result
-        grad_ref[...] = grad
-
-    @pl.when(step >= 2 * half)
-    def _():
-        q = step - 2 * half
-        cut = half * size
-        at = pl.ds(pl.multiple_of(q * rows, rows), rows)
-        gate = dot(xt_refs[0][...], dgate_s[:cut]) + dot(xt_refs[1][...], dgate_s[cut:])
-        up = dot(xt_refs[0][...], dup_s[:cut]) + dot(xt_refs[1][...], dup_s[cut:])
-        down = dot(ct_refs[0][...], hidden_s[:cut]) + dot(ct_refs[1][...], hidden_s[cut:])
-        gate, up, down = gate.astype(low_type), up.astype(low_type), down.astype(low_type)
-        packed_s[0, at, :] = gate[:, :part]
-        packed_s[1, at, : block - part] = gate[:, part:]
-        packed_s[1, at, block - part :] = up[:, : 2 * part - block]
-        packed_s[2, at, : 2 * block - 2 * part] = up[:, 2 * part - block :]
-        column = 2 * block + q * lane
-        b = lax.div(column, part)
-        there = pl.ds(pl.multiple_of(lax.rem(column, part), lane), lane)
-        for z in range(BLOCKS):
-            packed_s[b, z * rows : (z + 1) * rows, there] = down[:, z * lane : (z + 1) * lane]
-
-    @pl.when(step == pl.num_programs(0) - 1)
-    def _():
-        send_out(info, packed_s, outs, sems)
-
-
-def ffn_chunk(chunk, info, xs, cs, xts, cts, weights, pieces, sums, after, tuned):
+        coming = weights_in(j + 1) if j + 1 < CHUNKS else []
+        if j == 0:
+            for copy in there:
+                copy.wait()
+
+        def forward(t, _, j=j):
+            at = pl.ds(pl.multiple_of(t * size, size), size)
+            x, c = x_s[at, :], c_s[at, :]
+            gate = dot(x, gate_s[...])
+            upward = dot(x, up_s[...])
+            grad_hidden = dot(c, down_s[...])
+            sigmoid = 1.0 / (1.0 + jnp.exp(-gate))
+            silu = gate * sigmoid
+            hidden = (silu * upward).astype(low_type)
+            grad_gate = grad_hidden * upward * sigmoid * (1.0 + gate * (1.0 - sigmoid))
+            grad_gate = grad_gate.astype(low_type)
+            grad_up = (grad_hidden * silu).astype(low_type)
+            hidden_s[at, :], dgate_s[at, :], dup_s[at, :] = hidden, grad_gate, grad_up
+            result = dot(hidden, down_s[...], (1, 1))
+            grad = dot(grad_gate, gate_s[...], (1, 1)) + dot(grad_up, up_s[...], (1, 1))
+            if j > 0:
+                result, grad = result + result_s[at, :], grad + grad_s[at, :]
+            result_s[at, :], grad_s[at, :] = result, grad
+            return 0
+
+        lax.fori_loop(0, 2 * rows // size, forward, 0)
+        if j == 0:
+            for copy in across:
+                copy.wait()
+        if j == CHUNKS - 1:
+            result_low[...] = result_s[rows:, :].astype(low_type)
+            grad_low[...] = grad_s[rows:, :].astype(low_type)
+            sources = (result_s.at[:rows], grad_s.at[:rows], result_low, grad_low)
+            going[CHUNKS] = [begin(s, t, sems.at[3, 8 + i]) for i, (s, t) in enumerate(zip(sources, totals))]
+        if j >= 2:
+            for copy in going[j - 2]:
+                copy.wait()
+        packed = packed_s.at[j % 2]
+
+        def backward(q, _, packed=packed):
+            at = pl.ds(pl.multiple_of(q * turned, turned), turned)
+            xt = xt_s[at, :]
+            gate = dot(xt, dgate_s[...]).astype(low_type)
+            up = dot(xt, dup_s[...]).astype(low_type)
+            down = dot(ct_s[at, :], hidden_s[...]).astype(low_type)
+            packed[0, at, :] = gate[:, :part]
+            packed[1, at, : block - part] = gate[:, part:]
+            packed[1, at, block - part :] = up[:, : 2 * part - block]
+            packed[2, at, : 2 * block - 2 * part] = up[:, 2 * part - block :]
+            column = 2 * block + q * lane
+            b = lax.div(column, part)
+            place = pl.ds(pl.multiple_of(lax.rem(column, part), lane), lane)
+            for z in range(BLOCKS):
+                packed[b, z * turned : (z + 1) * turned, place] = down[:, z * lane : (z + 1) * lane]
+            return 0
+
+        lax.fori_loop(0, BLOCKS, backward, 0)
+        count = 4 if ways[j] == "xy" else 1
+        going[j] = send_out(info, packed, outs[:count], ways[j], sems.at[4 + j])
+        outs = outs[count:]
+    for copy in going[CHUNKS - 2] + going[CHUNKS - 1] + going[CHUNKS]:
+        copy.wait()
+
+
+def feed_forward(info, xs, cs, xts, cts, weights, pieces, ways, tuned, after):
     rows, width = xs[0].shape
-    size = rows // 2
-    part = weights.shape[2] // (BLOCKS if tuned else 1)
+    part = weights.shape[2] // BLOCKS if tuned else weights.shape[3]
     block = BLOCKS * part // 3
-    turned = width // BLOCKS
-
-    def first(i):
-        return (jnp.minimum(i, 1), 0)
-
-    def second(i):
-        return (jnp.clip(i - 2, 0, 1), 0)
-
-    def either(i):
-        return (jnp.minimum(i, 3), 0)
-
-    def later(i):
-        return (jnp.maximum(i - 4, 0), 0)
-
-    token = [pl.BlockSpec((size, width), first), pl.BlockSpec((size, width), second)]
-    across = [pl.BlockSpec((turned, rows), later)] * 2
-    total = [pl.BlockSpec((size, width), either)] * 2
-    held = len(sums) > 0
-    sent = sent_shapes(width, part, tuned)
+    sent = [sent_shapes(width, part, way) for way in ways]
+    given = sum((list(p) for p in pieces), [])
+    totals = [shape((rows, width), jnp.float32)] * 2 + [shape((rows, width))] * 2
 
     def kernel(info, *refs):
-        ffn_kernel(chunk, len(pieces), held, len(after), info, *refs)
-
-    return pl.pallas_call(
-        kernel,
-        grid=(8,),
-        in_specs=[SCALARS] + token + token + across + across + [ANY] * (1 + len(pieces))
-        + (total if held else []) + [ANY] * len(after),
-        out_specs=total + [ANY] * len(sent),
-        out_shape=[shape((2 * rows, width), jnp.float32)] * 2 + sent,
+        ffn_kernel(tuned, ways, info, *refs)
+
+    whole = pltpu.VMEM((2 * rows, width), low_type)
+    turned = pltpu.VMEM((width, 2 * rows), low_type)
+    total = pltpu.VMEM((2 * rows, width), jnp.float32)
+    low = pltpu.VMEM((rows, width), low_type)
+    packed = pltpu.VMEM((2, BLOCKS, width, part), low_type)
+    matrix = pltpu.VMEM((width, block), low_type)
+    tokens = pltpu.VMEM((2 * rows, block), low_type)
+    outs = pl.pallas_call(
+        ignoring(kernel, 10 + len(given), after),
+        in_specs=[SCALARS] + [ANY] * (9 + len(given) + len(after)),
+        out_specs=[ANY] * (4 + sum(len(s) for s in sent)),
+        out_shape=totals + sum(sent, []),
         scratch_shapes=[
-            pltpu.VMEM((width, block), low_type),
-            pltpu.VMEM((width, block), low_type),
-            pltpu.VMEM((width, block), low_type),
-            pltpu.VMEM((2 * rows, block), low_type),
-            pltpu.VMEM((2 * rows, block), low_type),
-            pltpu.VMEM((2 * rows, block), low_type),
-            pltpu.VMEM((BLOCKS, width, part), low_type),
-            pltpu.SemaphoreType.DMA((8,)),
-            pltpu.SemaphoreType.DMA((BLOCKS * BLOCKS,)),
+            whole, whole, turned, turned, total, total, low, low, packed, matrix, matrix, matrix,
+            tokens, tokens, tokens, packed, pltpu.SemaphoreType.DMA((4 + CHUNKS, 16)),
         ],
         compiler_params=params(),
-        cost_estimate=cost(18 * 2 * rows * width * block, 40 << 20, 2 * rows * block),
-    )(info, *xs, *cs, *xts, *cts, weights, *pieces, *sums, *after)
+        cost_estimate=cost(
+            36 * rows * width * block * CHUNKS, 40 << 20, 2 * rows * block * CHUNKS
+        ),
+    )(info, *xs, *cs, *xts, *cts, weights, *given, *after)
+    totals, outs = outs[:4], outs[4:]
+    groups = []
+    for shapes in sent:
+        groups.append(outs[: len(shapes)])
+        outs = outs[len(shapes) :]
+    return totals, groups
 
 
 def branch_kernel(g_ref, g_other_ref, w_ref, attended_ref, grad_ref, delta_ref, rows_ref):
@@ -797,13 +931,14 @@
     )
     packed_s[2] = jnp.concatenate([last, out[:, : part - hk]], axis=1)
     packed_s[3] = out[:, part - hk :]
-    send_out(info, packed_s, outs, sems)
+    for copy in send_out(info, packed_s, outs, "xy" if len(outs) > 1 else "whole", sems):
+        copy.wait()
 
 
 def attn_grads(info, grad_query, grad_kv, came, cosine, sine, normed, mine, other, after, tuned):
     width, both = normed.shape
     part = (2 * HALF_QUERY + 2 * HALF_KEY) // BLOCKS
-    sent = sent_shapes(width, part, tuned)
+    sent = sent_shapes(width, part, "xy" if tuned else "whole")
     return pl.pallas_call(
         ignoring(attn_grad_kernel, 9, after),
         in_specs=[SCALARS] + [pl.BlockSpec()] * 8 + [ANY] * len(after),
@@ -842,41 +977,53 @@
     )(d, weights, *after)
 
 
-def unpack_attn_kernel(all_ref, q_ref, k_ref, v_ref, o_ref):
-    hq, hk = HALF_QUERY, HALF_KEY
-    both = [
-        jnp.concatenate([all_ref[h, b, 0] for b in range(BLOCKS)], axis=1).astype(jnp.float32)
-        for h in range(2)
-    ]
+def halves(info, refs, chunk):
+    mine, other = refs[:BLOCKS], refs[BLOCKS:]
+    place = lax.rem(info[1], BLOCKS)
+
+    def ordered(values):
+        for bit in (1, 2):
+            flip = lax.rem(lax.div(place, bit), 2) == 1
+            values = [jnp.where(flip, values[b ^ bit], values[b]) for b in range(BLOCKS)]
+        return jnp.concatenate(values, axis=1)
+
+    mine = ordered([ref[chunk] for ref in mine])
+    other = ordered([ref[chunk] for ref in other])
+    low = info[0] == 0
+    return jnp.where(low, mine, other), jnp.where(low, other, mine)
+
+
+def unpack_attn_kernel(info, *refs):
+    refs, outs = refs[: 2 * BLOCKS], refs[2 * BLOCKS :]
+    both = [value.astype(jnp.float32) for value in halves(info, refs, 0)]
     start = 0
-    for ref, size in ((q_ref, hq), (k_ref, hk), (v_ref, hk), (o_ref, hq)):
+    for ref, size in zip(outs, (HALF_QUERY, HALF_KEY, HALF_KEY, HALF_QUERY)):
         ref[...] = jnp.concatenate([v[:, start : start + size] for v in both], axis=1)
         start += size
 
 
-def unpack_attn(everyone):
-    rows = everyone.shape[3]
+def unpack_attn(info, mine, other):
+    rows = mine[0].shape[1]
     return pl.pallas_call(
         unpack_attn_kernel,
-        in_specs=[pl.BlockSpec()],
+        in_specs=[SCALARS] + [pl.BlockSpec()] * (2 * BLOCKS),
         out_specs=[pl.BlockSpec()] * 4,
         out_shape=[
             shape((rows, 2 * n), jnp.float32) for n in (HALF_QUERY, HALF_KEY, HALF_KEY, HALF_QUERY)
         ],
         compiler_params=params(),
         cost_estimate=cost(0, 6 << 20),
-    )(everyone)
-
-
-def unpack_ffn_kernel(*refs):
-    all_refs, (gate_ref, up_ref, down_ref) = refs[:CHUNKS], refs[CHUNKS:]
-    rows, part = all_refs[0].shape[3], all_refs[0].shape[4]
+    )(info, *mine, *other)
+
+
+def unpack_ffn_kernel(all_ref, gate_ref, up_ref, down_ref):
+    part = all_ref.shape[3]
     block = BLOCKS * part // 3
     lane = block // BLOCKS
     half = CHUNKS * lane
     for h in range(2):
         for c in range(CHUNKS):
-            value = jnp.concatenate([all_refs[c][h, b, 0] for b in range(BLOCKS)], axis=1)
+            value = jnp.concatenate([all_ref[h * BLOCKS + b, c] for b in range(BLOCKS)], axis=1)
             value = value.astype(jnp.float32)
             for z in range(BLOCKS):
                 at = z * 2 * half + h * half + c * lane
@@ -889,12 +1036,12 @@
             down_ref[h * half + c * lane : h * half + (c + 1) * lane, :] = down.T
 
 
-def unpack_ffn(everyone):
-    rows, part = everyone[0].shape[3:]
+def unpack_ffn(info, everyone):
+    rows, part = everyone.shape[2:]
     lane = part // 3
     return pl.pallas_call(
         unpack_ffn_kernel,
-        in_specs=[pl.BlockSpec()] * CHUNKS,
+        in_specs=[pl.BlockSpec()],
         out_specs=[pl.BlockSpec()] * 3,
         out_shape=[
             shape((rows, 2 * BLOCKS * CHUNKS * lane), jnp.float32),
@@ -903,7 +1050,7 @@
         ],
         compiler_params=params(),
         cost_estimate=cost(0, 16 << 20),
-    )(*everyone)
+    )(everyone)
 
 
 def shards(sizes, *arrays):
@@ -925,33 +1072,7 @@
         info, (w_query, key_matrix, value_matrix, w_out), gains, tuned
     )
     ffn_own, *ffn_piece = pack_ffn(info, w_gate, w_up, w_down, tuned)
-    if tuned:
-        slots = travel_z(attn_piece[0], sizes)
-        stack = jnp.stack([s[:own_rows] for s in slots])
-        ffn_slots = travel_z(behind(ffn_piece[0], (stack,)), sizes)
-        ffn_stacks = [jnp.stack(ffn_slots)]
-        rest = lax.all_gather(behind(ffn_piece[1], ffn_slots), "z", axis=0)
-        ffn_stacks += pick(info, rest)
-        stacks = (
-            stack,
-            lax.ppermute(stack, "x", PAIR),
-            lax.ppermute(stack, "y", PAIR),
-            lax.ppermute(stack, ("y", "x"), [(i, 3 - i) for i in range(4)]),
-        )
-        weights = assemble(info, attn_own, stacks, nz)
-        ffn_weights = [ffn_own] * CHUNKS
-        gains = [gains.astype(low_type)] + [s[own_rows : own_rows + 2, :own_rows] for s in slots]
-        gains = jnp.stack(gains[::-1] + gains[::-1])
-        gains = lax.dynamic_slice_in_dim(gains, nz - 1 - lax.axis_index("z"), nz, 0)
-        gains = gains.transpose(1, 0, 2).reshape(2, width)
-    else:
-        weights = gather_whole(attn_own)
-        ffn_pieces = [()] * CHUNKS
-        before_attend = before_out = ()
-        ffn_weights = [gather_whole(ffn_own[c]) for c in range(CHUNKS)]
-        gains = lax.all_gather(gains.astype(low_type), "z", axis=1, tiled=True)
-    weights_other = swap_core(weights[2:])
-
+    ids, tokens_sent, cotangent_sent, _ = lax.optimization_barrier((ids, tokens, cotangent, ffn_own))
     all_ids = lax.all_gather(ids, "x", axis=0, tiled=True)
     first = jnp.sum((all_ids[:, None] < ids[None, :]).astype(jnp.int32), axis=0)
     firsts = jnp.concatenate([first[None], swap_core(first[None])])
@@ -964,25 +1085,61 @@
     info = jnp.concatenate([info, starts.reshape(-1)])
     firsts = firsts[:, None, :]
 
+    tokens_other, cotangent_other = swap_core(tokens_sent), swap_core(cotangent_sent)
+    cotangent_turned = cotangent_sent.T
+
+    if tuned:
+        cut = own_rows // 2
+        slots = travel_z(attn_piece[0], sizes)
+        stack = jnp.stack([s[:own_rows] for s in slots])
+        parts = [lax.all_gather(behind(piece, (stack,)), "z", axis=0) for piece in ffn_piece]
+        ffn_stacks = list(pick(info, parts[:1], ((0, 0, 0, own_rows, 0),), own_rows))
+        ffn_stacks += pick(
+            info,
+            parts,
+            ((0, 0, own_rows, own_rows + cut, 0), (0, 1, 0, cut, cut), (1, 1, cut, cut + own_rows, 0)),
+            own_rows,
+        )
+        stack = behind(stack, (cosine, firsts, tokens_other, cotangent_turned, cotangent_other))
+        stacks = (
+            stack,
+            lax.ppermute(stack, "x", PAIR),
+            lax.ppermute(stack, "y", PAIR),
+            lax.ppermute(stack, ("y", "x"), [(i, 3 - i) for i in range(4)]),
+        )
+        weights = assemble(info, attn_own, stacks, nz, ffn_stacks[:1])
+        ffn_weights = ffn_own
+        gains = [gains.astype(low_type)] + [s[own_rows : own_rows + 2, :own_rows] for s in slots]
+        gains = jnp.stack(gains[::-1] + gains[::-1])
+        gains = lax.dynamic_slice_in_dim(gains, nz - 1 - lax.axis_index("z"), nz, 0)
+        gains = gains.transpose(1, 0, 2).reshape(2, width)
+    else:
+        weights = gather_whole(attn_own)
+        ffn_pieces = [()] * CHUNKS
+        before_attend = before_out = ()
+        ffn_weights = jnp.stack([gather_whole(ffn_own[c]) for c in range(CHUNKS)])
+        gains = lax.all_gather(gains.astype(low_type), "z", axis=1, tiled=True)
     gain_one, gain_two = gains[:1].astype(jnp.float32), gains[1:].astype(jnp.float32)
 
-    turned = cotangent.T
-    cs, cts = (cotangent, swap_core(cotangent)), (turned, swap_core(turned))
+    cs = (cotangent, cotangent_other)
+    cts = (cotangent_turned, swap_core(cotangent_turned))
 
     normed, query, keyvalue = project(
-        tokens, swap_core(tokens), gain_one, weights, cosine, sine
-    )
+        tokens, tokens_other, gain_one, weights, cosine, sine
+    )
+    weights_other = swap_core(behind(weights, (keyvalue,))[2:])
     if tuned:
-        by_x = [lax.ppermute(s, "x", PAIR) for s in ffn_stacks]
-        by_y = [lax.ppermute(s, "y", PAIR) for s in ffn_stacks]
+        first_x, first_y = (lax.ppermute(ffn_stacks[0], axis, PAIR) for axis in ("x", "y"))
+        past = lax.ppermute(behind(keyvalue, (first_x, first_y)), "x", [(0, 1)])[None]
+        by_x = [first_x] + [lax.ppermute(s, "x", PAIR) for s in ffn_stacks[1:]]
+        by_y = [first_y] + [lax.ppermute(s, "y", PAIR) for s in ffn_stacks[1:]]
         far = [
             lax.ppermute(by_x[0], "y", PAIR),
             lax.ppermute(by_x[1], "y", PAIR),
             lax.ppermute(by_y[2], "x", PAIR),
         ]
         ffn_pieces = list(zip(ffn_stacks, by_x, by_y, far))
-        past = lax.ppermute(behind(keyvalue, (by_x[0],)), "x", [(0, 1)])[None]
-        before_attend = (by_y[0], *ffn_stacks[1:])
+        before_attend = ffn_stacks[1:]
         before_out = (by_x[1], by_y[1], far[0])
     else:
         past = lax.all_gather(keyvalue, "x", axis=0)
@@ -993,58 +1150,49 @@
     )
 
     xs, xts = (normed_two, swap_core(normed_two)), (normed_turned, swap_core(normed_turned))
-    sums, ready = (), ()
-    sent, first, send, second, mine_ffn = ([None] * (CHUNKS + 1) for _ in range(5))
-    for c in range(CHUNKS):
-        *sums, = ffn_chunk(
-            c, info, xs, cs, xts, cts, ffn_weights[c], ffn_pieces[c], sums, ready, tuned
-        )
-        sums, sent[c] = sums[:2], sums[2:]
-        first[c] = scatter_first(sent[c])
-        if c >= 1:
-            ready = send[c - 1] = scatter_sums(sent[c - 1], first[c - 1], sums[:1])
-            second[c - 1] = scatter_second(send[c - 1])
-        if c >= 2:
-            mine_ffn[c - 2] = scatter_mine(sent[c - 2], first[c - 2], second[c - 2], sums[:1], sizes)
-    result, grad_normed_two = sums
-
-    def pair_sum(value):
-        return value[:rows] + swap_core(value[rows:].astype(low_type)).astype(jnp.float32)
-
-    grad_normed_two = pair_sum(grad_normed_two)
+    sent, first, send, second, reduced = ([None] * (CHUNKS + 1) for _ in range(5))
+    ways = ["xy", "xy", "z"] if tuned else ["whole"] * CHUNKS
+    (result, grad_normed_two, result_other, grad_other), sent[:3] = feed_forward(
+        info, xs, cs, xts, cts, ffn_weights, ffn_pieces, ways, tuned, ()
+    )
+    if tuned:
+        rows_two = lax.psum_scatter(sent[2][0], "z", scatter_dimension=0, tiled=True)[0]
+    first[0] = scatter_first(sent[0])
+
+    grad_normed_two = grad_normed_two + swap_core(grad_other).astype(jnp.float32)
+    result = result + swap_core(result_other).astype(jnp.float32)
     scale_two = norm_scale(middle)
     grad_gain_two = jnp.sum(grad_normed_two * middle * scale_two, axis=0)
     grad_middle = cotangent.astype(jnp.float32) + norm_back(
         grad_normed_two * gain_two, middle, scale_two
     )
     grad_branch = grad_middle.astype(low_type)
-    output = (middle + pair_sum(result)).astype(low_type)
+    output = (middle + result).astype(low_type)
 
     grad_other = swap_core(grad_branch)
     grad_attended, delta, grad_rows = branch(
-        grad_branch, grad_other, out_rows, attended, (mine_ffn[0], *send[1])
+        grad_branch, grad_other, out_rows, attended, ()
     )
     hq = HALF_QUERY
     mine = lax.dynamic_slice_in_dim(grad_rows, core * hq, hq, 1)
     other = swap_core(lax.dynamic_slice_in_dim(grad_rows, (1 - core) * hq, hq, 1))
-    last = (grad_attended,)
-    send[2] = scatter_sums(sent[2], first[2], last)
-    second[2] = scatter_second(send[2])
-    mine_ffn[1] = scatter_mine(sent[1], first[1], second[1], last, sizes)
+    send[0] = scatter_sums(sent[0], first[0], (grad_attended,))
+    second[0] = scatter_second(send[0])
+    first[1] = scatter_first([behind(value, send[0]) for value in sent[1]])
     grad_query, grad_kv, grad_past = attend_back(
         info, query, keyvalue, past, grad_attended, firsts, log_total, delta, size,
-        (*send[2], mine_ffn[1]),
-    )
-    mine_ffn[2] = scatter_mine(sent[2], first[2], second[2], (grad_past,), sizes)
-    ffn_sums = [scatter_rows(mine) for mine in mine_ffn[:CHUNKS]]
-    ffn_all = [spread(total[None], sizes) for total in ffn_sums]
+        send[0],
+    )
     if tuned:
-        came = lax.ppermute(grad_past[0], "x", [(1, 0)])
+        came = lax.ppermute(behind(grad_past[0], (*second[0], *first[1])), "x", [(1, 0)])
     else:
         came = lax.psum_scatter(grad_past, "x", scatter_dimension=0, tiled=True)[0]
+    reduced[0] = scatter_mine(sent[0], first[0], second[0], (grad_past,), sizes)
+    send[1] = scatter_sums(sent[1], first[1], (grad_past,))
+    second[1] = scatter_second(send[1])
     grad_projected, *attn_sent = attn_grads(
         info, grad_query, grad_kv, came, cosine, sine, normed, mine, other,
-        (ffn_sums[0], mine_ffn[2]), tuned,
+        (*second[1], reduced[0]) if tuned else (), tuned,
     )
     normed_mine, normed_other = normed_grad(grad_projected, weights, ())
     grad_normed = normed_mine + swap_core(normed_other).astype(jnp.float32)
@@ -1061,12 +1209,24 @@
     gain_grads = lax.dynamic_slice_in_dim(gain_grads, lax.axis_index("z") * own_rows, own_rows, 1)
 
     sent[3], first[3] = attn_sent, scatter_first(attn_sent)
-    send[3] = scatter_sums(attn_sent, first[3], (normed_mine, ffn_all[0]))
+    last = (normed_mine,)
+    send[3] = scatter_sums(sent[3], first[3], last)
     second[3] = scatter_second(send[3])
-    mine_attn = scatter_mine(attn_sent, first[3], second[3], (ffn_all[1],), sizes)
-    attn_sum = scatter_rows(mine_attn)
-    grad_w_gate, grad_w_up, grad_w_down = unpack_ffn(ffn_all)
-    attn_out = unpack_attn(spread(attn_sum[None], sizes))
+    reduced[1] = scatter_mine(sent[1], first[1], second[1], send[3][:1] or last, sizes)
+    if tuned:
+        sent[2] = split(info, behind(rows_two, (reduced[1],)))
+        first[2] = scatter_first(sent[2])
+        reduced[3] = scatter_mine(sent[3], first[3], second[3], sent[2][:1], sizes)
+        last = (reduced[3],)
+        send[2] = scatter_sums(sent[2], first[2], last)
+        second[2] = scatter_second(send[2])
+        reduced[2] = scatter_mine(sent[2], first[2], second[2], last, sizes)
+    else:
+        reduced[2] = scatter_rows(scatter_mine(sent[2], (), (), last, sizes))
+        reduced[3] = scatter_mine(sent[3], (), (), last, sizes)
+    attn_out = unpack_attn(info, *spread(scatter_rows(reduced[3])[None], sizes))
+    ffn_total = jnp.stack([scatter_rows(reduced[0]), scatter_rows(reduced[1]), reduced[2]])
+    grad_w_gate, grad_w_up, grad_w_down = unpack_ffn(info, *gather_all(ffn_total, sizes))
     return (
         output[None], grad_inputs[None], gain_grads[0], *attn_out, gain_grads[1], grad_w_gate,
         grad_w_up, grad_w_down,

time: 521 us -> 499 us (0.958)
  other arithmetic: 43 us -> 24.8 us
    ppermute x8, waiting for transfers between devices: 19.9 us -> 40.1 us  [scatter_second(): return (lax.ppermute(sums[0], 'y', PAIR), lax.ppermute(sums[1], 'x', PAIR))]
    reduce_scatter x4 -> x3, waiting for transfers between devices: 21.2 us -> 1 us  [scatter_rows(): return lax.psum_scatter(mine, 'z', scatter_dimension=0, tiled=True)]
    ppermute x8 -> x11, waiting for transfers between devices: 38.3 us -> 21.3 us  [the longest x1 6.52 us: shards(): lax.ppermute(behind(keyvalue, (first_x, first_y)), 'x', [(0, 1)])[None]]
    convert_element_type x15 -> x8, other arithmetic: 16 us -> 1.62 us  [add_low(): (kept.astype(jnp.float32) + came.astype(jnp.float32)).astype(low_type)]
    all_gather x5 -> x3, waiting for transfers between devices: 26.2 us -> 39.6 us  [the longest x2 21.2 us: shards(): lax.all_gather(behind(piece, (stack,)), 'z', axis=0)]
    ppermute x1, waiting for transfers between devices: 0.01 us -> 12.5 us  [shards(): lax.ppermute(by_y[2], 'x', PAIR)]
    ppermute x5, starting transfers between devices: 4.11 us -> 14.7 us  [sum_over(): lax.ppermute(value, axis, [(i, i ^ step) for i in range(count)])]
    ppermute x8, waiting for transfers between devices: 38.1 us -> 30.7 us  [scatter_first(): return (lax.ppermute(outs[1], 'x', PAIR), lax.ppermute(outs[3], 'y', PAIR))]
  transfers between devices with their start and end apart: 63 -> 65, of which waited for: 30 -> 35; matrix products, arithmetic and copies ran while one was open for 12% -> 9% of each run, Pallas kernels for 27% -> 22%
where the time goes in v3:
time: 499 us; the launch traced here: 490 us
  waiting for transfers between devices  179 us (36%)
  Pallas kernels  168 us (34%)
  starting transfers between devices  69.6 us (14%)
  local copies, waits for them, and re-layouts  28.3 us (6%)
  other arithmetic  24.8 us (5%)
  between operations  15.4 us (3%)
    pallas_call x1, Pallas kernels, feed_forward(): pl.pallas_call(ignoring(kernel, 10 + len(given), after), in_specs=[SCALAR...  47.8 us
    ppermute x8, waiting for transfers between devices, scatter_second(): return (lax.ppermute(sums[0], 'y', PAIR), lax.ppermute(sums[1], 'x', PAIR))  40.1 us
    ppermute x8, waiting for transfers between devices, scatter_first(): return (lax.ppermute(outs[1], 'x', PAIR), lax.ppermute(outs[3], 'y', PAIR))  30.7 us
    all_gather x2, waiting for transfers between devices, shards(): lax.all_gather(behind(piece, (stack,)), 'z', axis=0)  21.2 us
    all_gather x1, waiting for transfers between devices, gather_all(): everyone = lax.all_gather(total, ('core', 'y', 'x'), axis=0)  18.4 us
    pallas_call x1, Pallas kernels, attend_back(): pl.pallas_call(ignoring(attend_back_kernel, 8, after), grid=grid, in_spec...  18.3 us
    pallas_call x1, Pallas kernels, attend(): pl.pallas_call(ignoring(attend_kernel, 5, after), grid=grid, in_specs=[SC...  15.3 us
    ppermute x5, starting transfers between devices, sum_over(): lax.ppermute(value, axis, [(i, i ^ step) for i in range(count)])  14.7 us
  transfers between devices with their start and end apart: 65, of which 35 were waited for; matrix products, arithmetic and copies ran while one was open for 9% of the time, Pallas kernels for 22%

profile of v3, /device:TPU:0, one launch (start us, length us, event | category | flops | bytes accessed | tf_op | source)
XLA Modules:
  0.0 489.7 jit_solution(6004081440751559797)
XLA Ops:
  19.2 6.1 %shard_map.203 = (bf16[3,288,1536]{2,1,0:T(8,128)(2,1)}, bf16[432,384]{1,0:T(8,128)(2,1)}, bf16[432,384]{1,0:T(8,128)(2,1)}) custom-call(s32[4]{0:T(128)} %pad_add_fusion.2.info, f32[288,3072]{1,0:T(8,128)} %gate_ref.1, f32[288,3072]{1,0:T(8,128)} %up_ref.1, f32[768,1152]{1,0:T(8,128)} %down_ref.1), custom_call_target="tpu_custom_call" | custom-call | bytes 796262 | tf_op jit(solution)/shard_map/pallas_call | solution.py:159
  25.4 12.8 %collective-permute-done.3 = bf16[304,384]{1,0:T(8,128)(2,1)S(1)} collective-permute-done((bf16[304,384]{1,0:T(8,128)(2,1)}, bf16[304,384]{1,0:T(8,128)(2,1)S(1)}, u32[]{:S(2)}, u32[]{:S(2)}) %collective-permute-start.3) | collective-permute-done | bytes 233504 | tf_op jit(solution)/shard_map/ppermute | solution.py:250
  55.3 17.2 %all-gather.8.cloned.1.call-done = bf16[1728,384]{1,0:T(8,128)(2,1)} async-done(((bf16[432,384]{1,0:T(8,128)(2,1)}), bf16[1728,384]{1,0:T(8,128)(2,1)}) %all-gather.8.cloned.1.call-update) | async-done | bytes 1327120 | tf_op jit(solution)/shard_map/all_gather | solution.py:1095
  89.2 7.4 %shard_map.207 = (bf16[1152,1024]{1,0:T(8,128)(2,1)}, bf16[576,1024]{1,0:T(8,128)(2,1)}, bf16[2,192,1024]{2,1,0:T(8,128)(2,1)}) custom-call(bf16[512,1152]{1,0:T(8,128)(2,1)} %bitcast.76, bf16[512,1152]{1,0:T(8,128)(2,1)} %collective-permute-done.1.other_ref, f32[1,1152]{1,0:T(1,128)} %reshape.194.gain_ref, ...), custom_call_target="tpu_custom_call" | custom-call | flops 226492416 | bytes 1468006 | tf_op jit(solution)/shard_map/pallas_call | solution.py:487
  113.0 6.5 %collective-permute-done.11 = bf16[2,192,1024]{2,1,0:T(8,128)(2,1)} collective-permute-done((bf16[2,192,1024]{2,1,0:T(8,128)(2,1)}, bf16[2,192,1024]{2,1,0:T(8,128)(2,1)}, u32[]{:S(2)}, u32[]{:S(2)}) %collective-permute-start.11) | collective-permute-done | bytes 786464 | tf_op jit(solution)/shard_map/ppermute | solution.py:1133
  120.2 15.3 %shard_map.209 = (f32[576,1024]{1,0:T(8,128)}, f32[3,8,1024]{2,1,0:T(8,128)}) custom-call(s32[8]{0:T(128)} %concatenate.25.refs_0_.info, bf16[576,1024]{1,0:T(8,128)(2,1)} %get-tuple-element.101.refs_1_, bf16[2,192,1024]{2,1,0:T(8,128)(2,1)} %get-tuple-element.103.refs_2_, bf16[1,2,192,1024]{3,2,1,0:T(8,128)(2,1)} %bitcast.19.refs_3_, ...), custom_call_target="tpu_custom_call" | custom-call | flops 905969664 | bytes 838860 | tf_op jit(solution)/shard_map/pallas_call | solution.py:625
  142.6 9.4 %shard_map.210 = (f32[512,1152]{1,0:T(8,128)}, bf16[512,1152]{1,0:T(8,128)(2,1)}, bf16[1152,512]{1,0:T(8,128)(2,1)}, bf16[576,1152]{1,0:T(8,128)(2,1)}) custom-call(s32[8]{0:T(128)} %concatenate.25.refs_0_.info, f32[576,1024]{1,0:T(8,128)} %get-tuple-element.108.refs_1_.refs_3_, bf16[576,512]{1,0:T(8,128)(2,1)} %collective-permute-done.12.refs_2_, ...), custom_call_target="tpu_custom_call" | custom-call | flops 135895456 | bytes 1677721 | tf_op jit(solution)/shard_map/pallas_call | solution.py:698
  157.7 5.2 %collective-permute-start.23 = (bf16[3,288,384]{2,1,0:T(8,128)(2,1)}, bf16[3,288,384]{2,1,0:T(8,128)(2,1)}, u32[]{:S(2)}, u32[]{:S(2)}) collective-permute-start(bf16[3,288,384]{2,1,0:T(8,128)(2,1)} %collective-permute-done.22.refs_20_), channel_id=1, source_target_pairs={{0,4},{4,0},{1,5},{5,1},{2,6},{6,2},{3,7},{7,3},{8,12},{12,8},{9,1... | collective-permute-start | bytes 1990664 | tf_op jit(solution)/shard_map/ppermute | solution.py:1139
  166.7 6.3 %collective-permute-done.21.refs_19_ = bf16[3,288,384]{2,1,0:T(8,128)(2,1)} collective-permute-done((bf16[3,288,384]{2,1,0:T(8,128)(2,1)S(1)}, bf16[3,288,384]{2,1,0:T(8,128)(2,1)}, u32[]{:S(2)}, u32[]{:S(2)}) %collective-permute-start.21) | collective-permute-done | bytes 663584 | tf_op jit(solution)/shard_map/ppermute | solution.py:1134
  174.2 12.5 %collective-permute-done.23.refs_21_ = bf16[3,288,384]{2,1,0:T(8,128)(2,1)} collective-permute-done((bf16[3,288,384]{2,1,0:T(8,128)(2,1)}, bf16[3,288,384]{2,1,0:T(8,128)(2,1)}, u32[]{:S(2)}, u32[]{:S(2)}) %collective-permute-start.23) | collective-permute-done | bytes 663584 | tf_op jit(solution)/shard_map/ppermute | solution.py:1139
  187.8 47.8 %shard_map.211 = (f32[512,1152]{1,0:T(8,128)}, f32[512,1152]{1,0:T(8,128)}, bf16[512,1152]{1,0:T(8,128)(2,1)}, bf16[512,1152]{1,0:T(8,128)(2,1)}, bf16[2,576,384...) custom-call(s32[8]{0:T(128)} %concatenate.25.refs_0_.info, ...), custom_call_target="tpu_custom_call" | custom-call | flops 3261490688 | bytes 4194304 | tf_op jit(solution)/shard_map/pallas_call | solution.py:857
  249.8 7.3 %shard_map.212 = (bf16[576,1024]{1,0:T(8,128)(2,1)}, f32[3,8,1024]{2,1,0:T(8,128)}, bf16[576,1152]{1,0:T(8,128)(2,1)}) custom-call(bf16[512,1152]{1,0:T(8,128)(2,1)} %copy-done.9, bf16[512,1152]{1,0:T(8,128)(2,1)} %copy-done.30, bf16[576,1152]{1,0:T(8,128)(2,1)} %get-tuple-element.117.refs_2_, f32[576,1024]{1,0:T(8,128)} %get-tuple-element.108.refs_1_.refs_3_), custom_call_target="tpu_custom_call" | custom-call | flops 271790912 | bytes 1258291 | tf_op jit(solution)/shard_map/pallas_call | solution.py:899
  257.2 11.1 %collective-permute-done.27.refs_1_ = bf16[2,576,384]{2,1,0:T(8,128)(2,1)S(1)} collective-permute-done((bf16[2,576,384]{2,1,0:T(8,128)(2,1)}, bf16[2,576,384]{2,1,0:T(8,128)(2,1)S(1)}, u32[]{:S(2)}, u32[]{:S(2)}) %collective-permute-start.27) | collective-permute-done | bytes 884768 | tf_op jit(solution)/shard_map/ppermute | solution.py:361
  277.3 18.3 %shard_map.213 = (f32[576,1024]{1,0:T(8,128)}, f32[2,192,1024]{2,1,0:T(8,128)}, bf16[1,2,192,1024]{3,2,1,0:T(8,128)(2,1)}) custom-call(s32[8]{0:T(128)} %concatenate.25.refs_0_.info, bf16[576,1024]{1,0:T(8,128)(2,1)} %get-tuple-element.101.refs_1_, bf16[2,192,1024]{2,1,0:T(8,128)(2,1)} %get-tuple-element.103.refs_2_, ...), custom_call_target="tpu_custom_call" | custom-call | flops 1358954496 | bytes 1258291 | tf_op jit(solution)/shard_map/pallas_call | solution.py:646
  295.6 5.8 %collective-permute-done.30.refs_5_ = bf16[576,384]{1,0:T(8,128)(2,1)} collective-permute-done((bf16[576,384]{1,0:T(8,128)(2,1)S(1)}, bf16[576,384]{1,0:T(8,128)(2,1)}, u32[]{:S(2)}, u32[]{:S(2)}) %collective-permute-start.30) | collective-permute-done | bytes 442400 | tf_op jit(solution)/shard_map/ppermute | solution.py:374
  310.4 23.9 %collective-permute-done.36.refs_10_.refs_5_ = bf16[576,384]{1,0:T(8,128)(2,1)S(1)} collective-permute-done((bf16[576,384]{1,0:T(8,128)(2,1)S(1)}, bf16[576,384]{1,0:T(8,128)(2,1)S(1)}, u32[]{:S(2)}, u32[]{:S(2)}) %collective-permute-start.36) | collective-permute-done | bytes 442400 | tf_op jit(solution)/shard_map/ppermute | solution.py:374
  335.5 9.9 %shard_map.215 = (bf16[960,1024]{1,0:T(8,128)(2,1)}, bf16[2,576,384]{2,1,0:T(8,128)(2,1)}, bf16[2,576,384]{2,1,0:T(8,128)(2,1)}, bf16[2,576,384]{2,1,0:T(8,128)(2,1)}, bf16[2,576,384]{2,1,0:T(8,128)(2,1)}) custom-call(s32[8]{0:T(128)} %concatenate.25.refs_0_.info, f32[576,1024]{1,0:T(8,128)} %get-tuple-element.127.refs_1_, ...), custom_call_target="tpu_custom_call" | custom-call | flops 226492416 | bytes 2097152 | tf_op jit(solution)/shard_map/pallas_call | solution.py:942
  346.1 7.6 %shard_map.216 = (f32[512,1152]{1,0:T(8,128)}, bf16[512,1152]{1,0:T(8,128)(2,1)}) custom-call(bf16[960,1024]{1,0:T(8,128)(2,1)} %get-tuple-element.143.refs_0_, bf16[4,1152,384]{2,1,0:T(8,128)(2,1)} %shard_map.206.w_ref.refs_3_.refs_1_), custom_call_target="tpu_custom_call" | custom-call | flops 226492416 | bytes 943718 | tf_op jit(solution)/shard_map/pallas_call | solution.py:970
  353.7 11.3 %collective-permute-done.43.refs_1_ = bf16[2,576,384]{2,1,0:T(8,128)(2,1)S(1)} collective-permute-done((bf16[2,576,384]{2,1,0:T(8,128)(2,1)}, bf16[2,576,384]{2,1,0:T(8,128)(2,1)S(1)}, u32[]{:S(2)}, u32[]{:S(2)}) %collective-permute-start.43) | collective-permute-done | bytes 884768 | tf_op jit(solution)/shard_map/ppermute | solution.py:361
  372.8 5.1 %collective-permute-done.46.refs_5_ = bf16[576,384]{1,0:T(8,128)(2,1)S(1)} collective-permute-done((bf16[576,384]{1,0:T(8,128)(2,1)S(1)}, bf16[576,384]{1,0:T(8,128)(2,1)S(1)}, u32[]{:S(2)}, u32[]{:S(2)}) %collective-permute-start.46) | collective-permute-done | bytes 442400 | tf_op jit(solution)/shard_map/ppermute | solution.py:374
  384.1 6.0 %collective-permute-done.54.refs_1_ = bf16[2,144,384]{2,1,0:T(8,128)(2,1)S(1)} collective-permute-done((bf16[2,144,384]{2,1,0:T(8,128)(2,1)S(1)}, bf16[2,144,384]{2,1,0:T(8,128)(2,1)S(1)}, u32[]{:S(2)}, u32[]{:S(2)}) %collective-permute-start.54) | collective-permute-done | bytes 221216 | tf_op jit(solution)/shard_map/ppermute | solution.py:361
  420.1 11.4 %collective-permute-start.41 = (f32[2,1152]{1,0:T(2,128)S(1)}, f32[2,1152]{1,0:T(2,128)S(1)}, u32[]{:S(2)}, u32[]{:S(2)}) collective-permute-start(f32[2,1152]{1,0:T(2,128)S(1)} %add.143), channel_id=1, source_target_pairs={{0,1},{1,0},{2,3},{3,2},{4,5},{5,4},{6,7},{7,6},{8,9},{9,8},{10,11... | collective-permute-start | bytes 27656 | tf_op jit(solution)/shard_map/ppermute | solution.py:349
  456.6 18.4 %all-gather.12.cloned.1.call-done = bf16[24,288,384]{2,1,0:T(8,128)(2,1)} async-done(((bf16[3,288,384]{2,1,0:T(8,128)(2,1)}), bf16[24,288,384]{2,1,0:T(8,128)(2,1)}) %all-gather.12.cloned.1.call-update) | async-done | bytes 5308432 | tf_op jit(solution)/shard_map/all_gather | solution.py:446
  475.0 7.4 %shard_map.222 = (f32[288,3072]{1,0:T(8,128)}, f32[288,3072]{1,0:T(8,128)}, f32[768,1152]{1,0:T(8,128)}) custom-call(bf16[8,3,288,384]{3,2,1,0:T(8,128)(2,1)} %bitcast.83), custom_call_target="tpu_custom_call" | custom-call | bytes 1677721 | tf_op jit(solution)/shard_map/pallas_call | solution.py:1042
  (332 shorter events, 184.2 us)
Async XLA Ops:
  7.2 65.4 %all-gather.8.cloned.1.call-start = ((), (), s32[]{:S(2)}) async-start(), calls=%async_computation.8 | async-start | bytes 1658880 | tf_op jit(solution)/shard_map/all_gather | solution.py:1095
  39.0 67.7 %all-gather.10.cloned.1.call-start = ((), (), s32[]{:S(2)}) async-start(), calls=%async_computation.9 | async-start | bytes 1658880 | tf_op jit(solution)/shard_map/all_gather | solution.py:1095
  48.9 321.8 %reduce-scatter.5.cloned.1.call-start = ((), (), s32[]{:S(2)}) async-start(), calls=%async_computation.4 | async-start | bytes 4423680 | tf_op jit(solution)/shard_map/reduce_scatter | solution.py:1159
  51.1 28.0 %collective-permute-start.6 = (bf16[3,288,384]{2,1,0:T(8,128)(2,1)S(1)}, bf16[3,288,384]{2,1,0:T(8,128)(2,1)S(1)}, u32[]{:S(2)}, u32[]{:S(2)}) collective-permute-start(bf16[3,288,384]{2,1,0:T(8,128)(2,1)S(1)} %pad_maximum_fusion.refs_2_), channel_id=1, source_target_pairs={{0,4},{4,0},{1,5},{5,1},{2,6},{6,2},{3,7},{7,3},{8,12},{12,8},{9,1... | collective-permute-start | bytes 1990664 | tf_op jit(solution)/shard_map/ppermute | solution.py:1106
  52.6 31.1 %collective-permute-start.7 = (bf16[3,288,384]{2,1,0:T(8,128)(2,1)S(1)}, bf16[3,288,384]{2,1,0:T(8,128)(2,1)S(1)}, u32[]{:S(2)}, u32[]{:S(2)}) collective-permute-start(bf16[3,288,384]{2,1,0:T(8,128)(2,1)S(1)} %pad_maximum_fusion.refs_2_), channel_id=1, source_target_pairs={{0,16},{16,0},{1,17},{17,1},{2,18},{18,2},{3,19},{19,3},{4,20},{20... | collective-permute-start | bytes 1990664 | tf_op jit(solution)/shard_map/ppermute | solution.py:1107
  54.1 30.1 %collective-permute-start.8 = (bf16[3,288,384]{2,1,0:T(8,128)(2,1)S(1)}, bf16[3,288,384]{2,1,0:T(8,128)(2,1)}, u32[]{:S(2)}, u32[]{:S(2)}) collective-permute-start(bf16[3,288,384]{2,1,0:T(8,128)(2,1)S(1)} %pad_maximum_fusion.refs_2_), channel_id=1, source_target_pairs={{0,20},{4,16},{16,4},{20,0},{1,21},{5,17},{17,5},{21,1},{2,22},{6,... | collective-permute-start | bytes 1990664 | tf_op jit(solution)/shard_map/ppermute | solution.py:1108
  98.1 44.5 %collective-permute-start.13 = (bf16[2,1152,384]{2,1,0:T(8,128)(2,1)}, bf16[2,1152,384]{2,1,0:T(8,128)(2,1)}, u32[]{:S(2)}, u32[]{:S(2)}) collective-permute-start(bf16[2,1152,384]{2,1,0:T(8,128)(2,1)} %slice.99), channel_id=1, source_target_pairs={{0,8},{8,0},{1,9},{9,1},{2,10},{10,2},{3,11},{11,3},{4,12},{12,4},... | collective-permute-start | bytes 5308424 | tf_op jit(solution)/shard_map/ppermute | solution.py:57
  110.0 27.7 %collective-permute-start.14 = (bf16[3,288,384]{2,1,0:T(8,128)(2,1)}, bf16[3,288,384]{2,1,0:T(8,128)(2,1)S(1)}, u32[]{:S(2)}, u32[]{:S(2)}) collective-permute-start(bf16[3,288,384]{2,1,0:T(8,128)(2,1)} %get-tuple-element.106.refs_5_.refs_14_), channel_id=1, source_target_pairs={{0,4},{4,0},{1,5},{5,1},{2,6},{6,2},{3,7},{7,3},{8,12},{12,8},{9,1... | collective-permute-start | bytes 1990664 | tf_op jit(solution)/shard_map/ppermute | solution.py:1134
  111.5 26.2 %collective-permute-start.15 = (bf16[3,288,384]{2,1,0:T(8,128)(2,1)}, bf16[3,288,384]{2,1,0:T(8,128)(2,1)S(1)}, u32[]{:S(2)}, u32[]{:S(2)}) collective-permute-start(bf16[3,288,384]{2,1,0:T(8,128)(2,1)} %get-tuple-element.106.refs_5_.refs_14_), channel_id=1, source_target_pairs={{0,16},{16,0},{1,17},{17,1},{2,18},{18,2},{3,19},{19,3},{4,20},{20... | collective-permute-start | bytes 1990664 | tf_op jit(solution)/shard_map/ppermute | solution.py:1135
  113.0 44.2 %collective-permute-start.19 = (bf16[1152,512]{0,1:T(8,128)(2,1)S(1)}, bf16[1152,512]{0,1:T(8,128)(2,1)}, u32[]{:S(2)}, u32[]{:S(2)}) collective-permute-start(bf16[1152,512]{0,1:T(8,128)(2,1)S(1)} %bitcast.81), channel_id=1, source_target_pairs={{0,8},{8,0},{1,9},{9,1},{2,10},{10,2},{3,11},{11,3},{4,12},{12,4},... | collective-permute-start | bytes 3538952 | tf_op jit(solution)/shard_map/ppermute | solution.py:57
  152.0 34.7 %collective-permute-start.17 = (bf16[512,1152]{1,0:T(8,128)(2,1)}, bf16[512,1152]{1,0:T(8,128)(2,1)S(1)}, u32[]{:S(2)}, u32[]{:S(2)}) collective-permute-start(bf16[512,1152]{1,0:T(8,128)(2,1)} %get-tuple-element.111.refs_1_), channel_id=1, source_target_pairs={{0,8},{8,0},{1,9},{9,1},{2,10},{10,2},{3,11},{11,3},{4,12},{12,4},... | collective-permute-start | bytes 3538952 | tf_op jit(solution)/shard_map/ppermute | solution.py:57
  152.0 34.7 %collective-permute-start.18 = (bf16[1152,512]{1,0:T(8,128)(2,1)}, bf16[1152,512]{1,0:T(8,128)(2,1)}, u32[]{:S(2)}, u32[]{:S(2)}) collective-permute-start(bf16[1152,512]{1,0:T(8,128)(2,1)} %get-tuple-element.112.refs_5_), channel_id=1, source_target_pairs={{0,8},{8,0},{1,9},{9,1},{2,10},{10,2},{3,11},{11,3},{4,12},{12,4},... | collective-permute-start | bytes 3538952 | tf_op jit(solution)/shard_map/ppermute | solution.py:57
  157.7 29.0 %collective-permute-start.23 = (bf16[3,288,384]{2,1,0:T(8,128)(2,1)}, bf16[3,288,384]{2,1,0:T(8,128)(2,1)}, u32[]{:S(2)}, u32[]{:S(2)}) collective-permute-start(bf16[3,288,384]{2,1,0:T(8,128)(2,1)} %collective-permute-done.22.refs_20_), channel_id=1, source_target_pairs={{0,4},{4,0},{1,5},{5,1},{2,6},{6,2},{3,7},{7,3},{8,12},{12,8},{9,1... | collective-permute-start | bytes 1990664 | tf_op jit(solution)/shard_map/ppermute | solution.py:1139
  235.6 165.0 %reduce-scatter.9.cloned.1.call-start = ((), (), s32[]{:S(2)}) async-start(), calls=%async_computation.6 | async-start | bytes 1105920 | tf_op jit(solution)/shard_map/reduce_scatter | solution.py:424
  270.0 34.5 %collective-permute-start.32 = (bf16[2,576,384]{2,1,0:T(8,128)(2,1)}, bf16[2,576,384]{2,1,0:T(8,128)(2,1)S(1)}, u32[]{:S(2)}, u32[]{:S(2)}) collective-permute-start(bf16[2,576,384]{2,1,0:T(8,128)(2,1)} %get-tuple-element.133), channel_id=1, source_target_pairs={{0,16},{16,0},{1,17},{17,1},{2,18},{18,2},{3,19},{19,3},{4,20},{20... | collective-permute-start | bytes 2654216 | tf_op jit(solution)/shard_map/ppermute | solution.py:361
  270.7 33.8 %collective-permute-start.31 = (bf16[2,576,384]{2,1,0:T(8,128)(2,1)}, bf16[2,576,384]{2,1,0:T(8,128)(2,1)S(1)}, u32[]{:S(2)}, u32[]{:S(2)}) collective-permute-start(bf16[2,576,384]{2,1,0:T(8,128)(2,1)} %get-tuple-element.131), channel_id=1, source_target_pairs={{0,4},{4,0},{1,5},{5,1},{2,6},{6,2},{3,7},{7,3},{8,12},{12,8},{9,1... | collective-permute-start | bytes 2654216 | tf_op jit(solution)/shard_map/ppermute | solution.py:361
  271.0 30.3 %collective-permute-start.30 = (bf16[576,384]{1,0:T(8,128)(2,1)S(1)}, bf16[576,384]{1,0:T(8,128)(2,1)}, u32[]{:S(2)}, u32[]{:S(2)}) collective-permute-start(bf16[576,384]{1,0:T(8,128)(2,1)S(1)} %fusion.11.refs_9_), channel_id=1, source_target_pairs={{0,4},{4,0},{1,5},{5,1},{2,6},{6,2},{3,7},{7,3},{8,12},{12,8},{9,1... | collective-permute-start | bytes 1327112 | tf_op jit(solution)/shard_map/ppermute | solution.py:374
  272.7 28.7 %collective-permute-start.29 = (bf16[576,384]{1,0:T(8,128)(2,1)S(1)}, bf16[576,384]{1,0:T(8,128)(2,1)}, u32[]{:S(2)}, u32[]{:S(2)}) collective-permute-start(bf16[576,384]{1,0:T(8,128)(2,1)S(1)} %fusion.10.refs_8_), channel_id=1, source_target_pairs={{0,16},{16,0},{1,17},{17,1},{2,18},{18,2},{3,19},{19,3},{4,20},{20... | collective-permute-start | bytes 1327112 | tf_op jit(solution)/shard_map/ppermute | solution.py:374
  277.3 33.1 %collective-permute-start.34 = (bf16[576,576]{1,0:T(8,128)(2,1)}, bf16[576,576]{1,0:T(8,128)(2,1)}, u32[]{:S(2)}, u32[]{:S(2)}) collective-permute-start(bf16[576,576]{1,0:T(8,128)(2,1)} %get-tuple-element.184), channel_id=1, source_target_pairs={{0,8},{8,0},{1,9},{9,1},{2,10},{10,2},{3,11},{11,3},{4,12},{12,4},... | collective-permute-start | bytes 1990664 | tf_op jit(solution)/shard_map/ppermute | solution.py:57
  304.4 97.2 %reduce-scatter.11.cloned.1.call-start = ((), (), s32[]{:S(2)}) async-start(), calls=%async_computation.7 | async-start | bytes 1105920 | tf_op jit(solution)/shard_map/reduce_scatter | solution.py:424
  304.5 29.8 %collective-permute-start.33 = (bf16[2,192,1024]{2,1,0:T(8,128)(2,1)}, bf16[2,192,1024]{2,1,0:T(8,128)(2,1)S(1)}, u32[]{:S(2)}, u32[]{:S(2)}) collective-permute-start(bf16[2,192,1024]{2,1,0:T(8,128)(2,1)} %bitcast.102), channel_id=1, source_target_pairs={{4,0},{5,1},{6,2},{7,3},{12,8},{13,9},{14,10},{15,11},{20,16},{21,... | collective-permute-start | bytes 2359304 | tf_op jit(solution)/shard_map/ppermute | solution.py:1187
  306.3 28.0 %collective-permute-start.36 = (bf16[576,384]{1,0:T(8,128)(2,1)S(1)}, bf16[576,384]{1,0:T(8,128)(2,1)S(1)}, u32[]{:S(2)}, u32[]{:S(2)}) collective-permute-start(bf16[576,384]{1,0:T(8,128)(2,1)S(1)} %fusion.13), channel_id=1, source_target_pairs={{0,4},{4,0},{1,5},{5,1},{2,6},{6,2},{3,7},{7,3},{8,12},{12,8},{9,1... | collective-permute-start | bytes 1327112 | tf_op jit(solution)/shard_map/ppermute | solution.py:374
  368.7 65.1 %reduce-scatter.7.cloned.1.call-start = ((), (), s32[]{:S(2)}) async-start(), calls=%async_computation.5 | async-start | bytes 1105920 | tf_op jit(solution)/shard_map/reduce_scatter | solution.py:424
  382.6 92.4 %all-gather.12.cloned.1.call-start = ((), (), s32[]{:S(2)}) async-start(), calls=%async_computation.10 | async-start | bytes 5971968 | tf_op jit(solution)/shard_map/all_gather | solution.py:446
  (103 other events, 1126.5 us)
Sparse Core Ops, SparseCore 0:
  39.2 33.3 all-gather.7
  74.7 31.9 all-gather.9
  235.7 67.9 reduce-scatter.4
  306.4 27.9 reduce-scatter.8
  368.8 32.7 reduce-scatter.10
  404.3 23.8 reduce-scatter.6
  430.7 44.2 all-gather.11

commit v4 on v3

--- a/solution.py
+++ b/solution.py
@@ -145,7 +145,7 @@
             two[cut:, :] = own_ref[2, :, at]
 
 
-def pack_ffn(info, gate, up, down, tuned):
+def pack_ffn(info, gate, up, down, after, tuned):
     rows, hidden = gate.shape
     hidden_rows, width = down.shape
     steps = hidden // hidden_rows
@@ -157,11 +157,12 @@
         outs += [shape((rows + rows // 2, part))] * 2
     columns = pl.BlockSpec((rows, half), lambda z, info: (0, 2 * z + info[0]))
     return pl.pallas_call(
-        pack_ffn_kernel,
+        ignoring(pack_ffn_kernel, 4, after),
         grid_spec=pltpu.PrefetchScalarGridSpec(
             num_scalar_prefetch=1,
             grid=(steps,),
-            in_specs=[columns, columns, pl.BlockSpec((half, width), lambda z, info: (info[0], 0))],
+            in_specs=[columns, columns, pl.BlockSpec((half, width), lambda z, info: (info[0], 0))]
+            + [ANY] * len(after),
             out_specs=[
                 pl.BlockSpec(o.shape, lambda z, info, n=len(o.shape): (0,) * n) for o in outs
             ],
@@ -169,7 +170,7 @@
         out_shape=outs,
         compiler_params=params(),
         cost_estimate=cost(0, rows * packed * CHUNKS * 6),
-    )(info, gate, up, down)
+    )(info, gate, up, down, *after)
 
 
 def ring(count, step):
@@ -199,14 +200,16 @@
     out = shape((BLOCKS, rows * count, width // BLOCKS))
 
     def kernel(info, own_ref, *refs):
-        for copy in place_pieces(info, count, own_ref, refs[:-2], False, refs[-2], refs[-1]):
+        *stack_refs, out_ref, tail_ref, sems = refs
+        for copy in place_pieces(info, count, own_ref, stack_refs, False, out_ref, sems):
             copy.wait()
+        tail_ref[...] = out_ref[BLOCKS // 2 :]
 
     return pl.pallas_call(
         ignoring(kernel, 2 + len(stacks), after),
         in_specs=[SCALARS] + [ANY] * (1 + len(stacks) + len(after)),
-        out_specs=pl.BlockSpec(),
-        out_shape=out,
+        out_specs=[pl.BlockSpec()] * 2,
+        out_shape=[out, shape((BLOCKS // 2, *out.shape[1:]))],
         scratch_shapes=[pltpu.SemaphoreType.DMA((BLOCKS * count,))],
         compiler_params=params(),
         cost_estimate=cost(0, rows * width * count * 4),
@@ -228,7 +231,7 @@
         copy.wait()
 
 
-def pick(info, arrays, parts, rows):
+def pick(info, arrays, parts, rows, after):
     count, _, part = arrays[0].shape
     outs = [shape((count - 1, rows, part))] * len({p[0] for p in parts})
 
@@ -236,14 +239,14 @@
         pick_kernel(parts, *refs)
 
     return pl.pallas_call(
-        kernel,
-        in_specs=[SCALARS] + [ANY] * len(arrays),
+        ignoring(kernel, 1 + len(arrays), after),
+        in_specs=[SCALARS] + [ANY] * (len(arrays) + len(after)),
         out_specs=[pl.BlockSpec()] * len(outs),
         out_shape=outs,
         scratch_shapes=[pltpu.SemaphoreType.DMA((len(parts) * (count - 1),))],
         compiler_params=params(),
         cost_estimate=cost(0, len(outs) * count * rows * part * 4),
-    )(info, *arrays)
+    )(info, *arrays, *after)
 
 
 def travel_z(piece, sizes):
@@ -290,24 +293,6 @@
     return [shape((BLOCKS, rows, part))]
 
 
-def split_kernel(info, packed_ref, *refs):
-    for copy in send_out(info, packed_ref, refs[:-1], "xy", refs[-1]):
-        copy.wait()
-
-
-def split(info, packed):
-    _, rows, part = packed.shape
-    return pl.pallas_call(
-        split_kernel,
-        in_specs=[SCALARS, pl.BlockSpec()],
-        out_specs=[ANY] * 4,
-        out_shape=sent_shapes(rows, part, "xy"),
-        scratch_shapes=[pltpu.SemaphoreType.DMA((8,))],
-        compiler_params=params(),
-        cost_estimate=cost(0, 4 * BLOCKS * rows * part),
-    )(info, packed)
-
-
 def sum_over(value, axis, count):
     if count & (count - 1):
         return lax.psum(value, axis)
@@ -341,83 +326,49 @@
     return lax.ppermute(sums[0], "y", PAIR), lax.ppermute(sums[1], "x", PAIR)
 
 
-def sum_over(value, axis, count):
-    if count & (count - 1):
-        return lax.psum(value, axis)
-    step = 1
-    while step < count:
-        value = value + lax.ppermute(value, axis, [(i, i ^ step) for i in range(count)])
-        step *= 2
-    return value
-
-
-def add_low(kept, came):
-    return (kept.astype(jnp.float32) + came.astype(jnp.float32)).astype(low_type)
-
-
-def scatter_first(outs):
-    if len(outs) == 1:
-        return ()
-    return lax.ppermute(outs[1], "x", PAIR), lax.ppermute(outs[3], "y", PAIR)
-
-
-def scatter_sums(outs, came, last):
-    if len(outs) == 1:
-        return ()
-    came = lax.optimization_barrier((*came, *last))
-    return add_low(outs[0][1], came[0][1]), add_low(outs[2][1], came[1][1])
-
-
-def scatter_second(sums):
-    if len(sums) == 0:
-        return ()
-    return lax.ppermute(sums[0], "y", PAIR), lax.ppermute(sums[1], "x", PAIR)
-
-
-def scatter_mine(outs, first, second, last, sizes):
+def merge_kernel(info, *refs):
+    parts, outs, mine_s = refs[:6], refs[6:-1], refs[-1]
+    cut = mine_s.shape[0] // 2
+    rows = outs[0].shape[0]
+    for i in range(2):
+        kept, came, second = (ref[...].astype(jnp.float32) for ref in parts[3 * i : 3 * i + 3])
+        mine_s[i * cut : (i + 1) * cut, :] = (kept[0] + came[0] + second).astype(low_type)
+    for k, out in enumerate(outs):
+        row = lax.rem(info[2] + k, len(outs)) * rows if len(outs) > 1 else 0
+        out[...] = mine_s[pl.ds(row, rows), :]
+
+
+def merge(info, outs, first, second, count):
+    cut, part = second[0].shape
+    half = pl.BlockSpec((1, cut, part), lambda i: (0, 0, 0))
+    whole = pl.BlockSpec((cut, part), lambda i: (0, 0))
+    rows = 2 * cut // count
+    return pl.pallas_call(
+        merge_kernel,
+        grid=(1,),
+        in_specs=[SCALARS] + [half, half, whole] * 2,
+        out_specs=[pl.BlockSpec((rows, part), lambda i: (0, 0))] * count,
+        out_shape=[shape((rows, part))] * count,
+        scratch_shapes=[pltpu.VMEM((2 * cut, part), low_type)],
+        compiler_params=params(),
+        cost_estimate=cost(0, 16 * cut * part),
+    )(info, outs[0], first[0], second[0], outs[2], first[1], second[1])
+
+
+def scatter_mine(info, outs, first, second, last, sizes):
     ny, nx, nz = sizes
     if len(outs) == 1:
         packed = outs[0]
         total = packed.shape[1]
         split = packed.transpose(1, 0, 2).reshape(total, ny * nx, -1).transpose(1, 0, 2)
         return lax.psum_scatter(split, ("y", "x"), scatter_dimension=0, tiled=True)[0]
-    second = lax.optimization_barrier((*second, *last))
-    one = add_low(add_low(outs[0][0], first[0][0]), second[0])
-    two = add_low(add_low(outs[2][0], first[1][0]), second[1])
-    return jnp.concatenate([one, two])
-
-
-def merge_kernel(*refs):
-    parts, out = refs[:6], refs[6]
-    cut = out.shape[0] // 2
-    for i in range(2):
-        kept, came, second = (ref[...].astype(jnp.float32) for ref in parts[3 * i : 3 * i + 3])
-        out[i * cut : (i + 1) * cut, :] = (kept[0] + came[0] + second).astype(low_type)
-
-
-def merge(outs, first, second):
-    cut, part = second[0].shape
-    half = pl.BlockSpec((1, cut, part), lambda i: (0, 0, 0))
-    whole = pl.BlockSpec((cut, part), lambda i: (0, 0))
-    return pl.pallas_call(
-        merge_kernel,
-        grid=(1,),
-        in_specs=[half, half, whole] * 2,
-        out_specs=pl.BlockSpec((2 * cut, part), lambda i: (0, 0)),
-        out_shape=shape((2 * cut, part)),
-        compiler_params=params(),
-        cost_estimate=cost(0, 16 * cut * part),
-    )(outs[0], first[0], second[0], outs[2], first[1], second[1])
-
-
-def scatter_mine(outs, first, second, last, sizes):
-    ny, nx, nz = sizes
-    if len(outs) == 1:
-        packed = outs[0]
-        total = packed.shape[1]
-        split = packed.transpose(1, 0, 2).reshape(total, ny * nx, -1).transpose(1, 0, 2)
-        return lax.psum_scatter(split, ("y", "x"), scatter_dimension=0, tiled=True)[0]
-    return merge(outs, first, lax.optimization_barrier((*second, *last))[: len(second)])
+    return merge(info, outs, first, lax.optimization_barrier((*second, *last))[: len(second)], 1)[0]
+
+
+def scatter_z(pieces, sizes):
+    mine, *others = pieces
+    came = [lax.ppermute(o, "z", ring(sizes[2], k + 1)) for k, o in enumerate(others)]
+    return sum((c.astype(jnp.float32) for c in came), mine.astype(jnp.float32)).astype(low_type)
 
 
 def scatter_rows(mine):
@@ -672,9 +623,9 @@
 
 
 def out_kernel(
-    info, mine_ref, came_ref, w_ref, w_other_ref, tokens_ref, gain_ref, middle_ref, normed_ref,
-    turned_ref, rows_ref, w_s,
+    info, mine_ref, came_ref, w_ref, w_other_ref, tokens_ref, gain_ref, middle_ref, *refs
 ):
+    normed_refs, turned_refs, (rows_ref, w_s) = refs[:2], refs[2:4], refs[4:]
     place_out(info[0], w_ref, w_other_ref, w_s)
     hq = HALF_QUERY
     mine = w_s[pl.ds(pl.multiple_of(info[0] * hq, hq), hq), :]
@@ -687,8 +638,11 @@
     )
     middle_ref[...] = middle
     normed = (middle * norm_scale(middle) * gain_ref[...]).astype(low_type)
-    normed_ref[...] = normed
-    turned_ref[...] = normed.T
+    cut = normed.shape[0] // 2
+    for i in range(2):
+        part = normed[i * cut : (i + 1) * cut]
+        normed_refs[i][...] = part
+        turned_refs[i][...] = part.T
 
 
 def project_out(info, attended, came, weights, weights_other, tokens, gain, after):
@@ -710,13 +664,15 @@
         + [ANY] * len(after),
         out_specs=[
             pl.BlockSpec((rows, width), lambda i: (0, 0)),
-            pl.BlockSpec((rows, width), lambda i: (0, 0)),
-            pl.BlockSpec((width, rows), lambda i: (0, 0)),
+            pl.BlockSpec((rows // 2, width), lambda i: (0, 0)),
+            pl.BlockSpec((rows // 2, width), lambda i: (0, 0)),
+            pl.BlockSpec((width, rows // 2), lambda i: (0, 0)),
+            pl.BlockSpec((width, rows // 2), lambda i: (0, 0)),
             pl.BlockSpec((hq, width), lambda i: (0, 0)),
         ],
         out_shape=[
-            shape((rows, width), jnp.float32), shape((rows, width)), shape((width, rows)),
-            shape((hq, width)),
+            shape((rows, width), jnp.float32), shape((rows // 2, width)), shape((rows // 2, width)),
+            shape((width, rows // 2)), shape((width, rows // 2)), shape((hq, width)),
         ],
         scratch_shapes=[pltpu.VMEM((width, width), low_type)],
         compiler_params=params(),
@@ -725,7 +681,7 @@
 
 
 def ffn_kernel(tuned, ways, info, *refs):
-    xs, cs, xts, cts, w_ref, refs = refs[0:2], refs[2:4], refs[4:6], refs[6:8], refs[8], refs[9:]
+    xs, xts, cs, cts, w_ref, refs = refs[0:4], refs[4:8], refs[8:10], refs[10:12], refs[12], refs[13:]
     stacks = [()] * CHUNKS
     if tuned:
         stacks, refs = [refs[4 * j : 4 * j + 4] for j in range(CHUNKS)], refs[4 * CHUNKS :]
@@ -734,7 +690,7 @@
         x_s, c_s, xt_s, ct_s, result_s, grad_s, result_low, grad_low, land_s, gate_s, up_s, down_s,
         hidden_s, dgate_s, dup_s, packed_s, sems,
     ) = scratch
-    rows = xs[0].shape[0]
+    rows = cs[0].shape[0]
     size = FFN_ROWS
     block, part = gate_s.shape[1], packed_s.shape[3]
     width = gate_s.shape[0]
@@ -752,10 +708,11 @@
         return [begin(w_ref.at[j], target, sems.at[j, 0])]
 
     coming = weights_in(0)
-    there = [begin(ref, x_s.at[i * rows : (i + 1) * rows], sems.at[3, i]) for i, ref in enumerate(xs)]
-    there += [begin(ref, c_s.at[i * rows : (i + 1) * rows], sems.at[3, 2 + i]) for i, ref in enumerate(cs)]
-    across = [begin(ref, xt_s.at[:, i * rows : (i + 1) * rows], sems.at[3, 4 + i]) for i, ref in enumerate(xts)]
-    across += [begin(ref, ct_s.at[:, i * rows : (i + 1) * rows], sems.at[3, 6 + i]) for i, ref in enumerate(cts)]
+    few = rows // 2
+    there = [begin(ref, x_s.at[i * few : (i + 1) * few], sems.at[3, i]) for i, ref in enumerate(xs)]
+    there += [begin(ref, c_s.at[i * rows : (i + 1) * rows], sems.at[3, 4 + i]) for i, ref in enumerate(cs)]
+    across = [begin(ref, xt_s.at[:, i * few : (i + 1) * few], sems.at[3, 6 + i]) for i, ref in enumerate(xts)]
+    across += [begin(ref, ct_s.at[:, i * rows : (i + 1) * rows], sems.at[3, 10 + i]) for i, ref in enumerate(cts)]
     going = [[] for _ in range(CHUNKS + 1)]
     for j in range(CHUNKS):
         for copy in coming:
@@ -805,7 +762,7 @@
             result_low[...] = result_s[rows:, :].astype(low_type)
             grad_low[...] = grad_s[rows:, :].astype(low_type)
             sources = (result_s.at[:rows], grad_s.at[:rows], result_low, grad_low)
-            going[CHUNKS] = [begin(s, t, sems.at[3, 8 + i]) for i, (s, t) in enumerate(zip(sources, totals))]
+            going[CHUNKS] = [begin(s, t, sems.at[3, 12 + i]) for i, (s, t) in enumerate(zip(sources, totals))]
         if j >= 2:
             for copy in going[j - 2]:
                 copy.wait()
@@ -837,7 +794,7 @@
 
 
 def feed_forward(info, xs, cs, xts, cts, weights, pieces, ways, tuned, after):
-    rows, width = xs[0].shape
+    rows, width = cs[0].shape
     part = weights.shape[2] // BLOCKS if tuned else weights.shape[3]
     block = BLOCKS * part // 3
     sent = [sent_shapes(width, part, way) for way in ways]
@@ -855,8 +812,8 @@
     matrix = pltpu.VMEM((width, block), low_type)
     tokens = pltpu.VMEM((2 * rows, block), low_type)
     outs = pl.pallas_call(
-        ignoring(kernel, 10 + len(given), after),
-        in_specs=[SCALARS] + [ANY] * (9 + len(given) + len(after)),
+        ignoring(kernel, 14 + len(given), after),
+        in_specs=[SCALARS] + [ANY] * (13 + len(given) + len(after)),
         out_specs=[ANY] * (4 + sum(len(s) for s in sent)),
         out_shape=totals + sum(sent, []),
         scratch_shapes=[
@@ -867,7 +824,7 @@
         cost_estimate=cost(
             36 * rows * width * block * CHUNKS, 40 << 20, 2 * rows * block * CHUNKS
         ),
-    )(info, *xs, *cs, *xts, *cts, weights, *given, *after)
+    )(info, *xs, *xts, *cs, *cts, weights, *given, *after)
     totals, outs = outs[:4], outs[4:]
     groups = []
     for shapes in sent:
@@ -876,8 +833,11 @@
     return totals, groups
 
 
-def branch_kernel(g_ref, g_other_ref, w_ref, attended_ref, grad_ref, delta_ref, rows_ref):
+def branch_kernel(g_ref, one_ref, two_ref, w_ref, attended_ref, grad_ref, delta_ref, rows_ref, other_s):
     rows = g_ref.shape[0]
+    other_s[: rows // 2, :] = one_ref[...]
+    other_s[rows // 2 :, :] = two_ref[...]
+    g_other_ref = other_s
     delta_ref[...] = jnp.zeros(delta_ref.shape, jnp.float32)
     for i, ref in enumerate((g_ref, g_other_ref)):
         at = slice(i * rows, (i + 1) * rows)
@@ -897,16 +857,17 @@
 def branch(grad, grad_other, out_rows, attended, after):
     rows, width = grad.shape
     return pl.pallas_call(
-        ignoring(branch_kernel, 4, after),
-        in_specs=[pl.BlockSpec()] * 4 + [ANY] * len(after),
+        ignoring(branch_kernel, 5, after),
+        in_specs=[pl.BlockSpec()] * 5 + [ANY] * len(after),
         out_specs=[pl.BlockSpec()] * 3,
         out_shape=[
             shape(attended.shape), shape((GROUPS, 8, 2 * rows), jnp.float32),
             shape((HALF_QUERY, width)),
         ],
+        scratch_shapes=[pltpu.VMEM(grad.shape, low_type)],
         compiler_params=params(),
         cost_estimate=cost(8 * rows * width * HALF_QUERY, 12 << 20),
-    )(grad, grad_other, out_rows, attended, *after)
+    )(grad, *grad_other, out_rows, attended, *after)
 
 
 def attn_grad_kernel(
@@ -1071,9 +1032,13 @@
     attn_own, *attn_piece = pack_attn(
         info, (w_query, key_matrix, value_matrix, w_out), gains, tuned
     )
-    ffn_own, *ffn_piece = pack_ffn(info, w_gate, w_up, w_down, tuned)
-    ids, tokens_sent, cotangent_sent, _ = lax.optimization_barrier((ids, tokens, cotangent, ffn_own))
-    all_ids = lax.all_gather(ids, "x", axis=0, tiled=True)
+    ids = behind(ids, (attn_own,))
+    if tuned:
+        past_ids = lax.ppermute(ids, "x", [(0, 1)])
+        past_ids = jnp.where(xi == 1, past_ids, jnp.iinfo(jnp.int32).max)
+        all_ids = jnp.concatenate([ids, past_ids])
+    else:
+        all_ids = lax.all_gather(ids, "x", axis=0, tiled=True)
     first = jnp.sum((all_ids[:, None] < ids[None, :]).astype(jnp.int32), axis=0)
     firsts = jnp.concatenate([first[None], swap_core(first[None])])
     token_place = xi * rows + jnp.arange(rows, dtype=jnp.int32)
@@ -1085,29 +1050,31 @@
     info = jnp.concatenate([info, starts.reshape(-1)])
     firsts = firsts[:, None, :]
 
-    tokens_other, cotangent_other = swap_core(tokens_sent), swap_core(cotangent_sent)
-    cotangent_turned = cotangent_sent.T
-
+    ffn_own, *ffn_piece = pack_ffn(info, w_gate, w_up, w_down, (cosine, sine, firsts), tuned)
+    tokens_sent, cotangent_sent, _ = lax.optimization_barrier((tokens, cotangent, ffn_own))
+    tokens_other, cotangent_other = swap_core(jnp.stack([tokens_sent, cotangent_sent]))
+    cotangent_turned, cotangent_turned_other = cotangent_sent.T, cotangent_other.T
     if tuned:
         cut = own_rows // 2
         slots = travel_z(attn_piece[0], sizes)
         stack = jnp.stack([s[:own_rows] for s in slots])
+        tables = (tokens_other, cotangent_turned, cotangent_turned_other)
         parts = [lax.all_gather(behind(piece, (stack,)), "z", axis=0) for piece in ffn_piece]
-        ffn_stacks = list(pick(info, parts[:1], ((0, 0, 0, own_rows, 0),), own_rows))
+        ffn_stacks = list(pick(info, parts[:1], ((0, 0, 0, own_rows, 0),), own_rows, tables))
         ffn_stacks += pick(
             info,
             parts,
             ((0, 0, own_rows, own_rows + cut, 0), (0, 1, 0, cut, cut), (1, 1, cut, cut + own_rows, 0)),
             own_rows,
+            (),
         )
-        stack = behind(stack, (cosine, firsts, tokens_other, cotangent_turned, cotangent_other))
         stacks = (
             stack,
             lax.ppermute(stack, "x", PAIR),
             lax.ppermute(stack, "y", PAIR),
             lax.ppermute(stack, ("y", "x"), [(i, 3 - i) for i in range(4)]),
         )
-        weights = assemble(info, attn_own, stacks, nz, ffn_stacks[:1])
+        weights, weights_tail = assemble(info, attn_own, stacks, nz, ffn_stacks[:1])
         ffn_weights = ffn_own
         gains = [gains.astype(low_type)] + [s[own_rows : own_rows + 2, :own_rows] for s in slots]
         gains = jnp.stack(gains[::-1] + gains[::-1])
@@ -1115,6 +1082,7 @@
         gains = gains.transpose(1, 0, 2).reshape(2, width)
     else:
         weights = gather_whole(attn_own)
+        weights_tail = weights[BLOCKS // 2 :]
         ffn_pieces = [()] * CHUNKS
         before_attend = before_out = ()
         ffn_weights = jnp.stack([gather_whole(ffn_own[c]) for c in range(CHUNKS)])
@@ -1122,12 +1090,12 @@
     gain_one, gain_two = gains[:1].astype(jnp.float32), gains[1:].astype(jnp.float32)
 
     cs = (cotangent, cotangent_other)
-    cts = (cotangent_turned, swap_core(cotangent_turned))
+    cts = (cotangent_turned, cotangent_turned_other)
 
     normed, query, keyvalue = project(
         tokens, tokens_other, gain_one, weights, cosine, sine
     )
-    weights_other = swap_core(behind(weights, (keyvalue,))[2:])
+    weights_other = swap_core(weights_tail)
     if tuned:
         first_x, first_y = (lax.ppermute(ffn_stacks[0], axis, PAIR) for axis in ("x", "y"))
         past = lax.ppermute(behind(keyvalue, (first_x, first_y)), "x", [(0, 1)])[None]
@@ -1139,17 +1107,18 @@
             lax.ppermute(by_y[2], "x", PAIR),
         ]
         ffn_pieces = list(zip(ffn_stacks, by_x, by_y, far))
-        before_attend = ffn_stacks[1:]
-        before_out = (by_x[1], by_y[1], far[0])
+        before_attend = (*ffn_stacks[1:], far[0])
+        before_out = (*by_x[1:], *by_y[1:])
     else:
         past = lax.all_gather(keyvalue, "x", axis=0)
     attended, log_total = attend(info, query, keyvalue, past, firsts, size, before_attend)
     came = swap_core(attended[:, rows:].astype(low_type))
-    middle, normed_two, normed_turned, out_rows = project_out(
+    middle, *normed_parts, out_rows = project_out(
         info, attended, came, weights, weights_other, tokens, gain_two, before_out
     )
 
-    xs, xts = (normed_two, swap_core(normed_two)), (normed_turned, swap_core(normed_turned))
+    normed_parts = [list(normed_parts[:2]), list(normed_parts[2:])]
+    xs, xts = (parts + [swap_core(part) for part in parts] for parts in normed_parts)
     sent, first, send, second, reduced = ([None] * (CHUNKS + 1) for _ in range(5))
     ways = ["xy", "xy", "z"] if tuned else ["whole"] * CHUNKS
     (result, grad_normed_two, result_other, grad_other), sent[:3] = feed_forward(
@@ -1157,6 +1126,7 @@
     )
     if tuned:
         rows_two = lax.psum_scatter(sent[2][0], "z", scatter_dimension=0, tiled=True)[0]
+        reduced[2] = lax.psum_scatter(rows_two, ("y", "x"), scatter_dimension=0, tiled=True)[0]
     first[0] = scatter_first(sent[0])
 
     grad_normed_two = grad_normed_two + swap_core(grad_other).astype(jnp.float32)
@@ -1169,7 +1139,7 @@
     grad_branch = grad_middle.astype(low_type)
     output = (middle + result).astype(low_type)
 
-    grad_other = swap_core(grad_branch)
+    grad_other = [swap_core(grad_branch[i * rows // 2 : (i + 1) * rows // 2]) for i in range(2)]
     grad_attended, delta, grad_rows = branch(
         grad_branch, grad_other, out_rows, attended, ()
     )
@@ -1184,15 +1154,17 @@
         send[0],
     )
     if tuned:
-        came = lax.ppermute(behind(grad_past[0], (*second[0], *first[1])), "x", [(1, 0)])
+        came = lax.ppermute(behind(grad_past[0], (*second[0], *first[1], other)), "x", [(1, 0)])
     else:
         came = lax.psum_scatter(grad_past, "x", scatter_dimension=0, tiled=True)[0]
-    reduced[0] = scatter_mine(sent[0], first[0], second[0], (grad_past,), sizes)
+    reduced[0] = scatter_mine(info, sent[0], first[0], second[0], (grad_past,), sizes)
     send[1] = scatter_sums(sent[1], first[1], (grad_past,))
     second[1] = scatter_second(send[1])
+    last = (came, rows_two) if tuned else (came,)
+    reduced[1] = scatter_mine(info, sent[1], first[1], second[1], last, sizes)
     grad_projected, *attn_sent = attn_grads(
         info, grad_query, grad_kv, came, cosine, sine, normed, mine, other,
-        (*second[1], reduced[0]) if tuned else (), tuned,
+        (reduced[0], reduced[1]) if tuned else (), tuned,
     )
     normed_mine, normed_other = normed_grad(grad_projected, weights, ())
     grad_normed = normed_mine + swap_core(normed_other).astype(jnp.float32)
@@ -1203,30 +1175,28 @@
         grad_middle + norm_back(grad_normed * gain_one, inputs, scale_one)
     ).astype(low_type)
 
-    gain_grads = jnp.stack([grad_gain_one, grad_gain_two])
-    for axis, count in (("core", 2), ("x", nx), ("y", ny), ("z", nz)):
-        gain_grads = sum_over(gain_grads, axis, count)
-    gain_grads = lax.dynamic_slice_in_dim(gain_grads, lax.axis_index("z") * own_rows, own_rows, 1)
 
     sent[3], first[3] = attn_sent, scatter_first(attn_sent)
     last = (normed_mine,)
     send[3] = scatter_sums(sent[3], first[3], last)
     second[3] = scatter_second(send[3])
-    reduced[1] = scatter_mine(sent[1], first[1], second[1], send[3][:1] or last, sizes)
     if tuned:
-        sent[2] = split(info, behind(rows_two, (reduced[1],)))
-        first[2] = scatter_first(sent[2])
-        reduced[3] = scatter_mine(sent[3], first[3], second[3], sent[2][:1], sizes)
-        last = (reduced[3],)
-        send[2] = scatter_sums(sent[2], first[2], last)
-        second[2] = scatter_second(send[2])
-        reduced[2] = scatter_mine(sent[2], first[2], second[2], last, sizes)
+        pieces = merge(info, sent[3], first[3], second[3], nz)
+        reduced[3] = scatter_z(pieces, sizes)
+        last = pieces[:1]
     else:
-        reduced[2] = scatter_rows(scatter_mine(sent[2], (), (), last, sizes))
-        reduced[3] = scatter_mine(sent[3], (), (), last, sizes)
-    attn_out = unpack_attn(info, *spread(scatter_rows(reduced[3])[None], sizes))
-    ffn_total = jnp.stack([scatter_rows(reduced[0]), scatter_rows(reduced[1]), reduced[2]])
+        reduced[2] = scatter_rows(scatter_mine(info, sent[2], (), (), last, sizes))
+        reduced[3] = scatter_rows(scatter_mine(info, sent[3], (), (), last, sizes))
+    attn_out = unpack_attn(info, *spread(reduced[3][None], sizes))
+    ffn_total = [scatter_rows(reduced[0]), scatter_rows(reduced[1]), reduced[2]]
+    ffn_total = jnp.stack(lax.optimization_barrier((*ffn_total, *last))[:CHUNKS])
     grad_w_gate, grad_w_up, grad_w_down = unpack_ffn(info, *gather_all(ffn_total, sizes))
+    gain_grads = jnp.stack([grad_gain_one, grad_gain_two])
+    if tuned:
+        gain_grads = behind(gain_grads, pieces[:1])
+    for axis, count in (("core", 2), ("x", nx), ("y", ny), ("z", nz)):
+        gain_grads = sum_over(gain_grads, axis, count)
+    gain_grads = lax.dynamic_slice_in_dim(gain_grads, lax.axis_index("z") * own_rows, own_rows, 1)
     return (
         output[None], grad_inputs[None], gain_grads[0], *attn_out, gain_grads[1], grad_w_gate,
         grad_w_up, grad_w_down,

time: 499 us -> 464 us (0.930)
  waiting for transfers between devices: 179 us -> 150 us
    all_gather x1, waiting for transfers between devices: 18.4 us -> 0.01 us  [gather_all(): everyone = lax.all_gather(total, ('core', 'y', 'x'), axis=0)]
    ppermute x8 -> x6, waiting for transfers between devices: 30.7 us -> 16.3 us  [scatter_first(): return (lax.ppermute(outs[1], 'x', PAIR), lax.ppermute(outs[3], 'y', PAIR))]
    ppermute x1, waiting for transfers between devices: 12.5 us -> 0.01 us  [shards(): lax.ppermute(by_y[2], 'x', PAIR)]
    ppermute x5, starting transfers between devices: 14.7 us -> 4.24 us  [sum_over(): lax.ppermute(value, axis, [(i, i ^ step) for i in range(count)])]
    ppermute x3, waiting for transfers between devices: 12.8 us -> 2.7 us  [travel_z(): lax.ppermute(piece, 'z', ring(sizes[2], k))]
    ppermute x2, waiting for transfers between devices: 6.28 us -> 15 us  [shards(): by_x = [first_x] + [lax.ppermute(s, 'x', PAIR) for s in ffn_stacks[1:]]]
    all_gather x2, waiting for transfers between devices: 21.2 us -> 29.9 us  [shards(): lax.all_gather(behind(piece, (stack,)), 'z', axis=0)]
    ppermute x1 -> x5, starting transfers between devices: 1.68 us -> 10.3 us  [the longest x3 5.59 us: scatter_z(): lax.ppermute(o, 'z', ring(sizes[2], k + 1))]
  transfers between devices with their start and end apart: 65 -> 66, of which waited for: 35 -> 30; matrix products, arithmetic and copies ran while one was open for 9% -> 9% of each run, Pallas kernels for 22% -> 23%
where the time goes in v4:
time: 464 us; the launch traced here: 457 us
  Pallas kernels  164 us (35%)
  waiting for transfers between devices  150 us (32%)
  starting transfers between devices  70.9 us (15%)
  local copies, waits for them, and re-layouts  29.6 us (6%)
  other arithmetic  26.7 us (6%)
  between operations  15.4 us (3%)
    pallas_call x1, Pallas kernels, feed_forward(): pl.pallas_call(ignoring(kernel, 14 + len(given), after), in_specs=[SCALAR...  47.8 us
    ppermute x6, waiting for transfers between devices, scatter_second(): return (lax.ppermute(sums[0], 'y', PAIR), lax.ppermute(sums[1], 'x', PAIR))  36 us
    all_gather x2, waiting for transfers between devices, shards(): lax.all_gather(behind(piece, (stack,)), 'z', axis=0)  29.9 us
    pallas_call x1, Pallas kernels, attend_back(): pl.pallas_call(ignoring(attend_back_kernel, 8, after), grid=grid, in_spec...  18.2 us
    ppermute x6, waiting for transfers between devices, scatter_first(): return (lax.ppermute(outs[1], 'x', PAIR), lax.ppermute(outs[3], 'y', PAIR))  16.3 us
    pallas_call x1, Pallas kernels, attend(): pl.pallas_call(ignoring(attend_kernel, 5, after), grid=grid, in_specs=[SC...  15.3 us
    ppermute x2, waiting for transfers between devices, shards(): by_x = [first_x] + [lax.ppermute(s, 'x', PAIR) for s in ffn_stacks[1:]]  15 us
    ppermute x5, waiting for transfers between devices, sum_over(): lax.ppermute(value, axis, [(i, i ^ step) for i in range(count)])  13.4 us
  transfers between devices with their start and end apart: 66, of which 30 were waited for; matrix products, arithmetic and copies ran while one was open for 9% of the time, Pallas kernels for 23%

profile of v4, /device:TPU:0, one launch (start us, length us, event | category | flops | bytes accessed | tf_op | source)
XLA Modules:
  0.0 457.2 jit_solution(6232935436727722020)
XLA Ops:
  13.2 5.0 %collective-permute-start.3 = (bf16[304,384]{1,0:T(8,128)(2,1)}, bf16[304,384]{1,0:T(8,128)(2,1)S(1)}, u32[]{:S(2)}, u32[]{:S(2)}) collective-permute-start(bf16[304,384]{1,0:T(8,128)(2,1)} %get-tuple-element.96), channel_id=1, source_target_pairs={{0,3},{1,0},{2,1},{3,2},{4,7},{5,4},{6,5},{7,6},{8,11},{9,8},{10,9... | collective-permute-start | bytes 700424 | tf_op jit(solution)/shard_map/ppermute | solution.py:253
  29.4 6.1 %shard_map.204 = (bf16[3,288,1536]{2,1,0:T(8,128)(2,1)}, bf16[432,384]{1,0:T(8,128)(2,1)}, bf16[432,384]{1,0:T(8,128)(2,1)}) custom-call(s32[8]{0:T(128)} %concatenate.29.refs_0_.info, f32[288,3072]{1,0:T(8,128)} %refs_1_.1, f32[288,3072]{1,0:T(8,128)} %refs_2_.1, f32[768,1152]{1,0:T(8,128)} %refs_3_.1, f32[32,1024]{1,0:T(8,128)} %get-tuple-element.190.refs_4_.cos_ref, ...), custom_call_target="tpu_custom_call" | custom-call | bytes 796262 | tf_op jit(solution)/shard_map/pallas_call | solution.py:159
  52.2 19.9 %all-gather.7.cloned.1.call-done = bf16[1728,384]{1,0:T(8,128)(2,1)} async-done(((bf16[432,384]{1,0:T(8,128)(2,1)}), bf16[1728,384]{1,0:T(8,128)(2,1)}) %all-gather.7.cloned.1.call-update) | async-done | bytes 1327120 | tf_op jit(solution)/shard_map/all_gather | solution.py:1062
  79.3 5.5 %shard_map.206 = (bf16[4,1152,384]{2,1,0:T(8,128)(2,1)}, bf16[2,1152,384]{2,1,0:T(8,128)(2,1)}) custom-call(s32[8]{0:T(128)} %concatenate.29.refs_0_.info, bf16[288,1536]{1,0:T(8,128)(2,1)} %get-tuple-element.91.refs_1_, bf16[3,288,384]{2,1,0:T(8,128)(2,1)} %copy-done.13, bf16[3,288,384]{2,1,0:T(8,128)(2,1)} %copy-done.31, ...), custom_call_target="tpu_custom_call" | custom-call | bytes 707788 | tf_op jit(solution)/shard_map/pallas_call | solution.py:208
  85.7 7.3 %shard_map.207 = (bf16[1152,1024]{1,0:T(8,128)(2,1)}, bf16[576,1024]{1,0:T(8,128)(2,1)}, bf16[2,192,1024]{2,1,0:T(8,128)(2,1)}) custom-call(bf16[512,1152]{1,0:T(8,128)(2,1)} %bitcast.82, bf16[512,1152]{1,0:T(8,128)(2,1)} %get-tuple-element.184.refs_2_.other_ref, f32[1,1152]{1,0:T(1,128)} %reshape.186.gain_ref, ...), custom_call_target="tpu_custom_call" | custom-call | flops 226492416 | bytes 1468006 | tf_op jit(solution)/shard_map/pallas_call | solution.py:438
  96.2 10.0 %all-gather.9.cloned.1.call-done = bf16[1728,384]{1,0:T(8,128)(2,1)} async-done(((bf16[432,384]{1,0:T(8,128)(2,1)}), bf16[1728,384]{1,0:T(8,128)(2,1)}) %all-gather.9.cloned.1.call-update) | async-done | bytes 1327120 | tf_op jit(solution)/shard_map/all_gather | solution.py:1062
  113.0 15.0 %collective-permute-done.15.refs_7_.refs_19_ = bf16[3,288,384]{2,1,0:T(8,128)(2,1)S(1)} collective-permute-done((bf16[3,288,384]{2,1,0:T(8,128)(2,1)}, bf16[3,288,384]{2,1,0:T(8,128)(2,1)S(1)}, u32[]{:S(2)}, u32[]{:S(2)}) %collective-permute-start.15) | collective-permute-done | bytes 663584 | tf_op jit(solution)/shard_map/ppermute | solution.py:1102
  131.1 15.3 %shard_map.209 = (f32[576,1024]{1,0:T(8,128)}, f32[3,8,1024]{2,1,0:T(8,128)}) custom-call(s32[8]{0:T(128)} %concatenate.29.refs_0_.info, bf16[576,1024]{1,0:T(8,128)(2,1)} %get-tuple-element.100.refs_1_, bf16[2,192,1024]{2,1,0:T(8,128)(2,1)} %get-tuple-element.102.refs_2_, bf16[1,2,192,1024]{3,2,1,0:T(8,128)(2,1)} %bitcast.91, ...), custom_call_target="tpu_custom_call" | custom-call | flops 905969664 | bytes 838860 | tf_op jit(solution)/shard_map/pallas_call | solution.py:576
  148.6 5.2 %collective-permute-start.24 = (bf16[3,288,384]{2,1,0:T(8,128)(2,1)S(1)}, bf16[3,288,384]{2,1,0:T(8,128)(2,1)S(1)}, u32[]{:S(2)}, u32[]{:S(2)}) collective-permute-start(bf16[3,288,384]{2,1,0:T(8,128)(2,1)S(1)} %collective-permute-done.18.refs_10_.refs_24_), channel_id=1, source_target_pairs={{0,4},{4,0},{1,5},{5,1},{2,6},{6,2},{3,7},{7,3},{8,12},{12,8},{9,1... | collective-permute-start | bytes 1990664 | tf_op jit(solution)/shard_map/ppermute | solution.py:1107
  154.5 5.8 %collective-permute-done.17.refs_9_.refs_20_ = bf16[3,288,384]{2,1,0:T(8,128)(2,1)S(1)} collective-permute-done((bf16[3,288,384]{2,1,0:T(8,128)(2,1)}, bf16[3,288,384]{2,1,0:T(8,128)(2,1)S(1)}, u32[]{:S(2)}, u32[]{:S(2)}) %collective-permute-start.17) | collective-permute-done | bytes 663584 | tf_op jit(solution)/shard_map/ppermute | solution.py:1103
  161.1 9.1 %shard_map.210 = (f32[512,1152]{1,0:T(8,128)}, bf16[256,1152]{1,0:T(8,128)(2,1)}, bf16[256,1152]{1,0:T(8,128)(2,1)}, bf16[1152,256]{1,0:T(8,128)(2,1)}, bf16[115...) custom-call(s32[8]{0:T(128)} %concatenate.29.refs_0_.info, f32[576,1024]{1,0:T(8,128)} %get-tuple-element.107.refs_1_.refs_4_, ...), custom_call_target="tpu_custom_call" | custom-call | flops 135895456 | bytes 1677721 | tf_op jit(solution)/shard_map/pallas_call | solution.py:652
  175.8 47.8 %shard_map.211 = (f32[512,1152]{1,0:T(8,128)}, f32[512,1152]{1,0:T(8,128)}, bf16[512,1152]{1,0:T(8,128)(2,1)}, bf16[512,1152]{1,0:T(8,128)(2,1)}, bf16[2,576,384...) custom-call(s32[8]{0:T(128)} %concatenate.29.refs_0_.info, ...), custom_call_target="tpu_custom_call" | custom-call | flops 3261490688 | bytes 4194304 | tf_op jit(solution)/shard_map/pallas_call | solution.py:814
  238.8 7.3 %shard_map.212 = (bf16[576,1024]{1,0:T(8,128)(2,1)}, f32[3,8,1024]{2,1,0:T(8,128)}, bf16[576,1152]{1,0:T(8,128)(2,1)}) custom-call(bf16[512,1152]{1,0:T(8,128)(2,1)} %copy-done.5, bf16[256,1152]{1,0:T(8,128)(2,1)} %copy-done.36, bf16[256,1152]{1,0:T(8,128)(2,1)} %copy-done.37, bf16[576,1152]{1,0:T(8,128)(2,1)} %get-tuple-element.118.refs_3_, ...), custom_call_target="tpu_custom_call" | custom-call | flops 271790912 | bytes 1258291 | tf_op jit(solution)/shard_map/pallas_call | solution.py:859
  256.1 18.2 %shard_map.213 = (f32[576,1024]{1,0:T(8,128)}, f32[2,192,1024]{2,1,0:T(8,128)}, bf16[1,2,192,1024]{3,2,1,0:T(8,128)(2,1)}) custom-call(s32[8]{0:T(128)} %concatenate.29.refs_0_.info, bf16[576,1024]{1,0:T(8,128)(2,1)} %get-tuple-element.100.refs_1_, bf16[2,192,1024]{2,1,0:T(8,128)(2,1)} %get-tuple-element.102.refs_2_, bf16[1,2,192,1024]{3,2,1,0:T(8,128)(2,1)} %bitcast.92, ...), custom_call_target="tpu_custom_call" | custom-call | flops 1358954496 | bytes 1258291 | tf_op jit(solution)/shard_map/pallas_call | solution.py:597
  286.2 5.2 %collective-permute-start.38 = (bf16[576,384]{1,0:T(8,128)(2,1)S(1)}, bf16[576,384]{1,0:T(8,128)(2,1)S(1)}, u32[]{:S(2)}, u32[]{:S(2)}) collective-permute-start(bf16[576,384]{1,0:T(8,128)(2,1)S(1)} %fusion.13), channel_id=1, source_target_pairs={{0,4},{4,0},{1,5},{5,1},{2,6},{6,2},{3,7},{7,3},{8,12},{12,8},{9,1... | collective-permute-start | bytes 1327112 | tf_op jit(solution)/shard_map/ppermute | solution.py:326
  294.5 23.0 %collective-permute-done.38.refs_5_ = bf16[576,384]{1,0:T(8,128)(2,1)S(1)} collective-permute-done((bf16[576,384]{1,0:T(8,128)(2,1)S(1)}, bf16[576,384]{1,0:T(8,128)(2,1)S(1)}, u32[]{:S(2)}, u32[]{:S(2)}) %collective-permute-start.38) | collective-permute-done | bytes 442400 | tf_op jit(solution)/shard_map/ppermute | solution.py:326
  322.1 9.9 %shard_map.216 = (bf16[960,1024]{1,0:T(8,128)(2,1)}, bf16[2,576,384]{2,1,0:T(8,128)(2,1)}, bf16[2,576,384]{2,1,0:T(8,128)(2,1)}, bf16[2,576,384]{2,1,0:T(8,128)(2,1)}, bf16[2,576,384]{2,1,0:T(8,128)(2,1)}) custom-call(s32[8]{0:T(128)} %concatenate.29.refs_0_.info, f32[576,1024]{1,0:T(8,128)} %get-tuple-element.128.refs_1_, ...), custom_call_target="tpu_custom_call" | custom-call | flops 226492416 | bytes 2097152 | tf_op jit(solution)/shard_map/pallas_call | solution.py:903
  335.2 7.7 %shard_map.217 = (f32[512,1152]{1,0:T(8,128)}, bf16[512,1152]{1,0:T(8,128)(2,1)}) custom-call(bf16[960,1024]{1,0:T(8,128)(2,1)} %get-tuple-element.147.refs_0_, bf16[4,1152,384]{2,1,0:T(8,128)(2,1)} %get-tuple-element.99.w_ref.refs_3_.refs_1_), custom_call_target="tpu_custom_call" | custom-call | flops 226492416 | bytes 943718 | tf_op jit(solution)/shard_map/pallas_call | solution.py:931
  342.9 10.6 %collective-permute-done.40.refs_1_ = bf16[2,576,384]{2,1,0:T(8,128)(2,1)S(1)} collective-permute-done((bf16[2,576,384]{2,1,0:T(8,128)(2,1)}, bf16[2,576,384]{2,1,0:T(8,128)(2,1)S(1)}, u32[]{:S(2)}, u32[]{:S(2)}) %collective-permute-start.40) | collective-permute-done | bytes 884768 | tf_op jit(solution)/shard_map/ppermute | solution.py:313
  358.5 9.8 %collective-permute-done.43.refs_5_ = bf16[576,384]{1,0:T(8,128)(2,1)S(1)} collective-permute-done((bf16[576,384]{1,0:T(8,128)(2,1)S(1)}, bf16[576,384]{1,0:T(8,128)(2,1)S(1)}, u32[]{:S(2)}, u32[]{:S(2)}) %collective-permute-start.43) | collective-permute-done | bytes 442400 | tf_op jit(solution)/shard_map/ppermute | solution.py:326
  375.6 8.3 %reduce-scatter.13.cloned.1.call-done = bf16[1,288,384]{2,1,0:T(8,128)(2,1)} async-done(((bf16[4,288,384]{2,1,0:T(8,128)(2,1)}), bf16[1,288,384]{2,1,0:T(8,128)(2,1)}) %reduce-scatter.13.cloned.1.call-update) | async-done | bytes 221200
  406.5 10.1 %collective-permute-done.47 = f32[2,1152]{1,0:T(2,128)S(1)} collective-permute-done((f32[2,1152]{1,0:T(2,128)S(1)}, f32[2,1152]{1,0:T(2,128)S(1)}, u32[]{:S(2)}, u32[]{:S(2)}) %collective-permute-start.47) | collective-permute-done | bytes 9248 | tf_op jit(solution)/shard_map/ppermute | solution.py:301
  425.7 5.6 %collective-permute-done.52.refs_1_ = bf16[1,288,384]{2,1,0:T(8,128)(2,1)S(1)} collective-permute-done((bf16[1,288,384]{2,1,0:T(8,128)(2,1)S(1)}, bf16[1,288,384]{2,1,0:T(8,128)(2,1)S(1)}, u32[]{:S(2)}, u32[]{:S(2)}) %collective-permute-start.52) | collective-permute-done | bytes 221216 | tf_op jit(solution)/shard_map/ppermute | solution.py:382
  442.5 7.4 %shard_map.220 = (f32[288,3072]{1,0:T(8,128)}, f32[288,3072]{1,0:T(8,128)}, f32[768,1152]{1,0:T(8,128)}) custom-call(bf16[8,3,288,384]{3,2,1,0:T(8,128)(2,1)} %bitcast.86), custom_call_target="tpu_custom_call" | custom-call | bytes 1677721 | tf_op jit(solution)/shard_map/pallas_call | solution.py:1003
  (334 shorter events, 166.8 us)
Async XLA Ops:
  7.2 64.9 %all-gather.7.cloned.1.call-start = ((), (), s32[]{:S(2)}) async-start(), calls=%async_computation.7 | async-start | bytes 1658880 | tf_op jit(solution)/shard_map/all_gather | solution.py:1062
  38.5 67.7 %all-gather.9.cloned.1.call-start = ((), (), s32[]{:S(2)}) async-start(), calls=%async_computation.8 | async-start | bytes 1658880 | tf_op jit(solution)/shard_map/all_gather | solution.py:1062
  41.8 36.7 %collective-permute-start.6 = (bf16[3,288,384]{2,1,0:T(8,128)(2,1)S(1)}, bf16[3,288,384]{2,1,0:T(8,128)(2,1)S(1)}, u32[]{:S(2)}, u32[]{:S(2)}) collective-permute-start(bf16[3,288,384]{2,1,0:T(8,128)(2,1)S(1)} %pad_maximum_fusion.1.refs_2_), channel_id=1, source_target_pairs={{0,4},{4,0},{1,5},{5,1},{2,6},{6,2},{3,7},{7,3},{8,12},{12,8},{9,1... | collective-permute-start | bytes 1990664 | tf_op jit(solution)/shard_map/ppermute | solution.py:1073
  43.2 35.2 %collective-permute-start.7 = (bf16[3,288,384]{2,1,0:T(8,128)(2,1)S(1)}, bf16[3,288,384]{2,1,0:T(8,128)(2,1)}, u32[]{:S(2)}, u32[]{:S(2)}) collective-permute-start(bf16[3,288,384]{2,1,0:T(8,128)(2,1)S(1)} %pad_maximum_fusion.1.refs_2_), channel_id=1, source_target_pairs={{0,16},{16,0},{1,17},{17,1},{2,18},{18,2},{3,19},{19,3},{4,20},{20... | collective-permute-start | bytes 1990664 | tf_op jit(solution)/shard_map/ppermute | solution.py:1074
  44.8 33.7 %collective-permute-start.8 = (bf16[3,288,384]{2,1,0:T(8,128)(2,1)S(1)}, bf16[3,288,384]{2,1,0:T(8,128)(2,1)}, u32[]{:S(2)}, u32[]{:S(2)}) collective-permute-start(bf16[3,288,384]{2,1,0:T(8,128)(2,1)S(1)} %pad_maximum_fusion.1.refs_2_), channel_id=1, source_target_pairs={{0,20},{4,16},{16,4},{20,0},{1,21},{5,17},{17,5},{21,1},{2,22},{6,... | collective-permute-start | bytes 1990664 | tf_op jit(solution)/shard_map/ppermute | solution.py:1075
  45.3 272.3 %reduce-scatter.7.cloned.1.call-start = ((), (), s32[]{:S(2)}) async-start(), calls=%async_computation.4 | async-start | bytes 4423680 | tf_op jit(solution)/shard_map/reduce_scatter | solution.py:1128
  84.8 75.5 %collective-permute-start.14 = (bf16[2,1152,384]{2,1,0:T(8,128)(2,1)}, bf16[2,1152,384]{2,1,0:T(8,128)(2,1)}, u32[]{:S(2)}, u32[]{:S(2)}) collective-permute-start(bf16[2,1152,384]{2,1,0:T(8,128)(2,1)} %get-tuple-element.108), channel_id=1, source_target_pairs={{0,8},{8,0},{1,9},{9,1},{2,10},{10,2},{3,11},{11,3},{4,12},{12,4},... | collective-permute-start | bytes 5308424 | tf_op jit(solution)/shard_map/ppermute | solution.py:57
  93.0 37.1 %collective-permute-start.11 = (bf16[2,192,1024]{2,1,0:T(8,128)(2,1)}, bf16[2,192,1024]{2,1,0:T(8,128)(2,1)S(1)}, u32[]{:S(2)}, u32[]{:S(2)}) collective-permute-start(bf16[2,192,1024]{2,1,0:T(8,128)(2,1)} %get-tuple-element.102.refs_2_), channel_id=1, source_target_pairs={{0,4},{1,5},{2,6},{3,7},{8,12},{9,13},{10,14},{11,15},{16,20},{17,... | collective-permute-start | bytes 2359304 | tf_op jit(solution)/shard_map/ppermute | solution.py:1101
  112.4 36.1 %collective-permute-start.16 = (bf16[3,288,384]{2,1,0:T(8,128)(2,1)}, bf16[3,288,384]{2,1,0:T(8,128)(2,1)S(1)}, u32[]{:S(2)}, u32[]{:S(2)}) collective-permute-start(bf16[3,288,384]{2,1,0:T(8,128)(2,1)} %get-tuple-element.106.refs_6_.refs_22_), channel_id=1, source_target_pairs={{0,4},{4,0},{1,5},{5,1},{2,6},{6,2},{3,7},{7,3},{8,12},{12,8},{9,1... | collective-permute-start | bytes 1990664 | tf_op jit(solution)/shard_map/ppermute | solution.py:1102
  129.0 31.2 %collective-permute-start.17 = (bf16[3,288,384]{2,1,0:T(8,128)(2,1)}, bf16[3,288,384]{2,1,0:T(8,128)(2,1)S(1)}, u32[]{:S(2)}, u32[]{:S(2)}) collective-permute-start(bf16[3,288,384]{2,1,0:T(8,128)(2,1)} %get-tuple-element.105.refs_5_.refs_18_), channel_id=1, source_target_pairs={{0,16},{16,0},{1,17},{17,1},{2,18},{18,2},{3,19},{19,3},{4,20},{20... | collective-permute-start | bytes 1990664 | tf_op jit(solution)/shard_map/ppermute | solution.py:1103
  130.1 42.5 %collective-permute-start.23 = (bf16[3,288,384]{2,1,0:T(8,128)(2,1)S(1)}, bf16[3,288,384]{2,1,0:T(8,128)(2,1)}, u32[]{:S(2)}, u32[]{:S(2)}) collective-permute-start(bf16[3,288,384]{2,1,0:T(8,128)(2,1)S(1)} %collective-permute-done.15.refs_7_.refs_19_), channel_id=1, source_target_pairs={{0,16},{16,0},{1,17},{17,1},{2,18},{18,2},{3,19},{19,3},{4,20},{20... | collective-permute-start | bytes 1990664 | tf_op jit(solution)/shard_map/ppermute | solution.py:1106
  148.6 24.0 %collective-permute-start.24 = (bf16[3,288,384]{2,1,0:T(8,128)(2,1)S(1)}, bf16[3,288,384]{2,1,0:T(8,128)(2,1)S(1)}, u32[]{:S(2)}, u32[]{:S(2)}) collective-permute-start(bf16[3,288,384]{2,1,0:T(8,128)(2,1)S(1)} %collective-permute-done.18.refs_10_.refs_24_), channel_id=1, source_target_pairs={{0,4},{4,0},{1,5},{5,1},{2,6},{6,2},{3,7},{7,3},{8,12},{12,8},{9,1... | collective-permute-start | bytes 1990664 | tf_op jit(solution)/shard_map/ppermute | solution.py:1107
  223.6 151.9 %reduce-scatter.9.cloned.1.call-start = ((), (), s32[]{:S(2)}) async-start(), calls=%async_computation.5 | async-start | bytes 1105920 | tf_op jit(solution)/shard_map/reduce_scatter | solution.py:375
  225.5 22.7 %collective-permute-start.29 = (bf16[2,576,384]{2,1,0:T(8,128)(2,1)}, bf16[2,576,384]{2,1,0:T(8,128)(2,1)}, u32[]{:S(2)}, u32[]{:S(2)}) collective-permute-start(bf16[2,576,384]{2,1,0:T(8,128)(2,1)} %get-tuple-element.123), channel_id=1, source_target_pairs={{0,4},{4,0},{1,5},{5,1},{2,6},{6,2},{3,7},{7,3},{8,12},{12,8},{9,1... | collective-permute-start | bytes 2654216 | tf_op jit(solution)/shard_map/ppermute | solution.py:313
  250.8 23.6 %collective-permute-start.32 = (bf16[576,384]{1,0:T(8,128)(2,1)S(1)}, bf16[576,384]{1,0:T(8,128)(2,1)S(1)}, u32[]{:S(2)}, u32[]{:S(2)}) collective-permute-start(bf16[576,384]{1,0:T(8,128)(2,1)S(1)} %fusion.11.refs_9_), channel_id=1, source_target_pairs={{0,4},{4,0},{1,5},{5,1},{2,6},{6,2},{3,7},{7,3},{8,12},{12,8},{9,1... | collective-permute-start | bytes 1327112 | tf_op jit(solution)/shard_map/ppermute | solution.py:326
  253.0 29.5 %collective-permute-start.34 = (bf16[2,576,384]{2,1,0:T(8,128)(2,1)}, bf16[2,576,384]{2,1,0:T(8,128)(2,1)S(1)}, u32[]{:S(2)}, u32[]{:S(2)}) collective-permute-start(bf16[2,576,384]{2,1,0:T(8,128)(2,1)} %get-tuple-element.134), channel_id=1, source_target_pairs={{0,16},{16,0},{1,17},{17,1},{2,18},{18,2},{3,19},{19,3},{4,20},{20... | collective-permute-start | bytes 2654216 | tf_op jit(solution)/shard_map/ppermute | solution.py:313
  254.5 28.0 %collective-permute-start.33 = (bf16[2,576,384]{2,1,0:T(8,128)(2,1)}, bf16[2,576,384]{2,1,0:T(8,128)(2,1)S(1)}, u32[]{:S(2)}, u32[]{:S(2)}) collective-permute-start(bf16[2,576,384]{2,1,0:T(8,128)(2,1)} %get-tuple-element.132), channel_id=1, source_target_pairs={{0,4},{4,0},{1,5},{5,1},{2,6},{6,2},{3,7},{7,3},{8,12},{12,8},{9,1... | collective-permute-start | bytes 2654216 | tf_op jit(solution)/shard_map/ppermute | solution.py:313
  278.5 97.0 %reduce-scatter.11.cloned.1.call-start = ((), (), s32[]{:S(2)}) async-start(), calls=%async_computation.6 | async-start | bytes 1105920 | tf_op jit(solution)/shard_map/reduce_scatter | solution.py:375
  284.8 32.8 %collective-permute-start.36 = (bf16[2,192,1024]{2,1,0:T(8,128)(2,1)S(1)}, bf16[2,192,1024]{2,1,0:T(8,128)(2,1)}, u32[]{:S(2)}, u32[]{:S(2)}) collective-permute-start(bf16[2,192,1024]{2,1,0:T(8,128)(2,1)S(1)} %bitcast.101), channel_id=1, source_target_pairs={{4,0},{5,1},{6,2},{7,3},{12,8},{13,9},{14,10},{15,11},{20,16},{21,... | collective-permute-start | bytes 2359304 | tf_op jit(solution)/shard_map/ppermute | solution.py:1157
  286.2 31.4 %collective-permute-start.38 = (bf16[576,384]{1,0:T(8,128)(2,1)S(1)}, bf16[576,384]{1,0:T(8,128)(2,1)S(1)}, u32[]{:S(2)}, u32[]{:S(2)}) collective-permute-start(bf16[576,384]{1,0:T(8,128)(2,1)S(1)} %fusion.13), channel_id=1, source_target_pairs={{0,4},{4,0},{1,5},{5,1},{2,6},{6,2},{3,7},{7,3},{8,12},{12,8},{9,1... | collective-permute-start | bytes 1327112 | tf_op jit(solution)/shard_map/ppermute | solution.py:326
  291.5 26.1 %collective-permute-start.37 = (bf16[576,384]{1,0:T(8,128)(2,1)S(1)}, bf16[576,384]{1,0:T(8,128)(2,1)S(1)}, u32[]{:S(2)}, u32[]{:S(2)}) collective-permute-start(bf16[576,384]{1,0:T(8,128)(2,1)S(1)} %fusion.12), channel_id=1, source_target_pairs={{0,16},{16,0},{1,17},{17,1},{2,18},{18,2},{3,19},{19,3},{4,20},{20... | collective-permute-start | bytes 1327112 | tf_op jit(solution)/shard_map/ppermute | solution.py:326
  321.7 62.1 %reduce-scatter.13.cloned.1.call-start = ((), (), s32[]{:S(2)}) async-start(), calls=%async_computation.10 | async-start | bytes 1105920
  332.1 22.7 %collective-permute-start.41 = (bf16[2,576,384]{2,1,0:T(8,128)(2,1)}, bf16[2,576,384]{2,1,0:T(8,128)(2,1)S(1)}, u32[]{:S(2)}, u32[]{:S(2)}) collective-permute-start(bf16[2,576,384]{2,1,0:T(8,128)(2,1)} %get-tuple-element.152), channel_id=1, source_target_pairs={{0,16},{16,0},{1,17},{17,1},{2,18},{18,2},{3,19},{19,3},{4,20},{20... | collective-permute-start | bytes 2654216 | tf_op jit(solution)/shard_map/ppermute | solution.py:313
  335.1 107.4 %all-gather.11.cloned.1.call-start = ((), (), s32[]{:S(2)}) async-start(), calls=%async_computation.9 | async-start | bytes 5971968 | tf_op jit(solution)/shard_map/all_gather | solution.py:397
  (104 other events, 1034.5 us)
Sparse Core Ops, SparseCore 0:
  38.6 33.3 all-gather.6
  74.2 31.9 all-gather.8
  223.7 67.6 reduce-scatter.6
  294.1 24.8 reduce-scatter.8
  321.9 32.5 reduce-scatter.10
  357.3 26.4 reduce-scatter.12
  386.3 47.0 all-gather.10

commit v5 on v4

--- a/solution.py
+++ b/solution.py
@@ -293,16 +293,6 @@
     return [shape((BLOCKS, rows, part))]
 
 
-def sum_over(value, axis, count):
-    if count & (count - 1):
-        return lax.psum(value, axis)
-    step = 1
-    while step < count:
-        value = value + lax.ppermute(value, axis, [(i, i ^ step) for i in range(count)])
-        step *= 2
-    return value
-
-
 def add_low(kept, came):
     return (kept.astype(jnp.float32) + came.astype(jnp.float32)).astype(low_type)
 
@@ -326,33 +316,40 @@
     return lax.ppermute(sums[0], "y", PAIR), lax.ppermute(sums[1], "x", PAIR)
 
 
-def merge_kernel(info, *refs):
-    parts, outs, mine_s = refs[:6], refs[6:-1], refs[-1]
+def merge_kernel(more, info, *refs):
+    parts, outs, mine_s = refs[:6], refs[6 + more : -1], refs[-1]
     cut = mine_s.shape[0] // 2
-    rows = outs[0].shape[0]
+    rows = mine_s.shape[0] // len(outs)
     for i in range(2):
         kept, came, second = (ref[...].astype(jnp.float32) for ref in parts[3 * i : 3 * i + 3])
         mine_s[i * cut : (i + 1) * cut, :] = (kept[0] + came[0] + second).astype(low_type)
     for k, out in enumerate(outs):
-        row = lax.rem(info[2] + k, len(outs)) * rows if len(outs) > 1 else 0
-        out[...] = mine_s[pl.ds(row, rows), :]
-
-
-def merge(info, outs, first, second, count):
+        z = lax.rem(info[2] + k, len(outs)) if len(outs) > 1 else 0
+        out[:rows, :] = mine_s[pl.ds(z * rows, rows), :]
+        if more:
+            out[rows:, :] = refs[6][z]
+
+
+def merge(info, outs, first, second, count, more=()):
     cut, part = second[0].shape
     half = pl.BlockSpec((1, cut, part), lambda i: (0, 0, 0))
     whole = pl.BlockSpec((cut, part), lambda i: (0, 0))
-    rows = 2 * cut // count
-    return pl.pallas_call(
-        merge_kernel,
+    rows = 2 * cut // count + sum(m.shape[1] for m in more)
+
+    def kernel(*refs):
+        merge_kernel(len(more), *refs)
+
+    return pl.pallas_call(
+        kernel,
         grid=(1,),
-        in_specs=[SCALARS] + [half, half, whole] * 2,
+        in_specs=[SCALARS] + [half, half, whole] * 2
+        + [pl.BlockSpec(m.shape, lambda i: (0, 0, 0)) for m in more],
         out_specs=[pl.BlockSpec((rows, part), lambda i: (0, 0))] * count,
         out_shape=[shape((rows, part))] * count,
         scratch_shapes=[pltpu.VMEM((2 * cut, part), low_type)],
         compiler_params=params(),
         cost_estimate=cost(0, 16 * cut * part),
-    )(info, outs[0], first[0], second[0], outs[2], first[1], second[1])
+    )(info, outs[0], first[0], second[0], outs[2], first[1], second[1], *more)
 
 
 def scatter_mine(info, outs, first, second, last, sizes):
@@ -365,9 +362,11 @@
     return merge(info, outs, first, lax.optimization_barrier((*second, *last))[: len(second)], 1)[0]
 
 
-def scatter_z(pieces, sizes):
-    mine, *others = pieces
-    came = [lax.ppermute(o, "z", ring(sizes[2], k + 1)) for k, o in enumerate(others)]
+def send_z(pieces, sizes):
+    return [lax.ppermute(o, "z", ring(sizes[2], k + 1)) for k, o in enumerate(pieces[1:])]
+
+
+def sum_z(mine, came):
     return sum((c.astype(jnp.float32) for c in came), mine.astype(jnp.float32)).astype(low_type)
 
 
@@ -914,15 +913,19 @@
     )(info, grad_query, grad_kv, came, cosine, sine, normed, mine, other, *after)
 
 
-def normed_grad_kernel(d_ref, w_ref, mine_ref, other_ref):
+def normed_grad_kernel(d_ref, w_ref, mine_ref, *other_refs):
     rows = mine_ref.shape[0]
     hk, part = HALF_KEY, w_ref.shape[2]
-    for i, ref in enumerate((other_ref, mine_ref)):
-        at = slice((1 - i) * rows, (2 - i) * rows)
-        d = d_ref[:, at].T
+    for i in range(2):
+        d = d_ref[:, i * rows : (i + 1) * rows].T
         value = dot(d[:, :part], w_ref[0], (1, 1)) + dot(d[:, part : 2 * part], w_ref[1], (1, 1))
         value = value + dot(d[:, 2 * part :], w_ref[2][:, :hk], (1, 1))
-        ref[...] = value.astype(ref.dtype)
+        if i == 0:
+            mine_ref[...] = value
+        else:
+            for j, ref in enumerate(other_refs):
+                cut = ref.shape[0]
+                ref[...] = value[j * cut : (j + 1) * cut].astype(low_type)
 
 
 def normed_grad(d, weights, after):
@@ -931,8 +934,8 @@
     return pl.pallas_call(
         ignoring(normed_grad_kernel, 2, after),
         in_specs=[pl.BlockSpec()] * 2 + [ANY] * len(after),
-        out_specs=[pl.BlockSpec()] * 2,
-        out_shape=[shape((rows, width), jnp.float32), shape((rows, width))],
+        out_specs=[pl.BlockSpec()] * 3,
+        out_shape=[shape((rows, width), jnp.float32)] + [shape((rows // 2, width))] * 2,
         compiler_params=params(),
         cost_estimate=cost(4 * rows * width * 960, 9 << 20),
     )(d, weights, *after)
@@ -954,27 +957,36 @@
     return jnp.where(low, mine, other), jnp.where(low, other, mine)
 
 
-def unpack_attn_kernel(info, *refs):
+def unpack_attn_kernel(gains, info, *refs):
     refs, outs = refs[: 2 * BLOCKS], refs[2 * BLOCKS :]
-    both = [value.astype(jnp.float32) for value in halves(info, refs, 0)]
+    rows = outs[0].shape[0]
+    both = [value[:rows].astype(jnp.float32) for value in halves(info, refs, 0)]
     start = 0
-    for ref, size in zip(outs, (HALF_QUERY, HALF_KEY, HALF_KEY, HALF_QUERY)):
+    for ref, size in zip(outs[:4], (HALF_QUERY, HALF_KEY, HALF_KEY, HALF_QUERY)):
         ref[...] = jnp.concatenate([v[:, start : start + size] for v in both], axis=1)
         start += size
-
-
-def unpack_attn(info, mine, other):
-    rows = mine[0].shape[1]
-    return pl.pallas_call(
-        unpack_attn_kernel,
-        in_specs=[SCALARS] + [pl.BlockSpec()] * (2 * BLOCKS),
-        out_specs=[pl.BlockSpec()] * 4,
-        out_shape=[
-            shape((rows, 2 * n), jnp.float32) for n in (HALF_QUERY, HALF_KEY, HALF_KEY, HALF_QUERY)
-        ],
+    if gains:
+        total = sum(ref[0, rows:, :].astype(jnp.float32) for ref in refs)
+        outs[4][...] = total[:2, :rows]
+
+
+def unpack_attn(info, mine, other, rows, after):
+    gains = mine[0].shape[1] > rows
+    outs = [shape((rows, 2 * n), jnp.float32) for n in (HALF_QUERY, HALF_KEY, HALF_KEY, HALF_QUERY)]
+    if gains:
+        outs.append(shape((2, rows), jnp.float32))
+
+    def kernel(*refs):
+        unpack_attn_kernel(gains, *refs)
+
+    return pl.pallas_call(
+        ignoring(kernel, 1 + 2 * BLOCKS, after),
+        in_specs=[SCALARS] + [pl.BlockSpec()] * (2 * BLOCKS) + [ANY] * len(after),
+        out_specs=[pl.BlockSpec()] * len(outs),
+        out_shape=outs,
         compiler_params=params(),
         cost_estimate=cost(0, 6 << 20),
-    )(info, *mine, *other)
+    )(info, *mine, *other, *after)
 
 
 def unpack_ffn_kernel(all_ref, gate_ref, up_ref, down_ref):
@@ -1098,20 +1110,22 @@
     weights_other = swap_core(weights_tail)
     if tuned:
         first_x, first_y = (lax.ppermute(ffn_stacks[0], axis, PAIR) for axis in ("x", "y"))
+        far_first = lax.ppermute(first_x, "y", PAIR)
         past = lax.ppermute(behind(keyvalue, (first_x, first_y)), "x", [(0, 1)])[None]
         by_x = [first_x] + [lax.ppermute(s, "x", PAIR) for s in ffn_stacks[1:]]
         by_y = [first_y] + [lax.ppermute(s, "y", PAIR) for s in ffn_stacks[1:]]
-        far = [
-            lax.ppermute(by_x[0], "y", PAIR),
-            lax.ppermute(by_x[1], "y", PAIR),
-            lax.ppermute(by_y[2], "x", PAIR),
-        ]
-        ffn_pieces = list(zip(ffn_stacks, by_x, by_y, far))
-        before_attend = (*ffn_stacks[1:], far[0])
+        before_attend = (*ffn_stacks[1:], far_first)
         before_out = (*by_x[1:], *by_y[1:])
     else:
         past = lax.all_gather(keyvalue, "x", axis=0)
     attended, log_total = attend(info, query, keyvalue, past, firsts, size, before_attend)
+    if tuned:
+        far = [
+            far_first,
+            lax.ppermute(behind(by_x[1], (attended,)), "y", PAIR),
+            lax.ppermute(behind(by_y[2], (attended,)), "x", PAIR),
+        ]
+        ffn_pieces = list(zip(ffn_stacks, by_x, by_y, far))
     came = swap_core(attended[:, rows:].astype(low_type))
     middle, *normed_parts, out_rows = project_out(
         info, attended, came, weights, weights_other, tokens, gain_two, before_out
@@ -1126,7 +1140,6 @@
     )
     if tuned:
         rows_two = lax.psum_scatter(sent[2][0], "z", scatter_dimension=0, tiled=True)[0]
-        reduced[2] = lax.psum_scatter(rows_two, ("y", "x"), scatter_dimension=0, tiled=True)[0]
     first[0] = scatter_first(sent[0])
 
     grad_normed_two = grad_normed_two + swap_core(grad_other).astype(jnp.float32)
@@ -1154,20 +1167,28 @@
         send[0],
     )
     if tuned:
-        came = lax.ppermute(behind(grad_past[0], (*second[0], *first[1], other)), "x", [(1, 0)])
+        pieces = merge(info, sent[0], first[0], lax.optimization_barrier((*second[0], grad_past))[:2], nz)
+        first_pieces, first_z = pieces, send_z(pieces, sizes)
+    else:
+        reduced[0] = scatter_mine(info, sent[0], first[0], second[0], (grad_past,), sizes)
+    if tuned:
+        came = lax.ppermute(behind(grad_past[0], (first_pieces[0], *first[1], other)), "x", [(1, 0)])
     else:
         came = lax.psum_scatter(grad_past, "x", scatter_dimension=0, tiled=True)[0]
-    reduced[0] = scatter_mine(info, sent[0], first[0], second[0], (grad_past,), sizes)
     send[1] = scatter_sums(sent[1], first[1], (grad_past,))
     second[1] = scatter_second(send[1])
+    if tuned:
+        rows_two, _ = lax.optimization_barrier((rows_two, came))
+        reduced[2] = lax.psum_scatter(rows_two, ("y", "x"), scatter_dimension=0, tiled=True)[0]
     last = (came, rows_two) if tuned else (came,)
     reduced[1] = scatter_mine(info, sent[1], first[1], second[1], last, sizes)
     grad_projected, *attn_sent = attn_grads(
         info, grad_query, grad_kv, came, cosine, sine, normed, mine, other,
-        (reduced[0], reduced[1]) if tuned else (), tuned,
-    )
-    normed_mine, normed_other = normed_grad(grad_projected, weights, ())
-    grad_normed = normed_mine + swap_core(normed_other).astype(jnp.float32)
+        (*first_z, reduced[1]) if tuned else (), tuned,
+    )
+    normed_mine, *normed_other = normed_grad(grad_projected, weights, ())
+    normed_came = [swap_core(part) for part in normed_other]
+    grad_normed = normed_mine + jnp.concatenate(normed_came).astype(jnp.float32)
     inputs = tokens.astype(jnp.float32)
     scale_one = norm_scale(inputs)
     grad_gain_one = jnp.sum(grad_normed * inputs * scale_one, axis=0)
@@ -1178,25 +1199,37 @@
 
     sent[3], first[3] = attn_sent, scatter_first(attn_sent)
     last = (normed_mine,)
-    send[3] = scatter_sums(sent[3], first[3], last)
+    if tuned:
+        first_z = lax.optimization_barrier((*first_z, normed_mine))[:-1]
+        reduced[0] = sum_z(first_pieces[0], first_z)
+    send[3] = scatter_sums(sent[3], first[3], (*normed_came, reduced[2]) if tuned else last)
     second[3] = scatter_second(send[3])
     if tuned:
-        pieces = merge(info, sent[3], first[3], second[3], nz)
-        reduced[3] = scatter_z(pieces, sizes)
-        last = pieces[:1]
+        gain_grads = jnp.stack([grad_gain_one, grad_gain_two]).reshape(2, nz, own_rows)
+        gain_grads = jnp.pad(
+            gain_grads.transpose(1, 0, 2).astype(low_type),
+            ((0, 0), (0, GAIN_ROWS - 2), (0, sent[3][0].shape[2] - own_rows)),
+        )
+        pieces = merge(info, sent[3], first[3], second[3], nz, (gain_grads,))
+        came_z = send_z(pieces, sizes)
+        reduced[3] = sum_z(pieces[0], came_z)
+        last = send[3]
     else:
         reduced[2] = scatter_rows(scatter_mine(info, sent[2], (), (), last, sizes))
         reduced[3] = scatter_rows(scatter_mine(info, sent[3], (), (), last, sizes))
-    attn_out = unpack_attn(info, *spread(reduced[3][None], sizes))
-    ffn_total = [scatter_rows(reduced[0]), scatter_rows(reduced[1]), reduced[2]]
+    ffn_total = [
+        reduced[0] if tuned else scatter_rows(reduced[0]),
+        scatter_rows(behind(reduced[1], (grad_projected,))),
+        reduced[2],
+    ]
     ffn_total = jnp.stack(lax.optimization_barrier((*ffn_total, *last))[:CHUNKS])
     grad_w_gate, grad_w_up, grad_w_down = unpack_ffn(info, *gather_all(ffn_total, sizes))
-    gain_grads = jnp.stack([grad_gain_one, grad_gain_two])
+    attn_out = unpack_attn(info, *spread(reduced[3][None], sizes), own_rows, ())
     if tuned:
-        gain_grads = behind(gain_grads, pieces[:1])
-    for axis, count in (("core", 2), ("x", nx), ("y", ny), ("z", nz)):
-        gain_grads = sum_over(gain_grads, axis, count)
-    gain_grads = lax.dynamic_slice_in_dim(gain_grads, lax.axis_index("z") * own_rows, own_rows, 1)
+        attn_out, gain_grads = attn_out[:4], attn_out[4]
+    else:
+        gain_grads = lax.psum(jnp.stack([grad_gain_one, grad_gain_two]), ("y", "core", "x", "z"))
+        gain_grads = lax.dynamic_slice_in_dim(gain_grads, lax.axis_index("z") * own_rows, own_rows, 1)
     return (
         output[None], grad_inputs[None], gain_grads[0], *attn_out, gain_grads[1], grad_w_gate,
         grad_w_up, grad_w_down,

time: 464 us -> 441 us (0.950)
  waiting for transfers between devices: 150 us -> 126 us
    ppermute x12 -> x10, waiting for transfers between devices: 15.2 us -> 42.2 us  [the longest x1 18.2 us: shards(): lax.ppermute(behind(grad_past[0], (first_pieces[0], *first[1], other)), '...]
    ppermute x6, waiting for transfers between devices: 36 us -> 19.5 us  [scatter_second(): return (lax.ppermute(sums[0], 'y', PAIR), lax.ppermute(sums[1], 'x', PAIR))]
    ppermute x2, waiting for transfers between devices: 15 us -> 2.64 us  [shards(): by_x = [first_x] + [lax.ppermute(s, 'x', PAIR) for s in ffn_stacks[1:]]]
    unnamed x8 -> x7, waiting for transfers between devices: 8.39 us -> 0.1 us
    ppermute x12 -> x10, starting transfers between devices: 18.8 us -> 25.2 us  [the longest x6 14 us: send_z(): lax.ppermute(o, 'z', ring(sizes[2], k + 1))]
    ppermute x2, waiting for transfers between devices: 5.8 us -> 0.01 us  [shards(): by_y = [first_y] + [lax.ppermute(s, 'y', PAIR) for s in ffn_stacks[1:]]]
    ppermute x6, starting transfers between devices: 12.8 us -> 7.12 us  [scatter_second(): return (lax.ppermute(sums[0], 'y', PAIR), lax.ppermute(sums[1], 'x', PAIR))]
    ppermute x18 -> x19, waiting for transfers between devices: 9.47 us -> 5.88 us  [swap_core(): return lax.ppermute(value, 'core', PAIR)]
  transfers between devices with their start and end apart: 66 -> 64, of which waited for: 30 -> 30; matrix products, arithmetic and copies ran while one was open for 9% -> 11% of each run, Pallas kernels for 23% -> 23%
where the time goes in v5:
time: 441 us; the launch traced here: 435 us
  Pallas kernels  160 us (36%)
  waiting for transfers between devices  126 us (29%)
  starting transfers between devices  70.9 us (16%)
  local copies, waits for them, and re-layouts  33.6 us (8%)
  other arithmetic  28.7 us (7%)
  between operations  15.4 us (3%)
    pallas_call x1, Pallas kernels, feed_forward(): pl.pallas_call(ignoring(kernel, 14 + len(given), after), in_specs=[SCALAR...  47.8 us
    all_gather x2, waiting for transfers between devices, shards(): lax.all_gather(behind(piece, (stack,)), 'z', axis=0)  28.9 us
    ppermute x6, waiting for transfers between devices, scatter_second(): return (lax.ppermute(sums[0], 'y', PAIR), lax.ppermute(sums[1], 'x', PAIR))  19.5 us
    ppermute x1, waiting for transfers between devices, shards(): lax.ppermute(behind(grad_past[0], (first_pieces[0], *first[1], other)), '...  18.2 us
    ppermute x6, waiting for transfers between devices, send_z(): lax.ppermute(o, 'z', ring(sizes[2], k + 1))  17.9 us
    pallas_call x1, Pallas kernels, attend_back(): pl.pallas_call(ignoring(attend_back_kernel, 8, after), grid=grid, in_spec...  16.1 us
    ppermute x6, starting transfers between devices, send_z(): lax.ppermute(o, 'z', ring(sizes[2], k + 1))  14 us
    unnamed x145, local copies, waits for them, and re-layouts  13.9 us
  transfers between devices with their start and end apart: 64, of which 30 were waited for; matrix products, arithmetic and copies ran while one was open for 11% of the time, Pallas kernels for 23%

profile of v5, /device:TPU:0, one launch (start us, length us, event | category | flops | bytes accessed | tf_op | source)
XLA Modules:
  0.0 435.1 jit_solution(10946559516722139955)
XLA Ops:
  13.2 5.0 %collective-permute-start.3 = (bf16[304,384]{1,0:T(8,128)(2,1)}, bf16[304,384]{1,0:T(8,128)(2,1)S(1)}, u32[]{:S(2)}, u32[]{:S(2)}) collective-permute-start(bf16[304,384]{1,0:T(8,128)(2,1)} %get-tuple-element.108), channel_id=1, source_target_pairs={{0,3},{1,0},{2,1},{3,2},{4,7},{5,4},{6,5},{7,6},{8,11},{9,8},{10,9... | collective-permute-start | bytes 700424 | tf_op jit(solution)/shard_map/ppermute | solution.py:253
  29.5 6.1 %shard_map.204 = (bf16[3,288,1536]{2,1,0:T(8,128)(2,1)}, bf16[432,384]{1,0:T(8,128)(2,1)}, bf16[432,384]{1,0:T(8,128)(2,1)}) custom-call(s32[8]{0:T(128)} %concatenate.34.refs_0_, f32[288,3072]{1,0:T(8,128)} %refs_1_.1, f32[288,3072]{1,0:T(8,128)} %refs_2_.1, f32[768,1152]{1,0:T(8,128)} %refs_3_.1, f32[32,1024]{1,0:T(8,128)} %get-tuple-element.214.refs_4_.cos_ref, ...), custom_call_target="tpu_custom_call" | custom-call | bytes 796262 | tf_op jit(solution)/shard_map/pallas_call | solution.py:159
  51.6 20.5 %all-gather.7.cloned.1.call-done = bf16[1728,384]{1,0:T(8,128)(2,1)} async-done(((bf16[432,384]{1,0:T(8,128)(2,1)}), bf16[1728,384]{1,0:T(8,128)(2,1)}) %all-gather.7.cloned.1.call-update) | async-done | bytes 1327120 | tf_op jit(solution)/shard_map/all_gather | solution.py:1074
  79.7 5.4 %shard_map.206 = (bf16[4,1152,384]{2,1,0:T(8,128)(2,1)}, bf16[2,1152,384]{2,1,0:T(8,128)(2,1)}) custom-call(s32[8]{0:T(128)} %concatenate.34.refs_0_, bf16[288,1536]{1,0:T(8,128)(2,1)} %get-tuple-element.103.refs_1_, bf16[3,288,384]{2,1,0:T(8,128)(2,1)} %copy-done.14, bf16[3,288,384]{2,1,0:T(8,128)(2,1)} %copy-done.36, bf16[3,288,384]{2,1,0:T(8,128)(2,1)} %copy-done.37, ...), custom_call_target="tpu_custom_call" | custom-call | bytes 707788 | tf_op jit(solution)/shard_map/pallas_call | solution.py:208
  86.0 7.3 %shard_map.207 = (bf16[1152,1024]{1,0:T(8,128)(2,1)}, bf16[576,1024]{1,0:T(8,128)(2,1)}, bf16[2,192,1024]{2,1,0:T(8,128)(2,1)}) custom-call(bf16[512,1152]{1,0:T(8,128)(2,1)} %bitcast.84, bf16[512,1152]{1,0:T(8,128)(2,1)} %get-tuple-element.208.refs_2_.other_ref, f32[1,1152]{1,0:T(1,128)} %reshape.193.gain_ref, ...), custom_call_target="tpu_custom_call" | custom-call | flops 226492416 | bytes 1468006 | tf_op jit(solution)/shard_map/pallas_call | solution.py:437
  97.8 8.4 %all-gather.9.cloned.1.call-done = bf16[1728,384]{1,0:T(8,128)(2,1)} async-done(((bf16[432,384]{1,0:T(8,128)(2,1)}), bf16[1728,384]{1,0:T(8,128)(2,1)}) %all-gather.9.cloned.1.call-update) | async-done | bytes 1327120 | tf_op jit(solution)/shard_map/all_gather | solution.py:1074
  115.9 13.7 %shard_map.209 = (f32[576,1024]{1,0:T(8,128)}, f32[3,8,1024]{2,1,0:T(8,128)}) custom-call(s32[8]{0:T(128)} %concatenate.34.refs_0_, bf16[576,1024]{1,0:T(8,128)(2,1)} %get-tuple-element.112.refs_1_, bf16[2,192,1024]{2,1,0:T(8,128)(2,1)} %get-tuple-element.114.refs_2_, bf16[1,2,192,1024]{3,2,1,0:T(8,128)(2,1)} %bitcast.22.refs_3_, ...), custom_call_target="tpu_custom_call" | custom-call | flops 905969664 | bytes 838860 | tf_op jit(solution)/shard_map/pallas_call | solution.py:575
  129.6 8.8 %collective-permute-start.24 = (bf16[3,288,384]{2,1,0:T(8,128)(2,1)S(1)}, bf16[3,288,384]{2,1,0:T(8,128)(2,1)S(1)}, u32[]{:S(2)}, u32[]{:S(2)}) collective-permute-start(bf16[3,288,384]{2,1,0:T(8,128)(2,1)S(1)} %collective-permute-done.18.refs_10_.refs_24_), channel_id=1, source_target_pairs={{0,4},{4,0},{1,5},{5,1},{2,6},{6,2},{3,7},{7,3},{8,12},{12,8},{9,1... | collective-permute-start | bytes 1990664 | tf_op jit(solution)/shard_map/ppermute | solution.py:1126
  145.4 9.1 %shard_map.210 = (f32[512,1152]{1,0:T(8,128)}, bf16[256,1152]{1,0:T(8,128)(2,1)}, bf16[256,1152]{1,0:T(8,128)(2,1)}, bf16[1152,256]{1,0:T(8,128)(2,1)}, bf16[115...) custom-call(s32[8]{0:T(128)} %concatenate.34.refs_0_, f32[576,1024]{1,0:T(8,128)} %get-tuple-element.119.refs_1_.refs_4_, ...), custom_call_target="tpu_custom_call" | custom-call | flops 135895456 | bytes 1677721 | tf_op jit(solution)/shard_map/pallas_call | solution.py:651
  160.1 47.8 %shard_map.211 = (f32[512,1152]{1,0:T(8,128)}, f32[512,1152]{1,0:T(8,128)}, bf16[512,1152]{1,0:T(8,128)(2,1)}, bf16[512,1152]{1,0:T(8,128)(2,1)}, bf16[2,576,384...) custom-call(s32[8]{0:T(128)} %concatenate.34.refs_0_, ...), custom_call_target="tpu_custom_call" | custom-call | flops 3261490688 | bytes 4194304 | tf_op jit(solution)/shard_map/pallas_call | solution.py:813
  223.4 7.2 %shard_map.212 = (bf16[576,1024]{1,0:T(8,128)(2,1)}, f32[3,8,1024]{2,1,0:T(8,128)}, bf16[576,1152]{1,0:T(8,128)(2,1)}) custom-call(bf16[512,1152]{1,0:T(8,128)(2,1)} %copy-done.5, bf16[256,1152]{1,0:T(8,128)(2,1)} %copy-done.42, bf16[256,1152]{1,0:T(8,128)(2,1)} %copy-done.43, bf16[576,1152]{1,0:T(8,128)(2,1)} %get-tuple-element.132.refs_3_, ...), custom_call_target="tpu_custom_call" | custom-call | flops 271790912 | bytes 1258291 | tf_op jit(solution)/shard_map/pallas_call | solution.py:858
  242.5 16.1 %shard_map.213 = (f32[576,1024]{1,0:T(8,128)}, f32[2,192,1024]{2,1,0:T(8,128)}, bf16[1,2,192,1024]{3,2,1,0:T(8,128)(2,1)}) custom-call(s32[8]{0:T(128)} %concatenate.34.refs_0_, bf16[576,1024]{1,0:T(8,128)(2,1)} %get-tuple-element.112.refs_1_, bf16[2,192,1024]{2,1,0:T(8,128)(2,1)} %get-tuple-element.114.refs_2_, bf16[1,2,192,1024]{3,2,1,0:T(8,128)(2,1)} %bitcast.22.refs_3_, ...), custom_call_target="tpu_custom_call" | custom-call | flops 1358954496 | bytes 1258291 | tf_op jit(solution)/shard_map/pallas_call | solution.py:596
  258.6 9.0 %collective-permute-done.32.refs_6_ = bf16[576,384]{1,0:T(8,128)(2,1)S(1)} collective-permute-done((bf16[576,384]{1,0:T(8,128)(2,1)}, bf16[576,384]{1,0:T(8,128)(2,1)S(1)}, u32[]{:S(2)}, u32[]{:S(2)}) %collective-permute-start.32) | collective-permute-done | bytes 442400 | tf_op jit(solution)/shard_map/ppermute | solution.py:316
  274.1 18.2 %collective-permute-done.36.refs_3_ = bf16[2,192,1024]{2,1,0:T(8,128)(2,1)} collective-permute-done((bf16[2,192,1024]{2,1,0:T(8,128)(2,1)}, bf16[2,192,1024]{2,1,0:T(8,128)(2,1)}, u32[]{:S(2)}, u32[]{:S(2)}) %collective-permute-start.36) | collective-permute-done | bytes 786464 | tf_op jit(solution)/shard_map/ppermute | solution.py:1175
  294.5 5.7 %collective-permute-start.38 = (bf16[288,384]{1,0:T(8,128)(2,1)}, bf16[288,384]{1,0:T(8,128)(2,1)S(1)}, u32[]{:S(2)}, u32[]{:S(2)}) collective-permute-start(bf16[288,384]{1,0:T(8,128)(2,1)} %get-tuple-element.156), channel_id=1, source_target_pairs={{0,2},{1,3},{2,0},{3,1},{4,6},{5,7},{6,4},{7,5},{8,10},{9,11},{10,... | collective-permute-start | bytes 663560 | tf_op jit(solution)/shard_map/ppermute | solution.py:366
  306.4 8.0 %collective-permute-done.38.refs_10_ = bf16[288,384]{1,0:T(8,128)(2,1)S(1)} collective-permute-done((bf16[288,384]{1,0:T(8,128)(2,1)}, bf16[288,384]{1,0:T(8,128)(2,1)S(1)}, u32[]{:S(2)}, u32[]{:S(2)}) %collective-permute-start.38) | collective-permute-done | bytes 221216 | tf_op jit(solution)/shard_map/ppermute | solution.py:366
  315.2 9.9 %shard_map.216 = (bf16[960,1024]{1,0:T(8,128)(2,1)}, bf16[2,576,384]{2,1,0:T(8,128)(2,1)}, bf16[2,576,384]{2,1,0:T(8,128)(2,1)}, bf16[2,576,384]{2,1,0:T(8,128)(2,1)}, bf16[2,576,384]{2,1,0:T(8,128)(2,1)}) custom-call(s32[8]{0:T(128)} %concatenate.34.refs_0_, f32[576,1024]{1,0:T(8,128)} %get-tuple-element.142.refs_1_, ...), custom_call_target="tpu_custom_call" | custom-call | flops 226492416 | bytes 2097152 | tf_op jit(solution)/shard_map/pallas_call | solution.py:902
  328.8 7.1 %shard_map.217 = (f32[512,1152]{1,0:T(8,128)}, bf16[256,1152]{1,0:T(8,128)(2,1)}, bf16[256,1152]{1,0:T(8,128)(2,1)}) custom-call(bf16[960,1024]{1,0:T(8,128)(2,1)} %get-tuple-element.166.refs_0_, bf16[4,1152,384]{2,1,0:T(8,128)(2,1)} %get-tuple-element.111.w_ref.refs_3_.refs_1_), custom_call_target="tpu_custom_call" | custom-call | flops 226492416 | bytes 943718 | tf_op jit(solution)/shard_map/pallas_call | solution.py:934
  339.0 8.0 %collective-permute-done.44.refs_2_ = bf16[2,576,384]{2,1,0:T(8,128)(2,1)} collective-permute-done((bf16[2,576,384]{2,1,0:T(8,128)(2,1)}, bf16[2,576,384]{2,1,0:T(8,128)(2,1)}, u32[]{:S(2)}, u32[]{:S(2)}) %collective-permute-start.44) | collective-permute-done | bytes 884768 | tf_op jit(solution)/shard_map/ppermute | solution.py:303
  365.4 6.9 %collective-permute-done.47.refs_6_ = bf16[576,384]{1,0:T(8,128)(2,1)} collective-permute-done((bf16[576,384]{1,0:T(8,128)(2,1)}, bf16[576,384]{1,0:T(8,128)(2,1)}, u32[]{:S(2)}, u32[]{:S(2)}) %collective-permute-start.47) | collective-permute-done | bytes 442400 | tf_op jit(solution)/shard_map/ppermute | solution.py:316
  377.9 4.9 %collective-permute-start.48 = (bf16[304,384]{1,0:T(8,128)(2,1)}, bf16[304,384]{1,0:T(8,128)(2,1)S(1)}, u32[]{:S(2)}, u32[]{:S(2)}) collective-permute-start(bf16[304,384]{1,0:T(8,128)(2,1)} %get-tuple-element.177), channel_id=1, source_target_pairs={{0,1},{1,2},{2,3},{3,0},{4,5},{5,6},{6,7},{7,4},{8,9},{9,10},{10,1... | collective-permute-start | bytes 700424 | tf_op jit(solution)/shard_map/ppermute | solution.py:366
  387.9 7.3 %collective-permute-done.49 = bf16[304,384]{1,0:T(8,128)(2,1)S(1)} collective-permute-done((bf16[304,384]{1,0:T(8,128)(2,1)}, bf16[304,384]{1,0:T(8,128)(2,1)S(1)}, u32[]{:S(2)}, u32[]{:S(2)}) %collective-permute-start.49) | collective-permute-done | bytes 233504 | tf_op jit(solution)/shard_map/ppermute | solution.py:366
  400.3 6.8 %collective-permute-done.51.refs_2_ = bf16[1,304,384]{2,1,0:T(8,128)(2,1)S(1)} collective-permute-done((bf16[1,304,384]{2,1,0:T(8,128)(2,1)S(1)}, bf16[1,304,384]{2,1,0:T(8,128)(2,1)S(1)}, u32[]{:S(2)}, u32[]{:S(2)}) %collective-permute-start.51) | collective-permute-done | bytes 233504 | tf_op jit(solution)/shard_map/ppermute | solution.py:381
  420.4 7.4 %shard_map.220 = (f32[288,3072]{1,0:T(8,128)}, f32[288,3072]{1,0:T(8,128)}, f32[768,1152]{1,0:T(8,128)}) custom-call(bf16[8,3,288,384]{3,2,1,0:T(8,128)(2,1)} %bitcast.88), custom_call_target="tpu_custom_call" | custom-call | bytes 1677721 | tf_op jit(solution)/shard_map/pallas_call | solution.py:1015
  (340 shorter events, 164.9 us)
Async XLA Ops:
  7.2 64.9 %all-gather.7.cloned.1.call-start = ((), (), s32[]{:S(2)}) async-start(), calls=%async_computation.5 | async-start | bytes 1658880 | tf_op jit(solution)/shard_map/all_gather | solution.py:1074
  13.2 22.4 %collective-permute-start.3 = (bf16[304,384]{1,0:T(8,128)(2,1)}, bf16[304,384]{1,0:T(8,128)(2,1)S(1)}, u32[]{:S(2)}, u32[]{:S(2)}) collective-permute-start(bf16[304,384]{1,0:T(8,128)(2,1)} %get-tuple-element.108), channel_id=1, source_target_pairs={{0,3},{1,0},{2,1},{3,2},{4,7},{5,4},{6,5},{7,6},{8,11},{9,8},{10,9... | collective-permute-start | bytes 700424 | tf_op jit(solution)/shard_map/ppermute | solution.py:253
  38.5 67.7 %all-gather.9.cloned.1.call-start = ((), (), s32[]{:S(2)}) async-start(), calls=%async_computation.6 | async-start | bytes 1658880 | tf_op jit(solution)/shard_map/all_gather | solution.py:1074
  41.8 36.9 %collective-permute-start.6 = (bf16[3,288,384]{2,1,0:T(8,128)(2,1)S(1)}, bf16[3,288,384]{2,1,0:T(8,128)(2,1)S(1)}, u32[]{:S(2)}, u32[]{:S(2)}) collective-permute-start(bf16[3,288,384]{2,1,0:T(8,128)(2,1)S(1)} %pad_maximum_fusion.1.refs_2_), channel_id=1, source_target_pairs={{0,4},{4,0},{1,5},{5,1},{2,6},{6,2},{3,7},{7,3},{8,12},{12,8},{9,1... | collective-permute-start | bytes 1990664 | tf_op jit(solution)/shard_map/ppermute | solution.py:1085
  43.2 35.4 %collective-permute-start.7 = (bf16[3,288,384]{2,1,0:T(8,128)(2,1)S(1)}, bf16[3,288,384]{2,1,0:T(8,128)(2,1)S(1)}, u32[]{:S(2)}, u32[]{:S(2)}) collective-permute-start(bf16[3,288,384]{2,1,0:T(8,128)(2,1)S(1)} %pad_maximum_fusion.1.refs_2_), channel_id=1, source_target_pairs={{0,16},{16,0},{1,17},{17,1},{2,18},{18,2},{3,19},{19,3},{4,20},{20... | collective-permute-start | bytes 1990664 | tf_op jit(solution)/shard_map/ppermute | solution.py:1086
  44.8 33.9 %collective-permute-start.8 = (bf16[3,288,384]{2,1,0:T(8,128)(2,1)S(1)}, bf16[3,288,384]{2,1,0:T(8,128)(2,1)}, u32[]{:S(2)}, u32[]{:S(2)}) collective-permute-start(bf16[3,288,384]{2,1,0:T(8,128)(2,1)S(1)} %pad_maximum_fusion.1.refs_2_), channel_id=1, source_target_pairs={{0,20},{4,16},{16,4},{20,0},{1,21},{5,17},{17,5},{21,1},{2,22},{6,... | collective-permute-start | bytes 1990664 | tf_op jit(solution)/shard_map/ppermute | solution.py:1087
  45.3 247.1 %reduce-scatter.6.cloned.1.call-start = ((), (), s32[]{:S(2)}) async-start(), calls=%async_computation.3 | async-start | bytes 4423680 | tf_op jit(solution)/shard_map/reduce_scatter | solution.py:1142
  85.2 59.3 %collective-permute-start.14 = (bf16[2,1152,384]{2,1,0:T(8,128)(2,1)}, bf16[2,1152,384]{2,1,0:T(8,128)(2,1)}, u32[]{:S(2)}, u32[]{:S(2)}) collective-permute-start(bf16[2,1152,384]{2,1,0:T(8,128)(2,1)} %get-tuple-element.120), channel_id=1, source_target_pairs={{0,8},{8,0},{1,9},{9,1},{2,10},{10,2},{3,11},{11,3},{4,12},{12,4},... | collective-permute-start | bytes 5308424 | tf_op jit(solution)/shard_map/ppermute | solution.py:57
  93.3 21.7 %collective-permute-start.11 = (bf16[2,192,1024]{2,1,0:T(8,128)(2,1)}, bf16[2,192,1024]{2,1,0:T(8,128)(2,1)}, u32[]{:S(2)}, u32[]{:S(2)}) collective-permute-start(bf16[2,192,1024]{2,1,0:T(8,128)(2,1)} %get-tuple-element.114.refs_2_), channel_id=1, source_target_pairs={{0,4},{1,5},{2,6},{3,7},{8,12},{9,13},{10,14},{11,15},{16,20},{17,... | collective-permute-start | bytes 2359304 | tf_op jit(solution)/shard_map/ppermute | solution.py:1114
  111.0 29.6 %collective-permute-start.15 = (bf16[3,288,384]{2,1,0:T(8,128)(2,1)}, bf16[3,288,384]{2,1,0:T(8,128)(2,1)S(1)}, u32[]{:S(2)}, u32[]{:S(2)}) collective-permute-start(bf16[3,288,384]{2,1,0:T(8,128)(2,1)} %get-tuple-element.117.refs_5_.refs_18_), channel_id=1, source_target_pairs={{0,4},{4,0},{1,5},{5,1},{2,6},{6,2},{3,7},{7,3},{8,12},{12,8},{9,1... | collective-permute-start | bytes 1990664 | tf_op jit(solution)/shard_map/ppermute | solution.py:1115
  115.0 28.2 %collective-permute-start.16 = (bf16[3,288,384]{2,1,0:T(8,128)(2,1)}, bf16[3,288,384]{2,1,0:T(8,128)(2,1)S(1)}, u32[]{:S(2)}, u32[]{:S(2)}) collective-permute-start(bf16[3,288,384]{2,1,0:T(8,128)(2,1)} %get-tuple-element.118.refs_6_.refs_22_), channel_id=1, source_target_pairs={{0,4},{4,0},{1,5},{5,1},{2,6},{6,2},{3,7},{7,3},{8,12},{12,8},{9,1... | collective-permute-start | bytes 1990664 | tf_op jit(solution)/shard_map/ppermute | solution.py:1115
  115.0 29.5 %collective-permute-start.17 = (bf16[3,288,384]{2,1,0:T(8,128)(2,1)}, bf16[3,288,384]{2,1,0:T(8,128)(2,1)S(1)}, u32[]{:S(2)}, u32[]{:S(2)}) collective-permute-start(bf16[3,288,384]{2,1,0:T(8,128)(2,1)} %get-tuple-element.117.refs_5_.refs_18_), channel_id=1, source_target_pairs={{0,16},{16,0},{1,17},{17,1},{2,18},{18,2},{3,19},{19,3},{4,20},{20... | collective-permute-start | bytes 1990664 | tf_op jit(solution)/shard_map/ppermute | solution.py:1116
  129.6 26.5 %collective-permute-start.24 = (bf16[3,288,384]{2,1,0:T(8,128)(2,1)S(1)}, bf16[3,288,384]{2,1,0:T(8,128)(2,1)S(1)}, u32[]{:S(2)}, u32[]{:S(2)}) collective-permute-start(bf16[3,288,384]{2,1,0:T(8,128)(2,1)S(1)} %collective-permute-done.18.refs_10_.refs_24_), channel_id=1, source_target_pairs={{0,4},{4,0},{1,5},{5,1},{2,6},{6,2},{3,7},{7,3},{8,12},{12,8},{9,1... | collective-permute-start | bytes 1990664 | tf_op jit(solution)/shard_map/ppermute | solution.py:1126
  207.9 140.6 %reduce-scatter.10.cloned.1.call-start = ((), (), s32[]{:S(2)}) async-start(), calls=%async_computation.8 | async-start | bytes 1105920
  209.8 22.6 %collective-permute-start.29 = (bf16[2,576,384]{2,1,0:T(8,128)(2,1)}, bf16[2,576,384]{2,1,0:T(8,128)(2,1)}, u32[]{:S(2)}, u32[]{:S(2)}) collective-permute-start(bf16[2,576,384]{2,1,0:T(8,128)(2,1)} %get-tuple-element.137), channel_id=1, source_target_pairs={{0,4},{4,0},{1,5},{5,1},{2,6},{6,2},{3,7},{7,3},{8,12},{12,8},{9,1... | collective-permute-start | bytes 2654216 | tf_op jit(solution)/shard_map/ppermute | solution.py:303
  212.2 21.7 %collective-permute-start.30 = (bf16[2,576,384]{2,1,0:T(8,128)(2,1)}, bf16[2,576,384]{2,1,0:T(8,128)(2,1)}, u32[]{:S(2)}, u32[]{:S(2)}) collective-permute-start(bf16[2,576,384]{2,1,0:T(8,128)(2,1)} %get-tuple-element.138), channel_id=1, source_target_pairs={{0,16},{16,0},{1,17},{17,1},{2,18},{18,2},{3,19},{19,3},{4,20},{20... | collective-permute-start | bytes 2654216 | tf_op jit(solution)/shard_map/ppermute | solution.py:303
  236.8 35.1 %collective-permute-start.34 = (bf16[2,576,384]{2,1,0:T(8,128)(2,1)}, bf16[2,576,384]{2,1,0:T(8,128)(2,1)S(1)}, u32[]{:S(2)}, u32[]{:S(2)}) collective-permute-start(bf16[2,576,384]{2,1,0:T(8,128)(2,1)} %get-tuple-element.151), channel_id=1, source_target_pairs={{0,16},{16,0},{1,17},{17,1},{2,18},{18,2},{3,19},{19,3},{4,20},{20... | collective-permute-start | bytes 2654216 | tf_op jit(solution)/shard_map/ppermute | solution.py:303
  237.6 34.4 %collective-permute-start.33 = (bf16[2,576,384]{2,1,0:T(8,128)(2,1)}, bf16[2,576,384]{2,1,0:T(8,128)(2,1)S(1)}, u32[]{:S(2)}, u32[]{:S(2)}) collective-permute-start(bf16[2,576,384]{2,1,0:T(8,128)(2,1)} %get-tuple-element.149), channel_id=1, source_target_pairs={{0,4},{4,0},{1,5},{5,1},{2,6},{6,2},{3,7},{7,3},{8,12},{12,8},{9,1... | collective-permute-start | bytes 2654216 | tf_op jit(solution)/shard_map/ppermute | solution.py:303
  239.7 32.3 %collective-permute-start.35 = (bf16[576,576]{1,0:T(8,128)(2,1)S(1)}, bf16[576,576]{1,0:T(8,128)(2,1)S(1)}, u32[]{:S(2)}, u32[]{:S(2)}) collective-permute-start(bf16[576,576]{1,0:T(8,128)(2,1)S(1)} %get-tuple-element.210), channel_id=1, source_target_pairs={{0,8},{8,0},{1,9},{9,1},{2,10},{10,2},{3,11},{11,3},{4,12},{12,4},... | collective-permute-start | bytes 1990664 | tf_op jit(solution)/shard_map/ppermute | solution.py:57
  239.7 27.9 %collective-permute-start.32 = (bf16[576,384]{1,0:T(8,128)(2,1)}, bf16[576,384]{1,0:T(8,128)(2,1)S(1)}, u32[]{:S(2)}, u32[]{:S(2)}) collective-permute-start(bf16[576,384]{1,0:T(8,128)(2,1)} %fusion.11.refs_9_), channel_id=1, source_target_pairs={{0,4},{4,0},{1,5},{5,1},{2,6},{6,2},{3,7},{7,3},{8,12},{12,8},{9,1... | collective-permute-start | bytes 1327112 | tf_op jit(solution)/shard_map/ppermute | solution.py:316
  241.2 26.4 %collective-permute-start.31 = (bf16[576,384]{1,0:T(8,128)(2,1)S(1)}, bf16[576,384]{1,0:T(8,128)(2,1)S(1)}, u32[]{:S(2)}, u32[]{:S(2)}) collective-permute-start(bf16[576,384]{1,0:T(8,128)(2,1)S(1)} %fusion.10.refs_8_), channel_id=1, source_target_pairs={{0,16},{16,0},{1,17},{17,1},{2,18},{18,2},{3,19},{19,3},{4,20},{20... | collective-permute-start | bytes 1327112 | tf_op jit(solution)/shard_map/ppermute | solution.py:316
  292.4 60.7 %reduce-scatter.8.cloned.1.call-start = ((), (), s32[]{:S(2)}) async-start(), calls=%async_computation.4 | async-start | bytes 1105920 | tf_op jit(solution)/shard_map/reduce_scatter | solution.py:374
  325.2 95.2 %all-gather.11.cloned.1.call-start = ((), (), s32[]{:S(2)}) async-start(), calls=%async_computation.7 | async-start | bytes 5971968 | tf_op jit(solution)/shard_map/all_gather | solution.py:396
  325.2 21.9 %collective-permute-start.44 = (bf16[2,576,384]{2,1,0:T(8,128)(2,1)}, bf16[2,576,384]{2,1,0:T(8,128)(2,1)}, u32[]{:S(2)}, u32[]{:S(2)}) collective-permute-start(bf16[2,576,384]{2,1,0:T(8,128)(2,1)} %get-tuple-element.171), channel_id=1, source_target_pairs={{0,4},{4,0},{1,5},{5,1},{2,6},{6,2},{3,7},{7,3},{8,12},{12,8},{9,1... | collective-permute-start | bytes 2654216 | tf_op jit(solution)/shard_map/ppermute | solution.py:303
  (109 other events, 1069.2 us)
Sparse Core Ops, SparseCore 0:
  38.6 33.3 all-gather.6
  74.2 31.9 all-gather.8
  208.0 66.1 reduce-scatter.5
  292.5 31.6 reduce-scatter.9
  327.0 26.0 reduce-scatter.7
  355.4 51.7 all-gather.10

commit v6 on v5

--- a/solution.py
+++ b/solution.py
@@ -374,7 +374,7 @@
     return lax.psum_scatter(mine, "z", scatter_dimension=0, tiled=True)
 
 
-def spread(total, sizes):
+def spread(total, sizes, late):
     if sizes[0] * sizes[1] == BLOCKS:
         mine = [
             total,
@@ -382,7 +382,7 @@
             lax.ppermute(total, "y", PAIR),
             lax.ppermute(total, ("y", "x"), [(i, 3 - i) for i in range(4)]),
         ]
-        return mine, [swap_core(value) for value in mine]
+        return mine, [swap_core(behind(value, late)) for value in mine]
     everyone = jnp.moveaxis(lax.all_gather(total, ("y", "x"), axis=0), 0, -2)
     everyone = jnp.moveaxis(everyone.reshape(total.shape[:2] + (BLOCKS, -1)), -2, 0)
     place = lax.axis_index("y") * sizes[1] + lax.axis_index("x")
@@ -1224,7 +1224,7 @@
     ]
     ffn_total = jnp.stack(lax.optimization_barrier((*ffn_total, *last))[:CHUNKS])
     grad_w_gate, grad_w_up, grad_w_down = unpack_ffn(info, *gather_all(ffn_total, sizes))
-    attn_out = unpack_attn(info, *spread(reduced[3][None], sizes), own_rows, ())
+    attn_out = unpack_attn(info, *spread(reduced[3][None], sizes, (grad_w_gate,)), own_rows, ())
     if tuned:
         attn_out, gain_grads = attn_out[:4], attn_out[4]
     else:

time: 441 us -> 444 us (level)
  waiting for transfers between devices: 126 us -> 121 us
    ppermute x6, waiting for transfers between devices: 19.5 us -> 28.5 us  [scatter_second(): return (lax.ppermute(sums[0], 'y', PAIR), lax.ppermute(sums[1], 'x', PAIR))]
    ppermute x6, waiting for transfers between devices: 17.9 us -> 9.7 us  [send_z(): lax.ppermute(o, 'z', ring(sizes[2], k + 1))]
    ppermute x1, waiting for transfers between devices: 6.75 us -> 0.01 us  [spread(): lax.ppermute(total, 'x', PAIR)]
    all_gather x1, waiting for transfers between devices: 0.01 us -> 5.64 us  [gather_all(): everyone = lax.all_gather(total, ('core', 'y', 'x'), axis=0)]
    unnamed x145 -> x133, local copies, waits for them, and re-layouts: 13.9 us -> 12.3 us
  transfers between devices with their start and end apart: 64 -> 64, of which waited for: 30 -> 25; matrix products, arithmetic and copies ran while one was open for 11% -> 10% of each run, Pallas kernels for 23% -> 25%
where the time goes in v6:
time: 444 us; the launch traced here: 436 us
  Pallas kernels  164 us (37%)
  waiting for transfers between devices  121 us (27%)
  starting transfers between devices  74.4 us (17%)
  local copies, waits for them, and re-layouts  32.1 us (7%)
  other arithmetic  29.3 us (7%)
  between operations  15.4 us (3%)
    pallas_call x1, Pallas kernels, feed_forward(): pl.pallas_call(ignoring(kernel, 14 + len(given), after), in_specs=[SCALAR...  47.8 us
    all_gather x2, waiting for transfers between devices, shards(): lax.all_gather(behind(piece, (stack,)), 'z', axis=0)  28.9 us
    ppermute x6, waiting for transfers between devices, scatter_second(): return (lax.ppermute(sums[0], 'y', PAIR), lax.ppermute(sums[1], 'x', PAIR))  28.5 us
    ppermute x1, waiting for transfers between devices, shards(): lax.ppermute(behind(grad_past[0], (first_pieces[0], *first[1], other)), '...  22 us
    pallas_call x1, Pallas kernels, attend_back(): pl.pallas_call(ignoring(attend_back_kernel, 8, after), grid=grid, in_spec...  18.2 us
    pallas_call x1, Pallas kernels, attend(): pl.pallas_call(ignoring(attend_kernel, 5, after), grid=grid, in_specs=[SC...  15.2 us
    unnamed x133, local copies, waits for them, and re-layouts  12.3 us
    ppermute x6, starting transfers between devices, send_z(): lax.ppermute(o, 'z', ring(sizes[2], k + 1))  10.8 us
  transfers between devices with their start and end apart: 64, of which 25 were waited for; matrix products, arithmetic and copies ran while one was open for 10% of the time, Pallas kernels for 25%

profile of v6, /device:TPU:0, one launch (start us, length us, event | category | flops | bytes accessed | tf_op | source)
XLA Modules:
  0.0 436.3 jit_solution(16983310343544914734)
XLA Ops:
  13.2 5.0 %collective-permute-start.3 = (bf16[304,384]{1,0:T(8,128)(2,1)}, bf16[304,384]{1,0:T(8,128)(2,1)S(1)}, u32[]{:S(2)}, u32[]{:S(2)}) collective-permute-start(bf16[304,384]{1,0:T(8,128)(2,1)} %get-tuple-element.112), channel_id=1, source_target_pairs={{0,3},{1,0},{2,1},{3,2},{4,7},{5,4},{6,5},{7,6},{8,11},{9,8},{10,9... | collective-permute-start | bytes 700424 | tf_op jit(solution)/shard_map/ppermute | solution.py:253
  29.4 6.1 %shard_map.204 = (bf16[3,288,1536]{2,1,0:T(8,128)(2,1)}, bf16[432,384]{1,0:T(8,128)(2,1)}, bf16[432,384]{1,0:T(8,128)(2,1)}) custom-call(s32[8]{0:T(128)} %concatenate.34.refs_0_, f32[288,3072]{1,0:T(8,128)} %refs_1_.1, f32[288,3072]{1,0:T(8,128)} %refs_2_.1, f32[768,1152]{1,0:T(8,128)} %refs_3_.1, f32[32,1024]{1,0:T(8,128)} %get-tuple-element.222.refs_4_.cos_ref, ...), custom_call_target="tpu_custom_call" | custom-call | bytes 796262 | tf_op jit(solution)/shard_map/pallas_call | solution.py:159
  51.7 20.4 %all-gather.7.cloned.1.call-done = bf16[1728,384]{1,0:T(8,128)(2,1)} async-done(((bf16[432,384]{1,0:T(8,128)(2,1)}), bf16[1728,384]{1,0:T(8,128)(2,1)}) %all-gather.7.cloned.1.call-update) | async-done | bytes 1327120 | tf_op jit(solution)/shard_map/all_gather | solution.py:1074
  79.7 5.4 %shard_map.206 = (bf16[4,1152,384]{2,1,0:T(8,128)(2,1)}, bf16[2,1152,384]{2,1,0:T(8,128)(2,1)}) custom-call(s32[8]{0:T(128)} %concatenate.34.refs_0_, bf16[288,1536]{1,0:T(8,128)(2,1)} %get-tuple-element.107.refs_1_, bf16[3,288,384]{2,1,0:T(8,128)(2,1)} %copy-done.14, bf16[3,288,384]{2,1,0:T(8,128)(2,1)} %copy-done.35, bf16[3,288,384]{2,1,0:T(8,128)(2,1)} %copy-done.36, ...), custom_call_target="tpu_custom_call" | custom-call | bytes 707788 | tf_op jit(solution)/shard_map/pallas_call | solution.py:208
  86.0 7.3 %shard_map.207 = (bf16[1152,1024]{1,0:T(8,128)(2,1)}, bf16[576,1024]{1,0:T(8,128)(2,1)}, bf16[2,192,1024]{2,1,0:T(8,128)(2,1)}) custom-call(bf16[512,1152]{1,0:T(8,128)(2,1)} %bitcast.84, bf16[512,1152]{1,0:T(8,128)(2,1)} %get-tuple-element.216.refs_2_.other_ref, f32[1,1152]{1,0:T(1,128)} %reshape.193.gain_ref, ...), custom_call_target="tpu_custom_call" | custom-call | flops 226492416 | bytes 1468006 | tf_op jit(solution)/shard_map/pallas_call | solution.py:437
  97.7 8.5 %all-gather.9.cloned.1.call-done = bf16[1728,384]{1,0:T(8,128)(2,1)} async-done(((bf16[432,384]{1,0:T(8,128)(2,1)}), bf16[1728,384]{1,0:T(8,128)(2,1)}) %all-gather.9.cloned.1.call-update) | async-done | bytes 1327120 | tf_op jit(solution)/shard_map/all_gather | solution.py:1074
  115.9 15.2 %shard_map.209 = (f32[576,1024]{1,0:T(8,128)}, f32[3,8,1024]{2,1,0:T(8,128)}) custom-call(s32[8]{0:T(128)} %concatenate.34.refs_0_, bf16[576,1024]{1,0:T(8,128)(2,1)} %get-tuple-element.116.refs_1_, bf16[2,192,1024]{2,1,0:T(8,128)(2,1)} %get-tuple-element.118.refs_2_, bf16[1,2,192,1024]{3,2,1,0:T(8,128)(2,1)} %bitcast.22.refs_3_, ...), custom_call_target="tpu_custom_call" | custom-call | flops 905969664 | bytes 838860 | tf_op jit(solution)/shard_map/pallas_call | solution.py:575
  131.1 10.2 %collective-permute-start.24 = (bf16[3,288,384]{2,1,0:T(8,128)(2,1)S(1)}, bf16[3,288,384]{2,1,0:T(8,128)(2,1)S(1)}, u32[]{:S(2)}, u32[]{:S(2)}) collective-permute-start(bf16[3,288,384]{2,1,0:T(8,128)(2,1)S(1)} %collective-permute-done.18.refs_10_.refs_24_), channel_id=1, source_target_pairs={{0,4},{4,0},{1,5},{5,1},{2,6},{6,2},{3,7},{7,3},{8,12},{12,8},{9,1... | collective-permute-start | bytes 1990664 | tf_op jit(solution)/shard_map/ppermute | solution.py:1126
  148.5 9.1 %shard_map.210 = (f32[512,1152]{1,0:T(8,128)}, bf16[256,1152]{1,0:T(8,128)(2,1)}, bf16[256,1152]{1,0:T(8,128)(2,1)}, bf16[1152,256]{1,0:T(8,128)(2,1)}, bf16[115...) custom-call(s32[8]{0:T(128)} %concatenate.34.refs_0_, f32[576,1024]{1,0:T(8,128)} %get-tuple-element.123.refs_1_.refs_4_, ...), custom_call_target="tpu_custom_call" | custom-call | flops 135895456 | bytes 1677721 | tf_op jit(solution)/shard_map/pallas_call | solution.py:651
  163.9 47.8 %shard_map.211 = (f32[512,1152]{1,0:T(8,128)}, f32[512,1152]{1,0:T(8,128)}, bf16[512,1152]{1,0:T(8,128)(2,1)}, bf16[512,1152]{1,0:T(8,128)(2,1)}, bf16[2,576,384...) custom-call(s32[8]{0:T(128)} %concatenate.34.refs_0_, ...), custom_call_target="tpu_custom_call" | custom-call | flops 3261490688 | bytes 4194304 | tf_op jit(solution)/shard_map/pallas_call | solution.py:813
  218.1 4.2 fusion.20
  226.1 7.3 %shard_map.212 = (bf16[576,1024]{1,0:T(8,128)(2,1)}, f32[3,8,1024]{2,1,0:T(8,128)}, bf16[576,1152]{1,0:T(8,128)(2,1)}) custom-call(bf16[512,1152]{1,0:T(8,128)(2,1)} %copy-done.5, bf16[256,1152]{1,0:T(8,128)(2,1)} %copy-done.41, bf16[256,1152]{1,0:T(8,128)(2,1)} %copy-done.42, bf16[576,1152]{1,0:T(8,128)(2,1)} %get-tuple-element.136.refs_3_, ...), custom_call_target="tpu_custom_call" | custom-call | flops 271790912 | bytes 1258291 | tf_op jit(solution)/shard_map/pallas_call | solution.py:858
  244.5 18.2 %shard_map.213 = (f32[576,1024]{1,0:T(8,128)}, f32[2,192,1024]{2,1,0:T(8,128)}, bf16[1,2,192,1024]{3,2,1,0:T(8,128)(2,1)}) custom-call(s32[8]{0:T(128)} %concatenate.34.refs_0_, bf16[576,1024]{1,0:T(8,128)(2,1)} %get-tuple-element.116.refs_1_, bf16[2,192,1024]{2,1,0:T(8,128)(2,1)} %get-tuple-element.118.refs_2_, bf16[1,2,192,1024]{3,2,1,0:T(8,128)(2,1)} %bitcast.22.refs_3_, ...), custom_call_target="tpu_custom_call" | custom-call | flops 1358954496 | bytes 1258291 | tf_op jit(solution)/shard_map/pallas_call | solution.py:596
  262.7 8.0 %collective-permute-done.32.refs_6_ = bf16[576,384]{1,0:T(8,128)(2,1)S(1)} collective-permute-done((bf16[576,384]{1,0:T(8,128)(2,1)}, bf16[576,384]{1,0:T(8,128)(2,1)S(1)}, u32[]{:S(2)}, u32[]{:S(2)}) %collective-permute-start.32) | collective-permute-done | bytes 442400 | tf_op jit(solution)/shard_map/ppermute | solution.py:316
  277.1 22.0 %collective-permute-done.36.refs_3_ = bf16[2,192,1024]{2,1,0:T(8,128)(2,1)} collective-permute-done((bf16[2,192,1024]{2,1,0:T(8,128)(2,1)}, bf16[2,192,1024]{2,1,0:T(8,128)(2,1)}, u32[]{:S(2)}, u32[]{:S(2)}) %collective-permute-start.36) | collective-permute-done | bytes 786464 | tf_op jit(solution)/shard_map/ppermute | solution.py:1175
  307.5 7.6 %collective-permute-done.41.refs_6_ = bf16[576,384]{1,0:T(8,128)(2,1)S(1)} collective-permute-done((bf16[576,384]{1,0:T(8,128)(2,1)S(1)}, bf16[576,384]{1,0:T(8,128)(2,1)S(1)}, u32[]{:S(2)}, u32[]{:S(2)}) %collective-permute-start.41) | collective-permute-done | bytes 442400 | tf_op jit(solution)/shard_map/ppermute | solution.py:316
  322.7 9.9 %shard_map.216 = (bf16[960,1024]{1,0:T(8,128)(2,1)}, bf16[2,576,384]{2,1,0:T(8,128)(2,1)}, bf16[2,576,384]{2,1,0:T(8,128)(2,1)}, bf16[2,576,384]{2,1,0:T(8,128)(2,1)}, bf16[2,576,384]{2,1,0:T(8,128)(2,1)}) custom-call(s32[8]{0:T(128)} %concatenate.34.refs_0_, f32[576,1024]{1,0:T(8,128)} %get-tuple-element.146.refs_1_, ...), custom_call_target="tpu_custom_call" | custom-call | flops 226492416 | bytes 2097152 | tf_op jit(solution)/shard_map/pallas_call | solution.py:902
  336.4 7.0 %shard_map.217 = (f32[512,1152]{1,0:T(8,128)}, bf16[256,1152]{1,0:T(8,128)(2,1)}, bf16[256,1152]{1,0:T(8,128)(2,1)}) custom-call(bf16[960,1024]{1,0:T(8,128)(2,1)} %get-tuple-element.170.refs_0_, bf16[4,1152,384]{2,1,0:T(8,128)(2,1)} %get-tuple-element.115.w_ref.refs_3_.refs_1_), custom_call_target="tpu_custom_call" | custom-call | flops 226492416 | bytes 943718 | tf_op jit(solution)/shard_map/pallas_call | solution.py:934
  346.6 6.5 %collective-permute-done.44.refs_2_ = bf16[2,576,384]{2,1,0:T(8,128)(2,1)} collective-permute-done((bf16[2,576,384]{2,1,0:T(8,128)(2,1)}, bf16[2,576,384]{2,1,0:T(8,128)(2,1)}, u32[]{:S(2)}, u32[]{:S(2)}) %collective-permute-start.44) | collective-permute-done | bytes 884768 | tf_op jit(solution)/shard_map/ppermute | solution.py:303
  370.5 7.7 %collective-permute-done.47.refs_6_ = bf16[576,384]{1,0:T(8,128)(2,1)} collective-permute-done((bf16[576,384]{1,0:T(8,128)(2,1)}, bf16[576,384]{1,0:T(8,128)(2,1)}, u32[]{:S(2)}, u32[]{:S(2)}) %collective-permute-start.47) | collective-permute-done | bytes 442400 | tf_op jit(solution)/shard_map/ppermute | solution.py:316
  383.8 4.1 collective-permute-start.48
  393.8 6.4 %collective-permute-done.49 = bf16[304,384]{1,0:T(8,128)(2,1)S(1)} collective-permute-done((bf16[304,384]{1,0:T(8,128)(2,1)}, bf16[304,384]{1,0:T(8,128)(2,1)S(1)}, u32[]{:S(2)}, u32[]{:S(2)}) %collective-permute-start.49) | collective-permute-done | bytes 233504 | tf_op jit(solution)/shard_map/ppermute | solution.py:366
  405.9 5.6 %all-gather.11.cloned.1.call-done = bf16[24,288,384]{2,1,0:T(8,128)(2,1)} async-done(((bf16[3,288,384]{2,1,0:T(8,128)(2,1)}), bf16[24,288,384]{2,1,0:T(8,128)(2,1)}) %all-gather.11.cloned.1.call-update) | async-done | bytes 5308432 | tf_op jit(solution)/shard_map/all_gather | solution.py:396
  411.5 7.5 %shard_map.219 = (f32[288,3072]{1,0:T(8,128)}, f32[288,3072]{1,0:T(8,128)}, f32[768,1152]{1,0:T(8,128)}) custom-call(bf16[8,3,288,384]{3,2,1,0:T(8,128)(2,1)} %bitcast.88), custom_call_target="tpu_custom_call" | custom-call | bytes 1677721 | tf_op jit(solution)/shard_map/pallas_call | solution.py:1015
  (328 shorter events, 163.9 us)
Async XLA Ops:
  7.2 64.9 %all-gather.7.cloned.1.call-start = ((), (), s32[]{:S(2)}) async-start(), calls=%async_computation.5 | async-start | bytes 1658880 | tf_op jit(solution)/shard_map/all_gather | solution.py:1074
  13.2 22.3 %collective-permute-start.3 = (bf16[304,384]{1,0:T(8,128)(2,1)}, bf16[304,384]{1,0:T(8,128)(2,1)S(1)}, u32[]{:S(2)}, u32[]{:S(2)}) collective-permute-start(bf16[304,384]{1,0:T(8,128)(2,1)} %get-tuple-element.112), channel_id=1, source_target_pairs={{0,3},{1,0},{2,1},{3,2},{4,7},{5,4},{6,5},{7,6},{8,11},{9,8},{10,9... | collective-permute-start | bytes 700424 | tf_op jit(solution)/shard_map/ppermute | solution.py:253
  38.5 67.7 %all-gather.9.cloned.1.call-start = ((), (), s32[]{:S(2)}) async-start(), calls=%async_computation.6 | async-start | bytes 1658880 | tf_op jit(solution)/shard_map/all_gather | solution.py:1074
  41.8 36.9 %collective-permute-start.6 = (bf16[3,288,384]{2,1,0:T(8,128)(2,1)S(1)}, bf16[3,288,384]{2,1,0:T(8,128)(2,1)S(1)}, u32[]{:S(2)}, u32[]{:S(2)}) collective-permute-start(bf16[3,288,384]{2,1,0:T(8,128)(2,1)S(1)} %pad_maximum_fusion.1.refs_2_), channel_id=1, source_target_pairs={{0,4},{4,0},{1,5},{5,1},{2,6},{6,2},{3,7},{7,3},{8,12},{12,8},{9,1... | collective-permute-start | bytes 1990664 | tf_op jit(solution)/shard_map/ppermute | solution.py:1085
  43.2 35.4 %collective-permute-start.7 = (bf16[3,288,384]{2,1,0:T(8,128)(2,1)S(1)}, bf16[3,288,384]{2,1,0:T(8,128)(2,1)S(1)}, u32[]{:S(2)}, u32[]{:S(2)}) collective-permute-start(bf16[3,288,384]{2,1,0:T(8,128)(2,1)S(1)} %pad_maximum_fusion.1.refs_2_), channel_id=1, source_target_pairs={{0,16},{16,0},{1,17},{17,1},{2,18},{18,2},{3,19},{19,3},{4,20},{20... | collective-permute-start | bytes 1990664 | tf_op jit(solution)/shard_map/ppermute | solution.py:1086
  44.8 33.9 %collective-permute-start.8 = (bf16[3,288,384]{2,1,0:T(8,128)(2,1)S(1)}, bf16[3,288,384]{2,1,0:T(8,128)(2,1)}, u32[]{:S(2)}, u32[]{:S(2)}) collective-permute-start(bf16[3,288,384]{2,1,0:T(8,128)(2,1)S(1)} %pad_maximum_fusion.1.refs_2_), channel_id=1, source_target_pairs={{0,20},{4,16},{16,4},{20,0},{1,21},{5,17},{17,5},{21,1},{2,22},{6,... | collective-permute-start | bytes 1990664 | tf_op jit(solution)/shard_map/ppermute | solution.py:1087
  45.3 253.8 %reduce-scatter.6.cloned.1.call-start = ((), (), s32[]{:S(2)}) async-start(), calls=%async_computation.3 | async-start | bytes 4423680 | tf_op jit(solution)/shard_map/reduce_scatter | solution.py:1142
  85.1 62.5 %collective-permute-start.14 = (bf16[2,1152,384]{2,1,0:T(8,128)(2,1)}, bf16[2,1152,384]{2,1,0:T(8,128)(2,1)}, u32[]{:S(2)}, u32[]{:S(2)}) collective-permute-start(bf16[2,1152,384]{2,1,0:T(8,128)(2,1)} %get-tuple-element.124), channel_id=1, source_target_pairs={{0,8},{8,0},{1,9},{9,1},{2,10},{10,2},{3,11},{11,3},{4,12},{12,4},... | collective-permute-start | bytes 5308424 | tf_op jit(solution)/shard_map/ppermute | solution.py:57
  93.3 21.7 %collective-permute-start.11 = (bf16[2,192,1024]{2,1,0:T(8,128)(2,1)}, bf16[2,192,1024]{2,1,0:T(8,128)(2,1)}, u32[]{:S(2)}, u32[]{:S(2)}) collective-permute-start(bf16[2,192,1024]{2,1,0:T(8,128)(2,1)} %get-tuple-element.118.refs_2_), channel_id=1, source_target_pairs={{0,4},{1,5},{2,6},{3,7},{8,12},{9,13},{10,14},{11,15},{16,20},{17,... | collective-permute-start | bytes 2359304 | tf_op jit(solution)/shard_map/ppermute | solution.py:1114
  111.0 32.5 %collective-permute-start.15 = (bf16[3,288,384]{2,1,0:T(8,128)(2,1)}, bf16[3,288,384]{2,1,0:T(8,128)(2,1)S(1)}, u32[]{:S(2)}, u32[]{:S(2)}) collective-permute-start(bf16[3,288,384]{2,1,0:T(8,128)(2,1)} %get-tuple-element.121.refs_5_.refs_18_), channel_id=1, source_target_pairs={{0,4},{4,0},{1,5},{5,1},{2,6},{6,2},{3,7},{7,3},{8,12},{12,8},{9,1... | collective-permute-start | bytes 1990664 | tf_op jit(solution)/shard_map/ppermute | solution.py:1115
  115.0 28.5 %collective-permute-start.16 = (bf16[3,288,384]{2,1,0:T(8,128)(2,1)}, bf16[3,288,384]{2,1,0:T(8,128)(2,1)S(1)}, u32[]{:S(2)}, u32[]{:S(2)}) collective-permute-start(bf16[3,288,384]{2,1,0:T(8,128)(2,1)} %get-tuple-element.122.refs_6_.refs_22_), channel_id=1, source_target_pairs={{0,4},{4,0},{1,5},{5,1},{2,6},{6,2},{3,7},{7,3},{8,12},{12,8},{9,1... | collective-permute-start | bytes 1990664 | tf_op jit(solution)/shard_map/ppermute | solution.py:1115
  115.0 32.6 %collective-permute-start.17 = (bf16[3,288,384]{2,1,0:T(8,128)(2,1)}, bf16[3,288,384]{2,1,0:T(8,128)(2,1)S(1)}, u32[]{:S(2)}, u32[]{:S(2)}) collective-permute-start(bf16[3,288,384]{2,1,0:T(8,128)(2,1)} %get-tuple-element.121.refs_5_.refs_18_), channel_id=1, source_target_pairs={{0,16},{16,0},{1,17},{17,1},{2,18},{18,2},{3,19},{19,3},{4,20},{20... | collective-permute-start | bytes 1990664 | tf_op jit(solution)/shard_map/ppermute | solution.py:1116
  131.1 27.1 %collective-permute-start.24 = (bf16[3,288,384]{2,1,0:T(8,128)(2,1)S(1)}, bf16[3,288,384]{2,1,0:T(8,128)(2,1)S(1)}, u32[]{:S(2)}, u32[]{:S(2)}) collective-permute-start(bf16[3,288,384]{2,1,0:T(8,128)(2,1)S(1)} %collective-permute-done.18.refs_10_.refs_24_), channel_id=1, source_target_pairs={{0,4},{4,0},{1,5},{5,1},{2,6},{6,2},{3,7},{7,3},{8,12},{12,8},{9,1... | collective-permute-start | bytes 1990664 | tf_op jit(solution)/shard_map/ppermute | solution.py:1126
  211.7 142.6 %reduce-scatter.10.cloned.1.call-start = ((), (), s32[]{:S(2)}) async-start(), calls=%async_computation.8 | async-start | bytes 1105920
  213.6 22.0 %collective-permute-start.29 = (bf16[2,576,384]{2,1,0:T(8,128)(2,1)}, bf16[2,576,384]{2,1,0:T(8,128)(2,1)}, u32[]{:S(2)}, u32[]{:S(2)}) collective-permute-start(bf16[2,576,384]{2,1,0:T(8,128)(2,1)} %get-tuple-element.141), channel_id=1, source_target_pairs={{0,4},{4,0},{1,5},{5,1},{2,6},{6,2},{3,7},{7,3},{8,12},{12,8},{9,1... | collective-permute-start | bytes 2654216 | tf_op jit(solution)/shard_map/ppermute | solution.py:303
  213.9 21.9 %collective-permute-start.30 = (bf16[2,576,384]{2,1,0:T(8,128)(2,1)}, bf16[2,576,384]{2,1,0:T(8,128)(2,1)}, u32[]{:S(2)}, u32[]{:S(2)}) collective-permute-start(bf16[2,576,384]{2,1,0:T(8,128)(2,1)} %get-tuple-element.142), channel_id=1, source_target_pairs={{0,16},{16,0},{1,17},{17,1},{2,18},{18,2},{3,19},{19,3},{4,20},{20... | collective-permute-start | bytes 2654216 | tf_op jit(solution)/shard_map/ppermute | solution.py:303
  238.7 36.2 %collective-permute-start.34 = (bf16[2,576,384]{2,1,0:T(8,128)(2,1)}, bf16[2,576,384]{2,1,0:T(8,128)(2,1)S(1)}, u32[]{:S(2)}, u32[]{:S(2)}) collective-permute-start(bf16[2,576,384]{2,1,0:T(8,128)(2,1)} %get-tuple-element.155), channel_id=1, source_target_pairs={{0,16},{16,0},{1,17},{17,1},{2,18},{18,2},{3,19},{19,3},{4,20},{20... | collective-permute-start | bytes 2654216 | tf_op jit(solution)/shard_map/ppermute | solution.py:303
  240.5 34.4 %collective-permute-start.33 = (bf16[2,576,384]{2,1,0:T(8,128)(2,1)}, bf16[2,576,384]{2,1,0:T(8,128)(2,1)S(1)}, u32[]{:S(2)}, u32[]{:S(2)}) collective-permute-start(bf16[2,576,384]{2,1,0:T(8,128)(2,1)} %get-tuple-element.153), channel_id=1, source_target_pairs={{0,4},{4,0},{1,5},{5,1},{2,6},{6,2},{3,7},{7,3},{8,12},{12,8},{9,1... | collective-permute-start | bytes 2654216 | tf_op jit(solution)/shard_map/ppermute | solution.py:303
  243.8 31.1 %collective-permute-start.35 = (bf16[576,576]{1,0:T(8,128)(2,1)S(1)}, bf16[576,576]{1,0:T(8,128)(2,1)S(1)}, u32[]{:S(2)}, u32[]{:S(2)}) collective-permute-start(bf16[576,576]{1,0:T(8,128)(2,1)S(1)} %get-tuple-element.218), channel_id=1, source_target_pairs={{0,8},{8,0},{1,9},{9,1},{2,10},{10,2},{3,11},{11,3},{4,12},{12,4},... | collective-permute-start | bytes 1990664 | tf_op jit(solution)/shard_map/ppermute | solution.py:57
  243.8 26.8 %collective-permute-start.32 = (bf16[576,384]{1,0:T(8,128)(2,1)}, bf16[576,384]{1,0:T(8,128)(2,1)S(1)}, u32[]{:S(2)}, u32[]{:S(2)}) collective-permute-start(bf16[576,384]{1,0:T(8,128)(2,1)} %fusion.11.refs_9_), channel_id=1, source_target_pairs={{0,4},{4,0},{1,5},{5,1},{2,6},{6,2},{3,7},{7,3},{8,12},{12,8},{9,1... | collective-permute-start | bytes 1327112 | tf_op jit(solution)/shard_map/ppermute | solution.py:316
  244.2 26.5 %collective-permute-start.31 = (bf16[576,384]{1,0:T(8,128)(2,1)S(1)}, bf16[576,384]{1,0:T(8,128)(2,1)S(1)}, u32[]{:S(2)}, u32[]{:S(2)}) collective-permute-start(bf16[576,384]{1,0:T(8,128)(2,1)S(1)} %fusion.10.refs_8_), channel_id=1, source_target_pairs={{0,16},{16,0},{1,17},{17,1},{2,18},{18,2},{3,19},{19,3},{4,20},{20... | collective-permute-start | bytes 1327112 | tf_op jit(solution)/shard_map/ppermute | solution.py:316
  275.8 23.3 %collective-permute-start.36 = (bf16[2,192,1024]{2,1,0:T(8,128)(2,1)}, bf16[2,192,1024]{2,1,0:T(8,128)(2,1)}, u32[]{:S(2)}, u32[]{:S(2)}) collective-permute-start(bf16[2,192,1024]{2,1,0:T(8,128)(2,1)} %bitcast.101), channel_id=1, source_target_pairs={{4,0},{5,1},{6,2},{7,3},{12,8},{13,9},{14,10},{15,11},{20,16},{21,... | collective-permute-start | bytes 2359304 | tf_op jit(solution)/shard_map/ppermute | solution.py:1175
  299.1 59.1 %reduce-scatter.8.cloned.1.call-start = ((), (), s32[]{:S(2)}) async-start(), calls=%async_computation.4 | async-start | bytes 1105920 | tf_op jit(solution)/shard_map/reduce_scatter | solution.py:374
  332.7 78.8 %all-gather.11.cloned.1.call-start = ((), (), s32[]{:S(2)}) async-start(), calls=%async_computation.7 | async-start | bytes 5971968 | tf_op jit(solution)/shard_map/all_gather | solution.py:396
  (103 other events, 989.0 us)
Sparse Core Ops, SparseCore 0:
  38.6 33.3 all-gather.6
  74.2 31.9 all-gather.8
  211.9 63.8 reduce-scatter.5
  299.3 27.0 reduce-scatter.9
  332.8 25.2 reduce-scatter.7
  360.5 50.9 all-gather.10
